TPU v7x, 32 devices: a whole 2x2x4 slice. The times are simulated.
32 devices in a mesh: fsdp: 8 (over z, y), ctx: 4 (over x, core).
Axes of the slice: x: 2, y: 2, z: 4, core: 2. Of those that a mesh axis runs over, the one named last changes fastest.
Arguments:
- tokens: bfloat16 [8, 1024, 2048], P('fsdp', 'ctx'), may hold values from -6 to 6
- positions: int32 [8, 1024], P('fsdp', 'ctx'), may hold values from 0 to 1021, as said below
- attn_gain: bfloat16 [2048], P(('fsdp', 'ctx')), may hold values from 0.25 to 1.75
- w_query: bfloat16 [2048, 2048], P(('fsdp', 'ctx')), may hold values from -0.125 to 0.125
- w_key: bfloat16 [2048, 2048], P(('fsdp', 'ctx')), may hold values from -0.125 to 0.125
- w_value: bfloat16 [2048, 2048], P(('fsdp', 'ctx')), may hold values from -0.125 to 0.125
- w_out: bfloat16 [2048, 2048], P(None, ('fsdp', 'ctx')), may hold values from -1 to 1
- mlp_gain: bfloat16 [2048], P(('fsdp', 'ctx')), may hold values from 0.25 to 1.75
- w_gate: bfloat16 [2048, 8192], P(('fsdp', 'ctx')), may hold values from -0.125 to 0.125
- w_up: bfloat16 [2048, 8192], P(('fsdp', 'ctx')), may hold values from -0.125 to 0.125
- w_down: bfloat16 [8192, 2048], P(None, ('fsdp', 'ctx')), may hold values from -0.0625 to 0.0625
- out_grad: bfloat16 [8, 1024, 2048], P('fsdp', 'ctx'), may hold values from -6 to 6
Outputs:
- block_out: bfloat16 [8, 1024, 2048], P('fsdp', 'ctx')
- tokens_grad: bfloat16 [8, 1024, 2048], P('fsdp', 'ctx')
- attn_gain_grad: float32 [2048], P(('fsdp', 'ctx'))
- w_query_grad: float32 [2048, 2048], P(('fsdp', 'ctx'))
- w_key_grad: float32 [2048, 2048], P(('fsdp', 'ctx'))
- w_value_grad: float32 [2048, 2048], P(('fsdp', 'ctx'))
- w_out_grad: float32 [2048, 2048], P(None, ('fsdp', 'ctx'))
- mlp_gain_grad: float32 [2048], P(('fsdp', 'ctx'))
- w_gate_grad: float32 [2048, 8192], P(('fsdp', 'ctx'))
- w_up_grad: float32 [2048, 8192], P(('fsdp', 'ctx'))
- w_down_grad: float32 [8192, 2048], P(None, ('fsdp', 'ctx'))
Inputs may be any that keep to these rules, and one draw needn't show every extreme that they name: `positions`: each sequence holds three documents laid end to end, and a token's position counts the tokens before it in its own document. The first document has 1 to 128 tokens, the last one likewise, and the middle one holds the rest. In at least one sequence the first and the last documents hold one token each.
All inputs are finite; a program needn't handle non-finite values.
Results may differ from a plain program's by a relative error of at most 0.015.
Values may be sent and summed in bfloat16 or wider, within the bound.
No kernel may reach another device: no remote copies, remote signals or barrier semaphores. Data moves between devices by JAX's collectives and lax.ppermute only.
A program may use at most 768 MiB of HBM per device.

v0:
```python
import jax
import jax.numpy as jnp
from jax import lax
from jax.sharding import PartitionSpec as P

H = 32
HD = 64


EPSILON = 1e-05
ROPE_BASE = 130000.0
MASKED_SCORE = -1e30
ROW_CONTRACT = (((0,), (0,)), ((), ()))
COL_CONTRACT = (((1,), (1,)), ((), ()))


def rms_rows(values):
    factor = lax.rsqrt(jnp.mean(values * values, axis=-1, keepdims=True) + EPSILON)
    return (values * factor, factor)


def norm_input(grad_normed, normed, factor, gain_vec):
    inner = grad_normed * gain_vec
    return factor * (inner - normed * jnp.mean(inner * normed, axis=-1, keepdims=True))


def norm_back(grad_normed, normed, factor, gain_vec):
    gain_grad = jnp.sum(grad_normed * normed, axis=0)
    return (gain_grad, norm_input(grad_normed, normed, factor, gain_vec))


def angle_tables(positions):
    inverse_freq = 1.0 / ROPE_BASE ** (jnp.arange(0, HD, 2, dtype=jnp.float32) / HD)
    angles = positions.astype(jnp.float32)[..., None] * inverse_freq
    return (jnp.cos(angles)[..., None, :], jnp.sin(angles)[..., None, :])


def rotate(values, cosine_table, sine_table):
    half_dim = values.shape[-1] // 2
    first = values[..., :half_dim]
    second = values[..., half_dim:]
    return jnp.concatenate(
        [first * cosine_table - second * sine_table, second * cosine_table + first * sine_table],
        axis=-1,
    )


def project(left_side, right_side):
    return jnp.dot(left_side, right_side, preferred_element_type=jnp.float32)


def project_back(left_side, right_side):
    return lax.dot_general(left_side, right_side, COL_CONTRACT, preferred_element_type=jnp.float32)


def outer_sum(left_side, right_side):
    return lax.dot_general(left_side, right_side, ROW_CONTRACT, preferred_element_type=jnp.float32)


def attend(queries, key_rows, value_rows, visible, score_scale):

    def score_rows():
        raw_scores = (
            jnp.einsum("bthe,bjhe->bhtj", queries, key_rows, preferred_element_type=jnp.float32)
            * score_scale
        )
        return jnp.where(visible[:, None], raw_scores, MASKED_SCORE)

    scores = score_rows()
    row_max = jnp.max(scores, axis=-1, keepdims=True)
    log_total = row_max + jnp.log(jnp.sum(jnp.exp(scores - row_max), axis=-1, keepdims=True))
    probs_low = jnp.exp(scores - log_total).astype(jnp.bfloat16)
    mixed_heads = jnp.einsum(
        "bhtj,bjhe->bthe", probs_low, value_rows, preferred_element_type=jnp.float32
    )
    return (mixed_heads, score_rows, log_total)


def attend_back(score_rows, log_total, grad_mixed, queries, key_rows, value_rows, score_scale):
    probs_full = jnp.exp(score_rows() - log_total)
    grad_values = jnp.einsum(
        "bhtj,bthe->bjhe",
        probs_full.astype(jnp.bfloat16),
        grad_mixed,
        preferred_element_type=jnp.float32,
    )
    grad_probs = jnp.einsum(
        "bthe,bjhe->bhtj", grad_mixed, value_rows, preferred_element_type=jnp.float32
    )
    grad_scores = (
        probs_full * (grad_probs - jnp.sum(probs_full * grad_probs, axis=-1, keepdims=True))
    ).astype(jnp.bfloat16)
    grad_query = (
        jnp.einsum("bhtj,bjhe->bthe", grad_scores, key_rows, preferred_element_type=jnp.float32)
        * score_scale
    )
    grad_keys = (
        jnp.einsum("bhtj,bthe->bjhe", grad_scores, queries, preferred_element_type=jnp.float32)
        * score_scale
    )
    return (grad_query, grad_keys, grad_values)


def local(
    tokens,
    positions,
    attn_gain,
    w_query,
    w_key,
    w_value,
    w_out,
    mlp_gain,
    w_gate,
    w_up,
    w_down,
    out_grad,
):
    seq_count, own_len, model_width = tokens.shape
    ctx_count = lax.axis_size("ctx")
    full_len = own_len * ctx_count
    hidden_width = w_gate.shape[1]
    score_scale = HD ** (-0.5)
    flat_shape = (seq_count, own_len, model_width)
    row_count = seq_count * own_len
    head_shape = (seq_count, own_len, H, HD)

    def gather_all():
        return (
            lax.all_gather(attn_gain, ("fsdp", "ctx"), axis=0, tiled=True),
            lax.all_gather(w_query, ("fsdp", "ctx"), axis=0, tiled=True),
            lax.all_gather(w_key, ("fsdp", "ctx"), axis=0, tiled=True),
            lax.all_gather(w_value, ("fsdp", "ctx"), axis=0, tiled=True),
            lax.all_gather(w_out, ("fsdp", "ctx"), axis=1, tiled=True),
            lax.all_gather(mlp_gain, ("fsdp", "ctx"), axis=0, tiled=True),
            lax.all_gather(w_gate, ("fsdp", "ctx"), axis=0, tiled=True),
            lax.all_gather(w_up, ("fsdp", "ctx"), axis=0, tiled=True),
            lax.all_gather(w_down, ("fsdp", "ctx"), axis=1, tiled=True),
        )

    (
        gain_one,
        query_full,
        key_full,
        value_full,
        out_full,
        gain_two,
        gate_full,
        up_full,
        down_full,
    ) = gather_all()
    inputs = tokens.reshape(row_count, model_width).astype(jnp.float32)
    normed_one, factor_one = rms_rows(inputs)
    input_low = (normed_one * gain_one).astype(jnp.bfloat16)
    cosine_table, sine_table = angle_tables(positions)
    queries = rotate(
        project(input_low, query_full).reshape(head_shape), cosine_table, sine_table
    ).astype(jnp.bfloat16)
    key_rows = rotate(
        project(input_low, key_full).reshape(head_shape), cosine_table, sine_table
    ).astype(jnp.bfloat16)
    value_rows = project(input_low, value_full).astype(jnp.bfloat16)
    key_all, value_all = (
        lax.all_gather(key_rows.reshape(flat_shape), "ctx", axis=1, tiled=True),
        lax.all_gather(value_rows.reshape(flat_shape), "ctx", axis=1, tiled=True),
    )
    key_all = key_all.reshape(seq_count, full_len, H, HD)
    value_all = value_all.reshape(seq_count, full_len, H, HD)
    query_at = lax.axis_index("ctx") * own_len + jnp.arange(own_len, dtype=jnp.int32)
    key_at = jnp.arange(full_len, dtype=jnp.int32)
    visible = (key_at[None, None, :] <= query_at[None, :, None]) & (
        key_at[None, None, :] >= (query_at[None, :] - positions)[:, :, None]
    )
    mixed_heads, score_rows, log_total = attend(queries, key_all, value_all, visible, score_scale)
    mixed_heads = mixed_heads.reshape(row_count, model_width).astype(jnp.bfloat16)
    first_sum = inputs + project(mixed_heads, out_full)
    normed_two, factor_two = rms_rows(first_sum)
    middle_low = (normed_two * gain_two).astype(jnp.bfloat16)
    gate_proj = project(middle_low, gate_full)
    up_proj = project(middle_low, up_full)
    gate_sigmoid = jax.nn.sigmoid(gate_proj)
    hidden = (gate_proj * gate_sigmoid * up_proj).astype(jnp.bfloat16)
    block_out = (first_sum + project(hidden, down_full)).astype(jnp.bfloat16)
    (
        gain_one,
        query_full,
        key_full,
        value_full,
        out_full,
        gain_two,
        gate_full,
        up_full,
        down_full,
    ) = gather_all()
    grad_rows = out_grad.reshape(row_count, model_width)
    grad_hidden = project_back(grad_rows, down_full)
    grad_up = (grad_hidden * gate_proj * gate_sigmoid).astype(jnp.bfloat16)
    grad_gate = (
        grad_hidden * up_proj * gate_sigmoid * (1.0 + gate_proj * (1.0 - gate_sigmoid))
    ).astype(jnp.bfloat16)
    grad_middle = project_back(grad_gate, gate_full) + project_back(grad_up, up_full)
    gain_two_grad, grad_first = norm_back(grad_middle, normed_two, factor_two, gain_two)
    grad_first = grad_first + grad_rows.astype(jnp.float32)
    mlp_grads = lax.psum_scatter(
        jnp.concatenate(
            [
                outer_sum(middle_low, grad_gate),
                outer_sum(middle_low, grad_up),
                outer_sum(grad_rows, hidden),
            ],
            axis=1,
        ),
        ("fsdp", "ctx"),
        scatter_dimension=0,
        tiled=True,
    )
    grad_attn = grad_first.astype(jnp.bfloat16)
    grad_mixed = project_back(grad_attn, out_full).astype(jnp.bfloat16).reshape(head_shape)
    grad_query, grad_keys, grad_values = attend_back(
        score_rows, log_total, grad_mixed, queries, key_all, value_all, score_scale
    )
    key_part, value_part = (
        lax.psum_scatter(
            grad_keys.reshape(seq_count, full_len, model_width).astype(jnp.bfloat16),
            "ctx",
            scatter_dimension=1,
            tiled=True,
        ).astype(jnp.float32),
        lax.psum_scatter(
            grad_values.reshape(seq_count, full_len, model_width).astype(jnp.bfloat16),
            "ctx",
            scatter_dimension=1,
            tiled=True,
        ).astype(jnp.float32),
    )
    query_low = (
        rotate(grad_query, cosine_table, -sine_table)
        .reshape(row_count, model_width)
        .astype(jnp.bfloat16)
    )
    key_low = (
        rotate(key_part.reshape(head_shape), cosine_table, -sine_table)
        .reshape(row_count, model_width)
        .astype(jnp.bfloat16)
    )
    value_low = value_part.reshape(row_count, model_width).astype(jnp.bfloat16)
    grad_input = (
        project_back(query_low, query_full)
        + project_back(key_low, key_full)
        + project_back(value_low, value_full)
    )
    gain_one_grad, grad_norm_one = norm_back(grad_input, normed_one, factor_one, gain_one)
    tokens_grad = (grad_first + grad_norm_one).astype(jnp.bfloat16).reshape(flat_shape)
    summed = (
        lax.psum_scatter(
            outer_sum(input_low, query_low), ("fsdp", "ctx"), scatter_dimension=0, tiled=True
        ),
        lax.psum_scatter(
            outer_sum(input_low, key_low), ("fsdp", "ctx"), scatter_dimension=0, tiled=True
        ),
        lax.psum_scatter(
            outer_sum(input_low, value_low), ("fsdp", "ctx"), scatter_dimension=0, tiled=True
        ),
        lax.psum_scatter(
            outer_sum(grad_attn, mixed_heads), ("fsdp", "ctx"), scatter_dimension=0, tiled=True
        ),
        lax.psum_scatter(gain_one_grad, ("fsdp", "ctx"), scatter_dimension=0, tiled=True),
        lax.psum_scatter(gain_two_grad, ("fsdp", "ctx"), scatter_dimension=0, tiled=True),
    )
    gate_grad = mlp_grads[:, :hidden_width]
    up_grad = mlp_grads[:, hidden_width : 2 * hidden_width]
    down_grad = jnp.transpose(mlp_grads[:, 2 * hidden_width :])
    return (
        block_out.reshape(flat_shape),
        tokens_grad,
        summed[4],
        summed[0],
        summed[1],
        summed[2],
        jnp.transpose(summed[3]),
        summed[5],
        gate_grad,
        up_grad,
        down_grad,
    )


def solution(mesh):
    in_specs = (
        P("fsdp", "ctx", None),
        P("fsdp", "ctx"),
        P(("fsdp", "ctx")),
        P(("fsdp", "ctx"), None),
        P(("fsdp", "ctx"), None),
        P(("fsdp", "ctx"), None),
        P(None, ("fsdp", "ctx")),
        P(("fsdp", "ctx")),
        P(("fsdp", "ctx"), None),
        P(("fsdp", "ctx"), None),
        P(None, ("fsdp", "ctx")),
        P("fsdp", "ctx", None),
    )
    out_specs = (
        P("fsdp", "ctx", None),
        P("fsdp", "ctx", None),
        P(("fsdp", "ctx")),
        P(("fsdp", "ctx"), None),
        P(("fsdp", "ctx"), None),
        P(("fsdp", "ctx"), None),
        P(None, ("fsdp", "ctx")),
        P(("fsdp", "ctx")),
        P(("fsdp", "ctx"), None),
        P(("fsdp", "ctx"), None),
        P(None, ("fsdp", "ctx")),
    )
    return jax.shard_map(local, mesh=mesh, in_specs=in_specs, out_specs=out_specs, check_vma=False)
```

profile of v0, /device:TPU:0, one launch (start us, length us, event | category | flops | bytes accessed | tf_op | source)
XLA Modules:
  0.0 3699.7 jit_solution(12158177213945040994)
XLA Ops:
  11.2 43.2 %all-reduce.5 = (bf16[2048]{0:T(1024)(128)(2,1)S(1)}, bf16[2048]{0:T(1024)(128)(2,1)S(1)}) all-reduce(bf16[2048]{0:T(1024)(128)(2,1)S(1)} %dynamic-update-slice, bf16[2048]{0:T(1024)(128)(2,1)S(1)} %dynamic-update-slice.1), channel_id=1, replica_groups=mesh['fsdp'=8,'ctx'=4] {'fsdp','ctx'}, use_global_device_ids=true, to_apply=%add | all-reduce | flops 4096 | bytes 16384
  55.9 35.3 all-gather.11.cloned.1.call-done
  99.2 70.9 %all-gather.15.cloned.1.call-done = bf16[2048,2048]{1,0:T(8,128)(2,1)} async-done(((bf16[64,2048]{1,0:T(8,128)(2,1)}), bf16[2048,2048]{1,0:T(8,128)(2,1)}) %all-gather.15.cloned.1.call-update) | async-done | bytes 8388624 | tf_op jit(solution)/shard_map/all_gather | solution.py:131
  182.4 66.6 %all-gather.13.cloned.1.call-done = bf16[2048,2048]{1,0:T(8,128)(2,1)} async-done(((bf16[64,2048]{1,0:T(8,128)(2,1)}), bf16[2048,2048]{1,0:T(8,128)(2,1)}) %all-gather.13.cloned.1.call-update) | async-done | bytes 8388624 | tf_op jit(solution)/shard_map/all_gather | solution.py:130
  290.6 30.6 all-gather.17.cloned.1.call-done
  321.2 16.2 fusion
  337.4 15.2 exponential_reduce_fusion
  352.6 16.8 convolution_convert_fusion.3
  369.4 31.9 all-gather.19.cloned.1.call-done
  407.9 189.7 %all-gather.23.cloned.1.call-done = bf16[2048,8192]{1,0:T(8,128)(2,1)} async-done(((bf16[64,8192]{1,0:T(8,128)(2,1)}), bf16[2048,8192]{1,0:T(8,128)(2,1)}) %all-gather.23.cloned.1.call-update) | async-done | bytes 33554448 | tf_op jit(solution)/shard_map/all_gather | solution.py:136
  597.6 18.4 fusion.60
  616.0 177.5 %all-gather.21.cloned.1.call-done = bf16[2048,8192]{1,0:T(8,128)(2,1)} async-done(((bf16[64,8192]{1,0:T(8,128)(2,1)}), bf16[2048,8192]{1,0:T(8,128)(2,1)}) %all-gather.21.cloned.1.call-update) | async-done | bytes 33554448 | tf_op jit(solution)/shard_map/all_gather | solution.py:135
  793.5 17.8 fusion.59
  811.3 178.0 %all-gather.25.cloned.1.call-done = bf16[8192,2048]{0,1:T(8,128)(2,1)} async-done(((bf16[8192,64]{0,1:T(8,128)(2,1)}), bf16[8192,2048]{0,1:T(8,128)(2,1)}) %all-gather.25.cloned.1.call-update) | async-done | bytes 33554448 | tf_op jit(solution)/shard_map/all_gather | solution.py:137
  989.4 24.7 multiply_convert_fusion.2
  1014.0 17.0 fusion.61
  1031.1 18.7 multiply_reduce_fusion.1
  1059.5 16.1 convolution_convert_fusion
  1075.6 26.9 multiply_reduce_fusion
  1102.5 30.2 multiply_convert_fusion
  1132.7 25.6 convolution_bitcast_fusion
  1169.3 25.5 fusion.64
  1194.8 23.1 fusion.63
  1217.9 132.7 %pad_maximum_fusion = f32[2048,24576]{1,0:T(8,128)} fusion(f32[2048,8192]{1,0:T(8,128)} %convolution_bitcast_fusion, f32[2048,8192]{1,0:T(8,128)} %fusion.64, f32[2048,8192]{1,0:T(8,128)} %fusion.63), kind=kLoop, calls=%fused_computation | loop fusion | flops 100663296 | bytes 402653184 | tf_op jit(solution)/shard_map/concatenate | solution.py:204
  1378.4 17.8 multiply_bitcast_fusion
  1426.8 25.1 fusion.10
  1471.9 38.6 %all-reduce.4 = (f32[2048]{0:T(1024)S(1)}, f32[2048]{0:T(1024)S(1)}) all-reduce(f32[2048]{0:T(1024)S(1)} %get-tuple-element.13, f32[2048]{0:T(1024)S(1)} %copy-done.27), channel_id=5, replica_groups=mesh['fsdp'=8,'ctx'=4] {'fsdp','ctx'}, use_global_device_ids=true, to_apply=%region_10.11.clone | all-reduce | flops 4096 | bytes 32768
  1515.2 1431.2 %reduce-scatter.20.cloned.1.call-done = f32[64,24576]{1,0:T(8,128)} async-done(((f32[2048,24576]{1,0:T(8,128)}), f32[64,24576]{1,0:T(8,128)}) %reduce-scatter.20.cloned.1.call-update) | async-done | bytes 6291472 | tf_op jit(solution)/shard_map/reduce_scatter | solution.py:203
  2952.1 179.2 %reduce-scatter.18.cloned.1.call-done = f32[64,2048]{1,0:T(8,128)} async-done(((f32[2048,2048]{1,0:T(8,128)}), f32[64,2048]{1,0:T(8,128)}) %reduce-scatter.18.cloned.1.call-update) | async-done | bytes 524304 | tf_op jit(solution)/shard_map/reduce_scatter | solution.py:263
  3131.3 187.2 %reduce-scatter.16.cloned.1.call-done = f32[64,2048]{1,0:T(8,128)} async-done(((f32[2048,2048]{1,0:T(8,128)}), f32[64,2048]{1,0:T(8,128)}) %reduce-scatter.16.cloned.1.call-update) | async-done | bytes 524304 | tf_op jit(solution)/shard_map/reduce_scatter | solution.py:260
  3318.5 187.0 %reduce-scatter.14.cloned.1.call-done = f32[64,2048]{1,0:T(8,128)} async-done(((f32[2048,2048]{1,0:T(8,128)}), f32[64,2048]{1,0:T(8,128)}) %reduce-scatter.14.cloned.1.call-update) | async-done | bytes 524304 | tf_op jit(solution)/shard_map/reduce_scatter | solution.py:257
  3505.5 187.2 %reduce-scatter.12.cloned.1.call-done = f32[64,2048]{1,0:T(8,128)} async-done(((f32[2048,2048]{1,0:T(8,128)}), f32[64,2048]{1,0:T(8,128)}) %reduce-scatter.12.cloned.1.call-update) | async-done | bytes 524304 | tf_op jit(solution)/shard_map/reduce_scatter | solution.py:254
  (143 shorter events, 182.8 us)
Async XLA Ops:
  7.2 84.0 %all-gather.11.cloned.1.call-start = ((), (), s32[]{:S(2)}) async-start(), calls=%async_computation.7 | async-start | bytes 8650752 | tf_op jit(solution)/shard_map/all_gather | solution.py:132
  7.9 162.2 %all-gather.15.cloned.1.call-start = ((), (), s32[]{:S(2)}) async-start(), calls=%async_computation.9 | async-start | bytes 8650752 | tf_op jit(solution)/shard_map/all_gather | solution.py:131
  8.7 240.4 %all-gather.13.cloned.1.call-start = ((), (), s32[]{:S(2)}) async-start(), calls=%async_computation.8 | async-start | bytes 8650752 | tf_op jit(solution)/shard_map/all_gather | solution.py:130
  9.4 274.7 %all-gather.27.cloned.1.call-start = ((), (), s32[]{:S(2)}) async-start(), calls=%async_computation.22 | async-start | bytes 5242880 | tf_op jit(solution)/shard_map/all_gather | solution.py:164
  54.4 213.3 %copy-start.20 = (f32[2048]{0:T(1024)}, f32[2048]{0:T(1024)S(1)}, u32[]{:S(2)}) copy-start(f32[2048]{0:T(1024)S(1)} %convert_element_type.190) | copy-start | bytes 24580
  55.9 211.8 %copy-start.25 = (f32[256]{0:T(256)}, f32[256]{0:T(256)S(1)}, u32[]{:S(2)}) copy-start(f32[256]{0:T(256)S(1)} %add_rsqrt_fusion.1) | copy-start | bytes 3076
  55.9 42.5 %copy-start.28 = (s32[1,256]{1,0:T(1,128)S(1)}, s32[1,256]{1,0:T(1,128)}, u32[]{:S(2)}) copy-start(s32[1,256]{1,0:T(1,128)} %param.13) | copy-start | bytes 3076
  98.3 222.9 %all-gather.17.cloned.1.call-start = ((), (), s32[]{:S(2)}) async-start(), calls=%async_computation.10 | async-start | bytes 5242880 | tf_op jit(solution)/shard_map/all_gather | solution.py:163
  99.2 170.9 %copy-start.22 = (f32[256,32]{0,1:T(8,128)}, f32[256,32]{0,1:T(8,128)S(1)}, u32[]{:S(2)}) copy-start(f32[256,32]{0,1:T(8,128)S(1)} %get-tuple-element.39) | copy-start | bytes 98308
  270.8 50.4 %copy-start.9 = (bf16[256,32,32]{0,2,1:T(8,128)(2,1)}, bf16[256,32,32]{0,2,1:T(8,128)(2,1)S(1)}, u32[]{:S(2)}) copy-start(bf16[256,32,32]{0,2,1:T(8,128)(2,1)S(1)} %get-tuple-element.29) | copy-start | bytes 1572868
  270.8 50.4 %copy-start.11 = (bf16[256,32,32]{0,2,1:T(8,128)(2,1)}, bf16[256,32,32]{0,2,1:T(8,128)(2,1)S(1)}, u32[]{:S(2)}) copy-start(bf16[256,32,32]{0,2,1:T(8,128)(2,1)S(1)} %get-tuple-element.30) | copy-start | bytes 1572868
  272.0 129.4 %all-gather.19.cloned.1.call-start = ((), (), s32[]{:S(2)}) async-start(), calls=%async_computation.11 | async-start | bytes 8650752 | tf_op jit(solution)/shard_map/all_gather | solution.py:133
  272.6 325.1 %all-gather.23.cloned.1.call-start = ((), (), s32[]{:S(2)}) async-start(), calls=%async_computation.13 | async-start | bytes 34603008 | tf_op jit(solution)/shard_map/all_gather | solution.py:136
  273.3 520.2 %all-gather.21.cloned.1.call-start = ((), (), s32[]{:S(2)}) async-start(), calls=%async_computation.12 | async-start | bytes 34603008 | tf_op jit(solution)/shard_map/all_gather | solution.py:135
  274.1 715.3 %all-gather.25.cloned.1.call-start = ((), (), s32[]{:S(2)}) async-start(), calls=%async_computation.14 | async-start | bytes 34603008 | tf_op jit(solution)/shard_map/all_gather | solution.py:137
  274.8 1089.0 %reduce-scatter.10.cloned.1.call-start = ((), (), s32[]{:S(2)}) async-start(), calls=%async_computation.16 | async-start | bytes 5242880 | tf_op jit(solution)/shard_map/reduce_scatter | solution.py:228
  407.6 642.2 %copy-start.6 = (f32[256,2048]{1,0:T(8,128)}, f32[256,2048]{1,0:T(8,128)S(1)}, u32[]{:S(2)}) copy-start(f32[256,2048]{1,0:T(8,128)S(1)} %get-tuple-element.45) | copy-start | bytes 6291460
  407.9 385.6 %copy-start.4 = (bf16[256,2048]{1,0:T(8,128)(2,1)}, bf16[256,2048]{1,0:T(8,128)(2,1)S(1)}, u32[]{:S(2)}) copy-start(bf16[256,2048]{1,0:T(8,128)(2,1)S(1)} %multiply_convert_fusion.5) | copy-start | bytes 3145732
  1031.1 18.8 copy-start.13
  1102.5 293.8 %reduce-scatter.8.cloned.1.call-start = ((), (), s32[]{:S(2)}) async-start(), calls=%async_computation.15 | async-start | bytes 5242880 | tf_op jit(solution)/shard_map/reduce_scatter | solution.py:222
  1102.5 30.2 copy-start.14
  1132.7 25.7 copy-start.10
  1132.7 25.7 copy-start.12
  1169.3 25.5 copy-start.15
  1217.9 1728.5 %reduce-scatter.20.cloned.1.call-start = ((), (), s32[]{:S(2)}) async-start(), calls=%async_computation.21 | async-start | bytes 207618048 | tf_op jit(solution)/shard_map/reduce_scatter | solution.py:203
  1350.7 1780.6 %reduce-scatter.18.cloned.1.call-start = ((), (), s32[]{:S(2)}) async-start(), calls=%async_computation.20 | async-start | bytes 17301504 | tf_op jit(solution)/shard_map/reduce_scatter | solution.py:263
  1363.8 1954.7 %reduce-scatter.16.cloned.1.call-start = ((), (), s32[]{:S(2)}) async-start(), calls=%async_computation.19 | async-start | bytes 17301504 | tf_op jit(solution)/shard_map/reduce_scatter | solution.py:260
  1378.4 19.6 copy-start.23
  1378.4 19.6 copy-start.24
  1378.4 2127.1 %reduce-scatter.14.cloned.1.call-start = ((), (), s32[]{:S(2)}) async-start(), calls=%async_computation.18 | async-start | bytes 17301504 | tf_op jit(solution)/shard_map/reduce_scatter | solution.py:257
  1413.3 2279.5 %reduce-scatter.12.cloned.1.call-start = ((), (), s32[]{:S(2)}) async-start(), calls=%async_computation.17 | async-start | bytes 17301504 | tf_op jit(solution)/shard_map/reduce_scatter | solution.py:254
  1451.9 15.8 slice-start
  (15 other events, 69.7 us)
Sparse Core Ops, SparseCore 0:
  10.9 80.2 all-gather.10
  94.0 76.0 all-gather.14
  173.0 76.0 all-gather.12
  251.0 33.0 all-gather.26
  286.1 35.0 all-gather.16
  323.9 77.4 all-gather.18
  404.2 193.3 all-gather.22
  600.5 192.9 all-gather.20
  796.4 192.9 all-gather.24
  1102.6 42.6 reduce-scatter.9
  1218.0 42.9 reduce-scatter.7
  1350.8 1595.5 reduce-scatter.19
  2949.3 181.9 reduce-scatter.17
  3134.0 184.4 reduce-scatter.15
  3321.2 184.2 reduce-scatter.13
  3508.3 184.4 reduce-scatter.11
where the time goes:
time: 3710 us; the launch traced here: 3700 us
  waiting for transfers between devices  2970 us (80%)
  matrix products  398 us (11%)
  other arithmetic  192 us (5%)
  blocking collectives  81.8 us (2%)
  local copies, waits for them, and re-layouts  46.4 us (1%)
    reduce_scatter x1, waiting for transfers between devices, local(): lax.psum_scatter(jnp.concatenate([outer_sum(middle_low, grad_gate), outer...  1430 us
    all_gather x1, waiting for transfers between devices, gather_all(): lax.all_gather(w_up, ('fsdp', 'ctx'), axis=0, tiled=True)  190 us
    reduce_scatter x1, waiting for transfers between devices, local(): lax.psum_scatter(outer_sum(input_low, query_low), ('fsdp', 'ctx'), scatte...  187 us
    reduce_scatter x1, waiting for transfers between devices, local(): lax.psum_scatter(outer_sum(input_low, value_low), ('fsdp', 'ctx'), scatte...  187 us
    reduce_scatter x1, waiting for transfers between devices, local(): lax.psum_scatter(outer_sum(input_low, key_low), ('fsdp', 'ctx'), scatter_...  187 us
    reduce_scatter x1, waiting for transfers between devices, local(): lax.psum_scatter(outer_sum(grad_attn, mixed_heads), ('fsdp', 'ctx'), scat...  179 us
    all_gather x1, waiting for transfers between devices, gather_all(): lax.all_gather(w_down, ('fsdp', 'ctx'), axis=1, tiled=True)  178 us
    all_gather x1, waiting for transfers between devices, gather_all(): lax.all_gather(w_gate, ('fsdp', 'ctx'), axis=0, tiled=True)  177 us
  transfers between devices with their start and end apart: 16, of which 14 were waited for; matrix products, arithmetic and copies ran while one was open for 14% of the time, Pallas kernels for 0%

commit v1 on v0

v1 whole, which is shorter than its diff:
```python
import functools

import jax
import jax.numpy as jnp
from jax import lax
from jax.experimental import pallas as pl
from jax.experimental.pallas import tpu as pltpu
from jax.sharding import Mesh
from jax.sharding import PartitionSpec as P

H = 32
HD = 64
EPSILON = 1e-05
ROPE_BASE = 130000.0
MASKED_SCORE = -1e30
SCALE = HD ** (-0.5)
LANES = 128
MIB = 1 << 20
BF16 = jnp.bfloat16
F32 = jnp.float32
AXES = ("r", "zh", "zl", "y", "x", "c")
NT = (((1,), (1,)), ((), ()))
TN = (((0,), (0,)), ((), ()))


def dot_nn(a, b):
    return jnp.dot(a, b, preferred_element_type=F32)


def dot_nt(a, b):
    return lax.dot_general(a, b, NT, preferred_element_type=F32)


def dot_tn(a, b):
    return lax.dot_general(a, b, TN, preferred_element_type=F32)


def swap(x, axis):
    return lax.ppermute(x, axis, [(0, 1), (1, 0)])


def swap_slot(x, axes, slot):
    if slot == 0:
        return x
    return lax.ppermute(x, axes, [(i, i ^ slot) for i in range(8)])


class Group:
    def __init__(self, d1, d2, g1, g2):
        self.d1, self.d2, self.g1, self.g2 = d1, d2, g1, g2
        self.axes = (d1, d2, "c")

    def index(self):
        return lax.axis_index(self.d1) * 4 + lax.axis_index(self.d2) * 2 + lax.axis_index("c")

    def column_chunks(self, outer):
        names = ("zh", "zl", "y", "x")
        strides = dict(zip(names, (8, 4, 2, 1)))
        order = []
        for r in range(outer):
            for slot in range(16):
                bits = dict(zip((self.g2, self.g1, self.d1, self.d2), ((slot >> 3) & 1, (slot >> 2) & 1, (slot >> 1) & 1, slot & 1)))
                order.append(r * 16 + sum(strides[n] * bits[n] for n in names))
        return order

    def reorder(self, x, order):
        if order == list(range(len(order))):
            return x
        width = x.shape[1] // len(order)
        return jnp.concatenate([x[:, i * width : (i + 1) * width] for i in order], axis=1)

    def flip_blocks(self, x, outer):
        mine = lax.axis_index(self.g2) * 2 + lax.axis_index(self.g1)
        width = x.shape[1] // (4 * outer)
        return jnp.concatenate(
            [
                lax.dynamic_slice_in_dim(x, (r * 4 + (slot ^ mine)) * width, width, axis=1)
                for r in range(outer)
                for slot in range(4)
            ],
            axis=1,
        )

    def to_slots(self, x, outer):
        return self.flip_blocks(self.reorder(x, self.column_chunks(outer)), outer)

    def from_slots(self, x, outer):
        order = self.column_chunks(outer)
        back = [order.index(i) for i in range(len(order))]
        return self.reorder(self.flip_blocks(x, outer), back)

    def gather_tokens(self, x):
        half = x.shape[0] // 2
        from_one = swap(x, self.d1)
        from_two = swap(x, self.d2)
        own_core = swap(x, "c")
        top = swap(from_two[:half], self.d1)
        bottom = swap(from_one[half:], self.d2)
        pieces = [x, own_core, from_two, swap(from_two, "c"), from_one, swap(from_one, "c")]
        pieces += [top, bottom, swap(top, "c"), swap(bottom, "c")]
        return jnp.concatenate(pieces, axis=0)

    def scatter_tokens(self, partial):
        def over_cores(i):
            both = partial(i)
            count = both.shape[0] // 2
            return both[:count] + swap(both[count:].astype(BF16), "c").astype(F32)

        far = over_cores(3)
        half = far.shape[0] // 2
        top = swap(far[:half].astype(BF16), self.d1).astype(F32)
        bottom = swap(far[half:].astype(BF16), self.d2).astype(F32)
        two = over_cores(1)
        one = over_cores(2)
        two_bottom = swap(two[half:].astype(BF16), self.d2)
        one_top = swap(one[:half].astype(BF16), self.d1)
        two_top = swap((two[:half] + top).astype(BF16), self.d2)
        one_bottom = swap((one[half:] + bottom).astype(BF16), self.d1)
        own = over_cores(0)
        from_two = jnp.concatenate([two_top, two_bottom], axis=0).astype(F32)
        from_one = jnp.concatenate([one_top, one_bottom], axis=0).astype(F32)
        return own + from_two + from_one

    def gather_weight(self, blocks):
        rows = [swap_slot(b, self.axes, s) for s, b in enumerate(blocks)]
        mine = join_rows(rows, self.index())
        one = swap(mine, self.g1)
        two = swap(mine, self.g2)
        both = swap(one, self.g2)
        whole = jnp.concatenate([mine, one, two, both], axis=0)
        if lax.axis_size("r") > 1:
            whole = lax.all_gather(whole, "r", axis=0, tiled=True)
        return whole

    def scatter_weight(self, left, right):
        width = left.shape[1] // 4
        if lax.axis_size("r") > 1:
            whole = lax.psum_scatter(dot_tn(left, right), "r", scatter_dimension=0, tiled=True)
            width = whole.shape[0] // 4

            def term(slot):
                return whole[slot * width : (slot + 1) * width]

        else:

            def term(slot):
                return dot_tn(left[:, slot * width : (slot + 1) * width], right)

        both = swap(term(3).astype(BF16), self.g2).astype(F32)
        one = swap((term(1) + both).astype(BF16), self.g1).astype(F32)
        two = swap(term(2).astype(BF16), self.g2).astype(F32)
        mine = (term(0) + two + one).astype(BF16)
        blocks = split_rows(mine, self.index())
        return [swap_slot(b, self.axes, s) for s, b in enumerate(blocks)]


def scalar(value):
    return jnp.reshape(value, (1,)).astype(jnp.int32)


SMEM_SPEC = pl.BlockSpec(memory_space=pltpu.SMEM)
VMEM_SPEC = pl.BlockSpec(memory_space=pltpu.VMEM)


def cost(flops, moved):
    return pl.CostEstimate(flops=flops, bytes_accessed=moved, transcendentals=0)


def parts_of(widths):
    if len(widths) == 1:
        return [(0, 0, widths[0])]
    return [(i, p * LANES, LANES) for p in range(widths[0] // LANES) for i in range(len(widths))]


def split_columns(weights, gain, index):
    rows = weights[0].shape[0]
    widths = [w.shape[1] // 8 for w in weights]
    total = sum(widths)
    parts = parts_of(widths)

    def body(index_ref, *refs):
        ins, outs = refs[: len(weights)], refs[-8:]
        factor = refs[len(weights)][...] if gain is not None else None
        me = index_ref[0]
        for slot in range(8):
            at = 0
            for i, offset, width in parts:
                start = pl.multiple_of((me ^ slot) * widths[i] + offset, LANES)
                piece = ins[i][:, pl.ds(start, width)]
                if factor is not None:
                    piece = (piece.astype(F32) * factor).astype(BF16)
                outs[slot][:, at : at + width] = piece
                at += width

    args = list(weights) + ([gain] if gain is not None else [])
    return pl.pallas_call(
        body,
        out_shape=[jax.ShapeDtypeStruct((rows, total), BF16)] * 8,
        in_specs=[SMEM_SPEC] + [VMEM_SPEC] * len(args),
        out_specs=[VMEM_SPEC] * 8,
        cost_estimate=cost(0, 32 * rows * total),
        name="split_columns",
    )(scalar(index), *args)


def join_rows(blocks, index):
    rows, total = blocks[0].shape

    def body(index_ref, *refs):
        me = index_ref[0]
        for slot in range(8):
            refs[8][pl.ds(pl.multiple_of((me ^ slot) * rows, rows), rows), :] = refs[slot][...]

    return pl.pallas_call(
        body,
        out_shape=jax.ShapeDtypeStruct((8 * rows, total), BF16),
        in_specs=[SMEM_SPEC] + [VMEM_SPEC] * 8,
        out_specs=VMEM_SPEC,
        cost_estimate=cost(0, 32 * rows * total),
        name="join_rows",
    )(scalar(index), *blocks)


def split_rows(whole, index):
    rows, total = whole.shape[0] // 8, whole.shape[1]

    def body(index_ref, whole_ref, *outs):
        me = index_ref[0]
        for slot in range(8):
            outs[slot][...] = whole_ref[pl.ds(pl.multiple_of((me ^ slot) * rows, rows), rows), :]

    return pl.pallas_call(
        body,
        out_shape=[jax.ShapeDtypeStruct((rows, total), BF16)] * 8,
        in_specs=[SMEM_SPEC, VMEM_SPEC],
        out_specs=[VMEM_SPEC] * 8,
        cost_estimate=cost(0, 32 * rows * total),
        name="split_rows",
    )(scalar(index), whole)


def join_columns(blocks, weights, gain, index, count):
    rows, total = blocks[0].shape
    widths = [total // count] * count
    parts = parts_of(widths)

    def body(index_ref, *refs):
        ins = refs[:8]
        outs = refs[-count:] if gain is None else refs[-count - 1 : -1]
        me = index_ref[0]
        acc = jnp.zeros((rows, LANES), F32)
        for slot in range(8):
            at = 0
            for i, offset, width in parts:
                start = pl.multiple_of((me ^ slot) * widths[i] + offset, LANES)
                value = ins[slot][:, at : at + width].astype(F32)
                if gain is not None:
                    term = refs[9 + i][:, pl.ds(start, width)].astype(F32) * value
                    for p in range(width // LANES):
                        acc = acc + term[:, p * LANES : (p + 1) * LANES]
                    value = value * refs[8][...]
                outs[i][:, pl.ds(start, width)] = value
                at += width
        if gain is not None:
            refs[-1][...] = jnp.sum(acc, axis=1, keepdims=True)

    args = list(blocks) + ([gain] + list(weights) if gain is not None else [])
    shapes = [jax.ShapeDtypeStruct((rows, 8 * w), F32) for w in widths]
    if gain is not None:
        shapes.append(jax.ShapeDtypeStruct((rows, 1), F32))
    return pl.pallas_call(
        body,
        out_shape=shapes,
        in_specs=[SMEM_SPEC] + [VMEM_SPEC] * len(args),
        out_specs=[VMEM_SPEC] * len(shapes),
        cost_estimate=cost(0, 64 * rows * total),
        name="join_columns",
    )(scalar(index), *args)


def rope(x, cosine, sine):
    lane = lax.broadcasted_iota(jnp.int32, x.shape, 1)
    other = jnp.where(lane % HD < HD // 2, pltpu.roll(x, LANES - HD // 2, 1), pltpu.roll(x, HD // 2, 1))
    return x * cosine + other * sine


def head_masks(shape):
    lane = lax.broadcasted_iota(jnp.int32, shape, 1)
    return [lane < HD, lane >= HD]


def attend_body(place_ref, proj_ref, cos_ref, sin_ref, start_ref, saved_ref, mixed_ref, lse_ref, *, blocks, size):
    place = place_ref[0]

    def slot_rows(j):
        return pl.ds(pl.multiple_of((place ^ j) * size, size), size)

    for j in range(blocks):
        rows = slot_rows(j)
        here = slice(j * size, (j + 1) * size)
        cosine, sine = cos_ref[rows, :], sin_ref[rows, :]
        for p in range(2):
            value = proj_ref[rows, p * LANES : (p + 1) * LANES]
            saved_ref[here, p * LANES : (p + 1) * LANES] = rope(value, cosine, sine).astype(BF16)
        saved_ref[here, 2 * LANES :] = proj_ref[rows, 2 * LANES :].astype(BF16)
    for j in range(blocks):
        here = slice(j * size, (j + 1) * size)
        upto = (j + 1) * size
        query = saved_ref[here, :LANES]
        keys = saved_ref[:upto, LANES : 2 * LANES]
        values = saved_ref[:upto, 2 * LANES :]
        row = lax.broadcasted_iota(jnp.int32, (size, upto), 0) + j * size
        col = lax.broadcasted_iota(jnp.int32, (size, upto), 1)
        visible = (col <= row) & (col >= start_ref[slot_rows(j), :])
        q_heads = head_masks(query.shape)
        v_heads = head_masks(values.shape)
        mixed, totals = [], []
        for h in range(2):
            scores = dot_nt(jnp.where(q_heads[h], query, jnp.zeros_like(query)), keys) * SCALE
            scores = jnp.where(visible, scores, MASKED_SCORE)
            top = jnp.max(scores, axis=1, keepdims=True)
            weights = jnp.exp(scores - top)
            total = jnp.sum(weights, axis=1, keepdims=True)
            probs = (weights * (1.0 / total)).astype(BF16)
            mixed.append(dot_nn(probs, jnp.where(v_heads[h], values, jnp.zeros_like(values))))
            totals.append(jnp.broadcast_to(top + jnp.log(total), query.shape))
        mixed_ref[slot_rows(j), :] = (mixed[0] + mixed[1]).astype(BF16)
        lse_ref[here, :] = jnp.where(q_heads[0], totals[0], totals[1])


def attend_back_body(place_ref, saved_ref, lse_ref, grad_ref, cos_ref, sin_ref, start_ref, out_ref, dk_ref, dv_ref, *, blocks, size):
    place = place_ref[0]

    def slot_rows(j):
        return pl.ds(pl.multiple_of((place ^ j) * size, size), size)

    dk_ref[...] = jnp.zeros_like(dk_ref)
    dv_ref[...] = jnp.zeros_like(dv_ref)
    for j in range(blocks):
        here = slice(j * size, (j + 1) * size)
        upto = (j + 1) * size
        rows = slot_rows(j)
        query = saved_ref[here, :LANES]
        keys = saved_ref[:upto, LANES : 2 * LANES]
        values = saved_ref[:upto, 2 * LANES :]
        grad = grad_ref[rows, :]
        row = lax.broadcasted_iota(jnp.int32, (size, upto), 0) + j * size
        col = lax.broadcasted_iota(jnp.int32, (size, upto), 1)
        visible = (col <= row) & (col >= start_ref[rows, :])
        q_heads = head_masks(query.shape)
        k_heads = head_masks(keys.shape)
        dq = jnp.zeros(query.shape, F32)
        dk = jnp.zeros(keys.shape, F32)
        dv = jnp.zeros(keys.shape, F32)
        for h in range(2):
            q_head = jnp.where(q_heads[h], query, jnp.zeros_like(query))
            g_head = jnp.where(q_heads[h], grad, jnp.zeros_like(grad))
            scores = dot_nt(q_head, keys) * SCALE
            log_total = lse_ref[here, h * HD : h * HD + 1]
            probs = jnp.exp(jnp.where(visible, scores, MASKED_SCORE) - log_total)
            d_probs = dot_nt(g_head, values)
            inner = jnp.sum(probs * d_probs, axis=1, keepdims=True)
            d_scores = (probs * (d_probs - inner)).astype(BF16)
            dq += dot_nn(d_scores, jnp.where(k_heads[h], keys, jnp.zeros_like(keys)))
            dk += dot_tn(d_scores, q_head)
            dv += dot_tn(probs.astype(BF16), g_head)
        out_ref[rows, :LANES] = rope(dq * SCALE, cos_ref[rows, :], -sin_ref[rows, :]).astype(BF16)
        dk_ref[:upto, :] += dk
        dv_ref[:upto, :] += dv
    for j in range(blocks):
        here = slice(j * size, (j + 1) * size)
        rows = slot_rows(j)
        out_ref[rows, LANES : 2 * LANES] = rope(dk_ref[here, :] * SCALE, cos_ref[rows, :], -sin_ref[rows, :]).astype(BF16)
        out_ref[rows, 2 * LANES :] = dv_ref[here, :].astype(BF16)


def attention_specs(length, width):
    return pl.BlockSpec((length, width), lambda s, p, place: (s, p))


def table_specs(length, width):
    return pl.BlockSpec((length, width), lambda s, p, place: (s, 0))


def attend(proj, cosine, sine, start, place, size, length):
    tokens = proj.shape[0]
    pairs = proj.shape[1] // (3 * LANES)
    seqs = tokens // length
    body = functools.partial(attend_body, blocks=length // size, size=size)
    return pl.pallas_call(
        body,
        grid_spec=pltpu.PrefetchScalarGridSpec(
            num_scalar_prefetch=1,
            grid=(seqs, pairs),
            in_specs=[attention_specs(length, 3 * LANES), table_specs(length, LANES), table_specs(length, LANES), table_specs(length, 1)],
            out_specs=[attention_specs(length, 3 * LANES), attention_specs(length, LANES), attention_specs(length, LANES)],
        ),
        out_shape=[
            jax.ShapeDtypeStruct(proj.shape, BF16),
            jax.ShapeDtypeStruct((tokens, pairs * LANES), BF16),
            jax.ShapeDtypeStruct((tokens, pairs * LANES), F32),
        ],
        compiler_params=pltpu.CompilerParams(vmem_limit_bytes=48 * MIB),
        cost_estimate=cost(16 * tokens * length * pairs * LANES, 16 * tokens * pairs * LANES),
        name="attend",
    )(scalar(place), proj, cosine, sine, start)


def attend_back(saved, lse, grad, cosine, sine, start, place, size, length):
    tokens = saved.shape[0]
    pairs = saved.shape[1] // (3 * LANES)
    seqs = tokens // length
    body = functools.partial(attend_back_body, blocks=length // size, size=size)
    return pl.pallas_call(
        body,
        grid_spec=pltpu.PrefetchScalarGridSpec(
            num_scalar_prefetch=1,
            grid=(seqs, pairs),
            in_specs=[
                attention_specs(length, 3 * LANES),
                attention_specs(length, LANES),
                attention_specs(length, LANES),
                table_specs(length, LANES),
                table_specs(length, LANES),
                table_specs(length, 1),
            ],
            out_specs=attention_specs(length, 3 * LANES),
            scratch_shapes=[pltpu.VMEM((length, LANES), F32), pltpu.VMEM((length, LANES), F32)],
        ),
        out_shape=jax.ShapeDtypeStruct(saved.shape, BF16),
        compiler_params=pltpu.CompilerParams(vmem_limit_bytes=48 * MIB),
        cost_estimate=cost(40 * tokens * length * pairs * LANES, 16 * tokens * pairs * LANES),
        name="attend_back",
    )(scalar(place), saved, lse, grad, cosine, sine, start)


def rms_rows(values):
    factor = lax.rsqrt(jnp.mean(values * values, axis=-1, keepdims=True) + EPSILON)
    return values * factor, factor


def norm_input(inner, normed, factor):
    return factor * (inner - normed * jnp.mean(inner * normed, axis=-1, keepdims=True))


def rope_tables(positions):
    inverse_freq = 1.0 / ROPE_BASE ** (jnp.arange(0, HD, 2, dtype=F32) / HD)
    angles = positions.astype(F32)[:, None] * inverse_freq
    cosine, sine = jnp.cos(angles), jnp.sin(angles)
    return (
        jnp.concatenate([cosine] * 4, axis=1),
        jnp.concatenate([-sine, sine, -sine, sine], axis=1),
    )


ATTN = Group("y", "x", "zh", "zl")
MLP = Group("y", "x", "zh", "zl")


def local(tokens, positions, attn_gain, w_query, w_key, w_value, w_out, mlp_gain, w_gate, w_up, w_down, out_grad):
    own = tokens.shape[1]
    model = tokens.shape[2]
    length = own * lax.axis_size("x") * lax.axis_size("c")
    outer = lax.axis_size("r")
    shape = tokens.shape
    gain_one = attn_gain.astype(F32)[:, None]
    gain_two = mlp_gain.astype(F32)[:, None]
    attn_at = ATTN.index()
    mlp_at = MLP.index()
    place = lax.axis_index("x") * 2 + lax.axis_index("c")

    qkv_all = ATTN.gather_weight(split_columns([w_query, w_key, w_value], gain_one, attn_at))
    out_all = ATTN.gather_weight(split_columns([jnp.transpose(w_out)], None, attn_at))
    gate_all = MLP.gather_weight(split_columns([w_gate], gain_two, mlp_at))
    up_all = MLP.gather_weight(split_columns([w_up], gain_two, mlp_at))
    down_all = MLP.gather_weight(split_columns([jnp.transpose(w_down)], None, mlp_at))

    inputs = tokens.reshape(own, model).astype(F32)
    normed_one, factor_one = rms_rows(inputs)
    one_all = ATTN.gather_tokens(ATTN.to_slots(normed_one.astype(BF16), outer))
    where = positions.reshape(own, 1)
    for axis in ("c", "x", "y"):
        where = jnp.concatenate([where, swap(where, axis)], axis=0)
    where = where.reshape(-1)
    cosine, sine = rope_tables(where)
    slot = (jnp.arange(length, dtype=jnp.int32) // own) ^ place
    at = slot * own + jnp.arange(length, dtype=jnp.int32) % own
    start = (jnp.tile(at, where.shape[0] // length) - where)[:, None]
    saved, mixed, lse = attend(dot_nn(one_all, qkv_all), cosine, sine, start, place, own, length)
    pair = 2 * own

    def piece(array, i):
        return array[i * pair : (i + 1) * pair]

    attn_out = ATTN.scatter_tokens(lambda i: dot_nt(piece(mixed, i), out_all))
    first_sum = inputs + ATTN.from_slots(attn_out, outer)

    grad_rows = out_grad.reshape(own, model)
    dy_all = MLP.gather_tokens(MLP.to_slots(grad_rows, outer))
    normed_two, factor_two = rms_rows(first_sum)
    two_all = MLP.gather_tokens(MLP.to_slots(normed_two.astype(BF16), outer))
    gate = dot_nn(two_all, gate_all)
    up = dot_nn(two_all, up_all)
    sigmoid = jax.nn.sigmoid(gate)
    hidden = (gate * sigmoid * up).astype(BF16)
    down_blocks = MLP.scatter_weight(dy_all, hidden)
    d_hidden = dot_nn(dy_all, down_all)
    d_up = (d_hidden * gate * sigmoid).astype(BF16)
    d_gate = (d_hidden * up * sigmoid * (1.0 + gate * (1.0 - sigmoid))).astype(BF16)
    inner_two = MLP.scatter_tokens(lambda i: dot_nt(piece(d_gate, i), gate_all) + dot_nt(piece(d_up, i), up_all))
    mlp_out = MLP.scatter_tokens(lambda i: dot_nt(piece(hidden, i), down_all))
    block_out = (first_sum + MLP.from_slots(mlp_out, outer)).astype(BF16)
    gate_blocks = MLP.scatter_weight(two_all, d_gate)
    up_blocks = MLP.scatter_weight(two_all, d_up)

    d_first = grad_rows.astype(F32) + norm_input(MLP.from_slots(inner_two, outer), normed_two, factor_two)
    d_attn_all = ATTN.gather_tokens(ATTN.to_slots(d_first.astype(BF16), outer))
    d_mixed = dot_nn(d_attn_all, out_all).astype(BF16)
    out_blocks = ATTN.scatter_weight(d_attn_all, mixed)
    d_qkv = attend_back(saved, lse, d_mixed, cosine, sine, start, place, own, length)
    inner_one = ATTN.scatter_tokens(lambda i: dot_nt(piece(d_qkv, i), qkv_all))
    qkv_blocks = ATTN.scatter_weight(one_all, d_qkv)
    tokens_grad = d_first + norm_input(ATTN.from_slots(inner_one, outer), normed_one, factor_one)

    (down_grad,) = join_columns(down_blocks, None, None, mlp_at, 1)
    gate_grad, gain_gate = join_columns(gate_blocks, [w_gate], gain_two, mlp_at, 1)
    up_grad, gain_up = join_columns(up_blocks, [w_up], gain_two, mlp_at, 1)
    (out_w_grad,) = join_columns(out_blocks, None, None, attn_at, 1)
    q_grad, k_grad, v_grad, gain_attn = join_columns(qkv_blocks, [w_query, w_key, w_value], gain_one, attn_at, 3)
    return (
        block_out.reshape(shape),
        tokens_grad.astype(BF16).reshape(shape),
        gain_attn.reshape(-1),
        q_grad,
        k_grad,
        v_grad,
        jnp.transpose(out_w_grad),
        (gain_gate + gain_up).reshape(-1),
        gate_grad,
        up_grad,
        jnp.transpose(down_grad),
    )


def solution(mesh):
    fsdp = mesh.shape["fsdp"]
    sizes = (fsdp // 8, 2, 2, 2, mesh.shape["ctx"] // 2, 2)
    fine = Mesh(mesh.devices.reshape(sizes), AXES)
    rows, cols = AXES[:4], AXES[4:]
    tokens, places, vector = P(rows, cols, None), P(rows, cols), P(AXES)
    first, second = P(AXES, None), P(None, AXES)
    in_specs = (tokens, places, vector, first, first, first, second, vector, first, first, second, tokens)
    out_specs = (tokens, tokens, vector, first, first, first, second, vector, first, first, second)
    return jax.shard_map(local, mesh=fine, in_specs=in_specs, out_specs=out_specs, check_vma=False)
```

time: 3710 us -> 1190 us (0.32)
  waiting for transfers between devices: 2970 us -> 560 us
  matrix products: 398 us -> 230 us
  starting transfers between devices: 1.02 us -> 157 us
  other arithmetic: 192 us -> 47.6 us
  Pallas kernels: 0 us -> 91.7 us
  blocking collectives: 81.8 us -> 0 us
  local copies, waits for them, and re-layouts: 46.4 us -> 91.7 us
    reduce_scatter x7 -> x0, waiting for transfers between devices: 2170 us -> none  [the longest x1 1430 us: local(): lax.psum_scatter(jnp.concatenate([outer_sum(middle_low, grad_gate), outer...]
    all_gather x9 -> x0, waiting for transfers between devices: 789 us -> none  [the longest x1 190 us: gather_all(): lax.all_gather(w_up, ('fsdp', 'ctx'), axis=0, tiled=True)]
    ppermute x0 -> x179, waiting for transfers between devices: none -> 560 us  [the longest x109 462 us: swap(): return lax.ppermute(x, axis, [(0, 1), (1, 0)])]
    dot_general x27 -> x45, matrix products: 398 us -> 230 us  [the longest x20 86.6 us: dot_tn(): return lax.dot_general(a, b, TN, preferred_element_type=F32)]
    ppermute x0 -> x179, starting transfers between devices: none -> 157 us  [the longest x109 92.1 us: swap(): return lax.ppermute(x, axis, [(0, 1), (1, 0)])]
    concatenate x3 -> x12, other arithmetic: 135 us -> 9.82 us  [the longest x4 7.56 us: flip_blocks(): jnp.concatenate([lax.dynamic_slice_in_dim(x, (r * 4 + (slot ^ mine)) * wi...]
    pallas_call x0 -> x22, Pallas kernels: none -> 91.7 us  [the longest x1 24.5 us: attend_back(): pl.pallas_call(body, grid_spec=pltpu.PrefetchScalarGridSpec(num_scalar_pr...]
    unnamed x2 -> x0, blocking collectives: 81.8 us -> none
  transfers between devices with their start and end apart: 16 -> 179, of which waited for: 14 -> 55; matrix products, arithmetic and copies ran while one was open for 14% -> 26% of each run, Pallas kernels for 0% -> 8%
where the time goes in v1:
time: 1190 us; the launch traced here: 1180 us
  waiting for transfers between devices  560 us (47%)
  matrix products  230 us (19%)
  starting transfers between devices  157 us (13%)
  Pallas kernels  91.7 us (8%)
  local copies, waits for them, and re-layouts  91.7 us (8%)
  other arithmetic  47.6 us (4%)
    ppermute x109, waiting for transfers between devices, swap(): return lax.ppermute(x, axis, [(0, 1), (1, 0)])  462 us
    ppermute x70, waiting for transfers between devices, swap_slot(): return lax.ppermute(x, axes, [(i, i ^ slot) for i in range(8)])  98.3 us
    ppermute x109, starting transfers between devices, swap(): return lax.ppermute(x, axis, [(0, 1), (1, 0)])  92.1 us
    dot_general x20, matrix products, dot_tn(): return lax.dot_general(a, b, TN, preferred_element_type=F32)  86.6 us
    dot_general x20, matrix products, dot_nt(): return lax.dot_general(a, b, NT, preferred_element_type=F32)  79.5 us
    ppermute x70, starting transfers between devices, swap_slot(): return lax.ppermute(x, axes, [(i, i ^ slot) for i in range(8)])  64.9 us
    dot_general x5, matrix products, dot_nn(): return jnp.dot(a, b, preferred_element_type=F32)  63.9 us
    unnamed x428, local copies, waits for them, and re-layouts  54.9 us
  transfers between devices with their start and end apart: 179, of which 55 were waited for; matrix products, arithmetic and copies ran while one was open for 26% of the time, Pallas kernels for 8%

profile of v1, /device:TPU:0, one launch (start us, length us, event | category | flops | bytes accessed | tf_op | source)
XLA Modules:
  0.0 1181.5 jit_solution(2976937143496120039)
XLA Ops:
  13.6 23.7 %collective-permute-done.20 = s32[512,1]{0,1:T(1,128)S(1)} collective-permute-done((s32[512,1]{0,1:T(1,128)S(1)}, s32[512,1]{0,1:T(1,128)S(1)}, u32[]{:S(2)}, u32[]{:S(2)}) %collective-permute-start.20) | collective-permute-done | bytes 2080 | tf_op jit(solution)/shard_map/ppermute | solution.py:39
  61.3 13.6 %collective-permute-done.12.refs_4_ = bf16[64,768]{1,0:T(8,128)(2,1)S(1)} collective-permute-done((bf16[64,768]{1,0:T(8,128)(2,1)}, bf16[64,768]{1,0:T(8,128)(2,1)S(1)}, u32[]{:S(2)}, u32[]{:S(2)}) %collective-permute-start.12) | collective-permute-done | bytes 98336 | tf_op jit(solution)/shard_map/ppermute | solution.py:45
  101.6 27.3 %collective-permute-done.16 = bf16[512,768]{1,0:T(8,128)(2,1)S(1)} collective-permute-done((bf16[512,768]{1,0:T(8,128)(2,1)}, bf16[512,768]{1,0:T(8,128)(2,1)S(1)}, u32[]{:S(2)}, u32[]{:S(2)}) %collective-permute-start.16) | collective-permute-done | bytes 786464 | tf_op jit(solution)/shard_map/ppermute | solution.py:39
  139.2 11.4 collective-permute-done.17
  150.6 16.9 %collective-permute-done.18 = bf16[512,768]{1,0:T(8,128)(2,1)S(1)} collective-permute-done((bf16[512,768]{1,0:T(8,128)(2,1)S(1)}, bf16[512,768]{1,0:T(8,128)(2,1)S(1)}, u32[]{:S(2)}, u32[]{:S(2)}) %collective-permute-start.18) | collective-permute-done | bytes 786464 | tf_op jit(solution)/shard_map/ppermute | solution.py:39
  167.4 11.0 fusion.183.proj_ref
  178.4 20.4 %attend.1 = (bf16[2048,768]{1,0:T(8,128)(2,1)}, bf16[2048,256]{1,0:T(8,128)(2,1)S(1)}, f32[2048,256]{1,0:T(8,128)}) custom-call(s32[1]{0:T(128)} %bitcast.place_ref, f32[2048,768]{1,0:T(8,128)} %fusion.183.proj_ref, f32[2048,128]{1,0:T(8,128)S(1)} %pad_maximum_fusion.7.cos_ref, f32[2048,128]{1,0:T(8,128)S(1)} %pad_maximum_fusion.8.sin_ref, ...), custom_call_target="tpu_custom_call" | custom-call | flops 8589934592 | bytes 8388608 | tf_op jit(solution)/shard_map/attend/pallas_call | solution.py:390
  211.6 10.8 collective-permute-done.40
  265.5 21.8 %collective-permute-done.52.refs_2_ = bf16[64,1024]{1,0:T(8,128)(2,1)} collective-permute-done((bf16[64,1024]{1,0:T(8,128)(2,1)}, bf16[64,1024]{1,0:T(8,128)(2,1)}, u32[]{:S(2)}, u32[]{:S(2)}) %collective-permute-start.52) | collective-permute-done | bytes 131104 | tf_op jit(solution)/shard_map/ppermute | solution.py:45
  303.3 24.4 %collective-permute-done.75.refs_5_ = bf16[64,1024]{1,0:T(8,128)(2,1)S(1)} collective-permute-done((bf16[64,1024]{1,0:T(8,128)(2,1)}, bf16[64,1024]{1,0:T(8,128)(2,1)S(1)}, u32[]{:S(2)}, u32[]{:S(2)}) %collective-permute-start.75) | collective-permute-done | bytes 131104 | tf_op jit(solution)/shard_map/ppermute | solution.py:45
  378.8 23.9 %collective-permute-done.78 = bf16[512,1024]{1,0:T(8,128)(2,1)S(1)} collective-permute-done((bf16[512,1024]{1,0:T(8,128)(2,1)}, bf16[512,1024]{1,0:T(8,128)(2,1)S(1)}, u32[]{:S(2)}, u32[]{:S(2)}) %collective-permute-start.78) | collective-permute-done | bytes 1048608 | tf_op jit(solution)/shard_map/ppermute | solution.py:39
  412.9 9.2 collective-permute-done.79
  422.1 42.3 %collective-permute-done.80 = bf16[512,1024]{1,0:T(8,128)(2,1)S(1)} collective-permute-done((bf16[512,1024]{1,0:T(8,128)(2,1)S(1)}, bf16[512,1024]{1,0:T(8,128)(2,1)S(1)}, u32[]{:S(2)}, u32[]{:S(2)}) %collective-permute-start.80) | collective-permute-done | bytes 1048608 | tf_op jit(solution)/shard_map/ppermute | solution.py:39
  464.5 13.5 %fusion.184 = f32[2048,1024]{1,0:T(8,128)} fusion(bf16[2048,2048]{1,0:T(8,128)(2,1)} %constant_dynamic-update-slice_fusion.20, bf16[512,1024]{1,0:T(8,128)(2,1)S(1)} %collective-permute-done.80, bf16[512,1024]{1,0:T(8,128)(2,1)S(1)} %collective-permute-done.79, bf16[512,1024]{1,0:T(8,128)(2,1)S(1)} %collective-permute-done.78, ...), kind=kOutput, calls=%fused_computation.319 | convolution fusion | flops 8606711808 | bytes 20971520 | tf_op jit(solution)/shard_map/dot_general | solution.py:27
  485.1 41.6 %collective-permute-done.58 = bf16[512,1024]{1,0:T(8,128)(2,1)S(1)} collective-permute-done((bf16[512,1024]{1,0:T(8,128)(2,1)S(1)}, bf16[512,1024]{1,0:T(8,128)(2,1)S(1)}, u32[]{:S(2)}, u32[]{:S(2)}) %collective-permute-start.58) | collective-permute-done | bytes 1048608 | tf_op jit(solution)/shard_map/ppermute | solution.py:39
  529.1 22.5 %collective-permute-done.70 = bf16[512,1024]{1,0:T(8,128)(2,1)S(1)} collective-permute-done((bf16[512,1024]{1,0:T(8,128)(2,1)S(1)}, bf16[512,1024]{1,0:T(8,128)(2,1)S(1)}, u32[]{:S(2)}, u32[]{:S(2)}) %collective-permute-start.70) | collective-permute-done | bytes 1048608 | tf_op jit(solution)/shard_map/ppermute | solution.py:39
  551.6 11.2 fusion.185
  562.8 11.2 collective-permute-done.59
  575.0 20.8 %collective-permute-done.60 = bf16[512,1024]{1,0:T(8,128)(2,1)} collective-permute-done((bf16[512,1024]{1,0:T(8,128)(2,1)S(1)}, bf16[512,1024]{1,0:T(8,128)(2,1)}, u32[]{:S(2)}, u32[]{:S(2)}) %collective-permute-start.60) | collective-permute-done | bytes 1048608 | tf_op jit(solution)/shard_map/ppermute | solution.py:39
  595.8 22.4 %multiply_convert_fusion.1 = (bf16[2048,1024]{1,0:T(8,128)(2,1)}, bf16[2048,1024]{1,0:T(8,128)(2,1)}, bf16[2048,1024]{1,0:T(8,128)(2,1)}) fusion(f32[2048,1024]{1,0:T(8,128)} %fusion.184, f32[2048,1024]{1,0:T(8,128)} %fusion.185, bf16[2048,2048]{1,0:T(8,128)(2,1)} %copy-done.68, bf16[512,1024]{1,0:T(8,128)(2,1)} %collective-permute-done.60, ...), kind=kOutput, calls=%fused_computation.1 | convolution fusion | flops 8640266240 | bytes 41943040 | tf_op jit(solution)/shard_map/dot_general | solution.py:27
  656.7 9.3 fusion.131
  672.4 9.4 fusion.134
  688.1 9.2 fusion.138
  704.2 9.5 fusion.141
  786.1 10.5 collective-permute-done.161
  814.9 55.8 %collective-permute-done.169 = bf16[512,1024]{1,0:T(8,128)(2,1)S(1)} collective-permute-done((bf16[512,1024]{1,0:T(8,128)(2,1)S(1)}, bf16[512,1024]{1,0:T(8,128)(2,1)S(1)}, u32[]{:S(2)}, u32[]{:S(2)}) %collective-permute-start.169) | collective-permute-done | bytes 1048608 | tf_op jit(solution)/shard_map/ppermute | solution.py:39
  871.6 19.5 %collective-permute-done.149 = bf16[512,1024]{1,0:T(8,128)(2,1)S(1)} collective-permute-done((bf16[512,1024]{1,0:T(8,128)(2,1)S(1)}, bf16[512,1024]{1,0:T(8,128)(2,1)S(1)}, u32[]{:S(2)}, u32[]{:S(2)}) %collective-permute-start.149) | collective-permute-done | bytes 1048608 | tf_op jit(solution)/shard_map/ppermute | solution.py:39
  917.6 11.0 collective-permute-done.111
  928.6 8.3 collective-permute-done.85
  974.0 24.5 %attend_back.1 = bf16[2048,768]{1,0:T(8,128)(2,1)} custom-call(s32[1]{0:T(128)} %bitcast.place_ref, bf16[2048,768]{1,0:T(8,128)(2,1)} %get-tuple-element.143.saved_ref, f32[2048,256]{1,0:T(8,128)} %get-tuple-element.144.lse_ref, bf16[2048,256]{1,0:T(8,128)(2,1)S(1)} %convolution_convert_fusion.grad_ref, f32[2048,128]{1,0:T(8,128)S(1)} %pad_maximum_fusion.7.cos_ref, ...), custom_call_target="tpu_custom_call" | custom-call | flops 21474836480 | bytes 8388608 | tf_op jit(solution)/shard_map/attend_back/pallas_call | solution.py:414
  1034.1 14.1 %collective-permute-done.141 = bf16[512,256]{1,0:T(8,128)(2,1)S(1)} collective-permute-done((bf16[512,256]{1,0:T(8,128)(2,1)S(1)}, bf16[512,256]{1,0:T(8,128)(2,1)S(1)}, u32[]{:S(2)}, u32[]{:S(2)}) %collective-permute-start.141) | collective-permute-done | bytes 262176 | tf_op jit(solution)/shard_map/ppermute | solution.py:39
  1097.7 21.4 %collective-permute-done.129 = bf16[512,768]{1,0:T(8,128)(2,1)S(1)} collective-permute-done((bf16[512,768]{1,0:T(8,128)(2,1)S(1)}, bf16[512,768]{1,0:T(8,128)(2,1)S(1)}, u32[]{:S(2)}, u32[]{:S(2)}) %collective-permute-start.129) | collective-permute-done | bytes 786464 | tf_op jit(solution)/shard_map/ppermute | solution.py:39
  (936 shorter events, 575.7 us)
Async XLA Ops:
  76.9 54.0 %collective-permute-start.4 = (bf16[256,2048]{1,0:T(8,128)(2,1)}, bf16[256,2048]{1,0:T(8,128)(2,1)}, u32[]{:S(2)}, u32[]{:S(2)}) collective-permute-start(bf16[256,2048]{1,0:T(8,128)(2,1)} %collective-permute-done.3), channel_id=1, source_target_pairs={{0,1},{1,0},{2,3},{3,2},{4,5},{5,4},{6,7},{7,6},{8,9},{9,8},{10,11... | collective-permute-start | bytes 3145736 | tf_op jit(solution)/shard_map/ppermute | solution.py:39
  135.5 63.3 %collective-permute-start.30 = (bf16[512,256]{1,0:T(8,128)(2,1)S(1)}, bf16[512,256]{1,0:T(8,128)(2,1)S(1)}, u32[]{:S(2)}, u32[]{:S(2)}) collective-permute-start(bf16[512,256]{1,0:T(8,128)(2,1)S(1)} %copy-done.29), channel_id=1, source_target_pairs={{0,8},{8,0},{1,9},{9,1},{2,10},{10,2},{3,11},{11,3},{4,12},{12,4},... | collective-permute-start | bytes 786440 | tf_op jit(solution)/shard_map/ppermute | solution.py:39
  135.5 63.2 %collective-permute-start.31 = (bf16[512,256]{1,0:T(8,128)(2,1)S(1)}, bf16[512,256]{1,0:T(8,128)(2,1)S(1)}, u32[]{:S(2)}, u32[]{:S(2)}) collective-permute-start(bf16[512,256]{1,0:T(8,128)(2,1)S(1)} %collective-permute-done.29), channel_id=1, source_target_pairs={{0,8},{8,0},{1,9},{9,1},{2,10},{10,2},{3,11},{11,3},{4,12},{12,4},... | collective-permute-start | bytes 786440 | tf_op jit(solution)/shard_map/ppermute | solution.py:39
  258.2 84.9 %collective-permute-start.92 = (bf16[256,2048]{1,0:T(8,128)(2,1)}, bf16[256,2048]{1,0:T(8,128)(2,1)}, u32[]{:S(2)}, u32[]{:S(2)}) collective-permute-start(bf16[256,2048]{1,0:T(8,128)(2,1)} %get-tuple-element.226), channel_id=1, source_target_pairs={{0,2},{2,0},{1,3},{3,1},{4,6},{6,4},{5,7},{7,5},{8,10},{10,8},{9,1... | collective-permute-start | bytes 3145736 | tf_op jit(solution)/shard_map/ppermute | solution.py:39
  291.1 53.0 %collective-permute-start.91 = (bf16[256,2048]{1,0:T(8,128)(2,1)}, bf16[256,2048]{1,0:T(8,128)(2,1)}, u32[]{:S(2)}, u32[]{:S(2)}) collective-permute-start(bf16[256,2048]{1,0:T(8,128)(2,1)} %get-tuple-element.226), channel_id=1, source_target_pairs={{0,1},{1,0},{2,3},{3,2},{4,5},{5,4},{6,7},{7,6},{8,9},{9,8},{10,11... | collective-permute-start | bytes 3145736 | tf_op jit(solution)/shard_map/ppermute | solution.py:39
  301.0 52.4 %collective-permute-start.94 = (bf16[256,2048]{1,0:T(8,128)(2,1)}, bf16[256,2048]{1,0:T(8,128)(2,1)}, u32[]{:S(2)}, u32[]{:S(2)}) collective-permute-start(bf16[256,2048]{1,0:T(8,128)(2,1)} %get-tuple-element.226), channel_id=1, source_target_pairs={{0,4},{4,0},{1,5},{5,1},{2,6},{6,2},{3,7},{7,3},{8,12},{12,8},{9,1... | collective-permute-start | bytes 3145736 | tf_op jit(solution)/shard_map/ppermute | solution.py:39
  302.1 52.9 %collective-permute-start.42 = (bf16[256,2048]{1,0:T(8,128)(2,1)}, bf16[256,2048]{1,0:T(8,128)(2,1)}, u32[]{:S(2)}, u32[]{:S(2)}) collective-permute-start(bf16[256,2048]{1,0:T(8,128)(2,1)} %get-tuple-element.238), channel_id=1, source_target_pairs={{0,1},{1,0},{2,3},{3,2},{4,5},{5,4},{6,7},{7,6},{8,9},{9,8},{10,11... | collective-permute-start | bytes 3145736 | tf_op jit(solution)/shard_map/ppermute | solution.py:39
  353.4 49.3 %collective-permute-start.78 = (bf16[512,1024]{1,0:T(8,128)(2,1)}, bf16[512,1024]{1,0:T(8,128)(2,1)S(1)}, u32[]{:S(2)}, u32[]{:S(2)}) collective-permute-start(bf16[512,1024]{1,0:T(8,128)(2,1)} %join_rows.9), channel_id=1, source_target_pairs={{0,16},{16,0},{1,17},{17,1},{2,18},{18,2},{3,19},{19,3},{4,20},{20... | collective-permute-start | bytes 3145736 | tf_op jit(solution)/shard_map/ppermute | solution.py:39
  355.0 50.9 %collective-permute-start.95 = (bf16[256,2048]{1,0:T(8,128)(2,1)}, bf16[256,2048]{1,0:T(8,128)(2,1)S(1)}, u32[]{:S(2)}, u32[]{:S(2)}) collective-permute-start(bf16[256,2048]{1,0:T(8,128)(2,1)} %collective-permute-done.94), channel_id=1, source_target_pairs={{0,1},{1,0},{2,3},{3,2},{4,5},{5,4},{6,7},{7,6},{8,9},{9,8},{10,11... | collective-permute-start | bytes 3145736 | tf_op jit(solution)/shard_map/ppermute | solution.py:39
  402.7 79.1 %collective-permute-start.68 = (bf16[512,1024]{1,0:T(8,128)(2,1)S(1)}, bf16[512,1024]{1,0:T(8,128)(2,1)S(1)}, u32[]{:S(2)}, u32[]{:S(2)}) collective-permute-start(bf16[512,1024]{1,0:T(8,128)(2,1)S(1)} %copy-done.54), channel_id=1, source_target_pairs={{0,16},{16,0},{1,17},{17,1},{2,18},{18,2},{3,19},{19,3},{4,20},{20... | collective-permute-start | bytes 3145736 | tf_op jit(solution)/shard_map/ppermute | solution.py:39
  402.7 61.7 %collective-permute-start.80 = (bf16[512,1024]{1,0:T(8,128)(2,1)S(1)}, bf16[512,1024]{1,0:T(8,128)(2,1)S(1)}, u32[]{:S(2)}, u32[]{:S(2)}) collective-permute-start(bf16[512,1024]{1,0:T(8,128)(2,1)S(1)} %collective-permute-done.78), channel_id=1, source_target_pairs={{0,8},{8,0},{1,9},{9,1},{2,10},{10,2},{3,11},{11,3},{4,12},{12,4},... | collective-permute-start | bytes 3145736 | tf_op jit(solution)/shard_map/ppermute | solution.py:39
  409.2 75.1 %collective-permute-start.47 = (bf16[128,2048]{1,0:T(8,128)(2,1)S(1)}, bf16[128,2048]{1,0:T(8,128)(2,1)S(1)}, u32[]{:S(2)}, u32[]{:S(2)}) collective-permute-start(bf16[128,2048]{1,0:T(8,128)(2,1)S(1)} %slice.668), channel_id=1, source_target_pairs={{0,4},{4,0},{1,5},{5,1},{2,6},{6,2},{3,7},{7,3},{8,12},{12,8},{9,1... | collective-permute-start | bytes 1572872 | tf_op jit(solution)/shard_map/ppermute | solution.py:39
  411.2 73.3 %collective-permute-start.48 = (bf16[128,2048]{1,0:T(8,128)(2,1)S(1)}, bf16[128,2048]{1,0:T(8,128)(2,1)S(1)}, u32[]{:S(2)}, u32[]{:S(2)}) collective-permute-start(bf16[128,2048]{1,0:T(8,128)(2,1)S(1)} %slice.669), channel_id=1, source_target_pairs={{0,2},{2,0},{1,3},{3,1},{4,6},{6,4},{5,7},{7,5},{8,10},{10,8},{9,1... | collective-permute-start | bytes 1572872 | tf_op jit(solution)/shard_map/ppermute | solution.py:39
  422.1 55.9 %collective-permute-start.44 = (bf16[256,2048]{1,0:T(8,128)(2,1)}, bf16[256,2048]{1,0:T(8,128)(2,1)S(1)}, u32[]{:S(2)}, u32[]{:S(2)}) collective-permute-start(bf16[256,2048]{1,0:T(8,128)(2,1)} %collective-permute-done.43), channel_id=1, source_target_pairs={{0,1},{1,0},{2,3},{3,2},{4,5},{5,4},{6,7},{7,6},{8,9},{9,8},{10,11... | collective-permute-start | bytes 3145736 | tf_op jit(solution)/shard_map/ppermute | solution.py:39
  484.3 67.3 %collective-permute-start.70 = (bf16[512,1024]{1,0:T(8,128)(2,1)S(1)}, bf16[512,1024]{1,0:T(8,128)(2,1)S(1)}, u32[]{:S(2)}, u32[]{:S(2)}) collective-permute-start(bf16[512,1024]{1,0:T(8,128)(2,1)S(1)} %collective-permute-done.68), channel_id=1, source_target_pairs={{0,8},{8,0},{1,9},{9,1},{2,10},{10,2},{3,11},{11,3},{4,12},{12,4},... | collective-permute-start | bytes 3145736 | tf_op jit(solution)/shard_map/ppermute | solution.py:39
  527.0 68.8 %collective-permute-start.60 = (bf16[512,1024]{1,0:T(8,128)(2,1)S(1)}, bf16[512,1024]{1,0:T(8,128)(2,1)}, u32[]{:S(2)}, u32[]{:S(2)}) collective-permute-start(bf16[512,1024]{1,0:T(8,128)(2,1)S(1)} %collective-permute-done.58), channel_id=1, source_target_pairs={{0,8},{8,0},{1,9},{9,1},{2,10},{10,2},{3,11},{11,3},{4,12},{12,4},... | collective-permute-start | bytes 3145736 | tf_op jit(solution)/shard_map/ppermute | solution.py:39
  636.6 148.4 %collective-permute-start.159 = (bf16[512,1024]{1,0:T(8,128)(2,1)}, bf16[512,1024]{1,0:T(8,128)(2,1)}, u32[]{:S(2)}, u32[]{:S(2)}) collective-permute-start(bf16[512,1024]{1,0:T(8,128)(2,1)} %fusion.74), channel_id=1, source_target_pairs={{0,8},{8,0},{1,9},{9,1},{2,10},{10,2},{3,11},{11,3},{4,12},{12,4},... | collective-permute-start | bytes 3145736 | tf_op jit(solution)/shard_map/ppermute | solution.py:39
  636.6 93.6 %collective-permute-start.160 = (bf16[512,1024]{1,0:T(8,128)(2,1)}, bf16[512,1024]{1,0:T(8,128)(2,1)}, u32[]{:S(2)}, u32[]{:S(2)}) collective-permute-start(bf16[512,1024]{1,0:T(8,128)(2,1)} %fusion.80), channel_id=1, source_target_pairs={{0,8},{8,0},{1,9},{9,1},{2,10},{10,2},{3,11},{11,3},{4,12},{12,4},... | collective-permute-start | bytes 3145736 | tf_op jit(solution)/shard_map/ppermute | solution.py:39
  638.6 97.3 %collective-permute-start.170 = (bf16[512,1024]{1,0:T(8,128)(2,1)}, bf16[512,1024]{1,0:T(8,128)(2,1)}, u32[]{:S(2)}, u32[]{:S(2)}) collective-permute-start(bf16[512,1024]{1,0:T(8,128)(2,1)} %fusion.86), channel_id=1, source_target_pairs={{0,8},{8,0},{1,9},{9,1},{2,10},{10,2},{3,11},{11,3},{4,12},{12,4},... | collective-permute-start | bytes 3145736 | tf_op jit(solution)/shard_map/ppermute | solution.py:39
  638.7 111.3 %collective-permute-start.150 = (bf16[512,1024]{1,0:T(8,128)(2,1)}, bf16[512,1024]{1,0:T(8,128)(2,1)}, u32[]{:S(2)}, u32[]{:S(2)}) collective-permute-start(bf16[512,1024]{1,0:T(8,128)(2,1)} %fusion.77), channel_id=1, source_target_pairs={{0,8},{8,0},{1,9},{9,1},{2,10},{10,2},{3,11},{11,3},{4,12},{12,4},... | collective-permute-start | bytes 3145736 | tf_op jit(solution)/shard_map/ppermute | solution.py:39
  644.3 98.4 %collective-permute-start.87 = (bf16[256,2048]{1,0:T(8,128)(2,1)}, bf16[256,2048]{1,0:T(8,128)(2,1)S(1)}, u32[]{:S(2)}, u32[]{:S(2)}) collective-permute-start(bf16[256,2048]{1,0:T(8,128)(2,1)} %slice.978), channel_id=1, source_target_pairs={{0,1},{1,0},{2,3},{3,2},{4,5},{5,4},{6,7},{7,6},{8,9},{9,8},{10,11... | collective-permute-start | bytes 3145736 | tf_op jit(solution)/shard_map/ppermute | solution.py:39
  747.1 55.0 %collective-permute-start.100 = (bf16[256,2048]{1,0:T(8,128)(2,1)S(1)}, bf16[256,2048]{1,0:T(8,128)(2,1)S(1)}, u32[]{:S(2)}, u32[]{:S(2)}) collective-permute-start(bf16[256,2048]{1,0:T(8,128)(2,1)S(1)} %slice.977), channel_id=1, source_target_pairs={{0,1},{1,0},{2,3},{3,2},{4,5},{5,4},{6,7},{7,6},{8,9},{9,8},{10,11... | collective-permute-start | bytes 3145736 | tf_op jit(solution)/shard_map/ppermute | solution.py:39
  747.8 48.8 %collective-permute-start.161 = (bf16[512,1024]{1,0:T(8,128)(2,1)}, bf16[512,1024]{1,0:T(8,128)(2,1)S(1)}, u32[]{:S(2)}, u32[]{:S(2)}) collective-permute-start(bf16[512,1024]{1,0:T(8,128)(2,1)} %add_convert_fusion.3), channel_id=1, source_target_pairs={{0,16},{16,0},{1,17},{17,1},{2,18},{18,2},{3,19},{19,3},{4,20},{20... | collective-permute-start | bytes 3145736 | tf_op jit(solution)/shard_map/ppermute | solution.py:39
  802.1 68.6 %collective-permute-start.169 = (bf16[512,1024]{1,0:T(8,128)(2,1)S(1)}, bf16[512,1024]{1,0:T(8,128)(2,1)S(1)}, u32[]{:S(2)}, u32[]{:S(2)}) collective-permute-start(bf16[512,1024]{1,0:T(8,128)(2,1)S(1)} %copy-done.125), channel_id=1, source_target_pairs={{0,8},{8,0},{1,9},{9,1},{2,10},{10,2},{3,11},{11,3},{4,12},{12,4},... | collective-permute-start | bytes 3145736 | tf_op jit(solution)/shard_map/ppermute | solution.py:39
  802.3 88.8 %collective-permute-start.149 = (bf16[512,1024]{1,0:T(8,128)(2,1)S(1)}, bf16[512,1024]{1,0:T(8,128)(2,1)S(1)}, u32[]{:S(2)}, u32[]{:S(2)}) collective-permute-start(bf16[512,1024]{1,0:T(8,128)(2,1)S(1)} %fusion.71), channel_id=1, source_target_pairs={{0,8},{8,0},{1,9},{9,1},{2,10},{10,2},{3,11},{11,3},{4,12},{12,4},... | collective-permute-start | bytes 3145736 | tf_op jit(solution)/shard_map/ppermute | solution.py:39
  804.2 94.4 %collective-permute-start.81 = (bf16[256,2048]{1,0:T(8,128)(2,1)S(1)}, bf16[256,2048]{1,0:T(8,128)(2,1)}, u32[]{:S(2)}, u32[]{:S(2)}) collective-permute-start(bf16[256,2048]{1,0:T(8,128)(2,1)S(1)} %copy-done.60), channel_id=1, source_target_pairs={{0,1},{1,0},{2,3},{3,2},{4,5},{5,4},{6,7},{7,6},{8,9},{9,8},{10,11... | collective-permute-start | bytes 3145736 | tf_op jit(solution)/shard_map/ppermute | solution.py:39
  804.2 88.2 %collective-permute-start.171 = (bf16[512,1024]{1,0:T(8,128)(2,1)S(1)}, bf16[512,1024]{1,0:T(8,128)(2,1)S(1)}, u32[]{:S(2)}, u32[]{:S(2)}) collective-permute-start(bf16[512,1024]{1,0:T(8,128)(2,1)S(1)} %copy-done.126), channel_id=1, source_target_pairs={{0,16},{16,0},{1,17},{17,1},{2,18},{18,2},{3,19},{19,3},{4,20},{20... | collective-permute-start | bytes 3145736 | tf_op jit(solution)/shard_map/ppermute | solution.py:39
  810.0 96.1 %collective-permute-start.151 = (bf16[512,1024]{1,0:T(8,128)(2,1)S(1)}, bf16[512,1024]{1,0:T(8,128)(2,1)S(1)}, u32[]{:S(2)}, u32[]{:S(2)}) collective-permute-start(bf16[512,1024]{1,0:T(8,128)(2,1)S(1)} %add_convert_fusion.5), channel_id=1, source_target_pairs={{0,16},{16,0},{1,17},{17,1},{2,18},{18,2},{3,19},{19,3},{4,20},{20... | collective-permute-start | bytes 3145736 | tf_op jit(solution)/shard_map/ppermute | solution.py:39
  917.3 100.0 %collective-permute-start.162 = (bf16[64,1024]{1,0:T(8,128)(2,1)}, bf16[64,1024]{1,0:T(8,128)(2,1)S(1)}, u32[]{:S(2)}, u32[]{:S(2)}) collective-permute-start(bf16[64,1024]{1,0:T(8,128)(2,1)} %get-tuple-element.175), channel_id=1, source_target_pairs={{0,1},{1,0},{2,3},{3,2},{4,5},{5,4},{6,7},{7,6},{8,9},{9,8},{10,11... | collective-permute-start | bytes 393224 | tf_op jit(solution)/shard_map/ppermute | solution.py:45
  951.0 68.2 %collective-permute-start.163 = (bf16[64,1024]{1,0:T(8,128)(2,1)S(1)}, bf16[64,1024]{1,0:T(8,128)(2,1)S(1)}, u32[]{:S(2)}, u32[]{:S(2)}) collective-permute-start(bf16[64,1024]{1,0:T(8,128)(2,1)S(1)} %copy-done.166), channel_id=1, source_target_pairs={{0,2},{1,3},{2,0},{3,1},{4,6},{5,7},{6,4},{7,5},{8,10},{9,11},{10,... | collective-permute-start | bytes 393224 | tf_op jit(solution)/shard_map/ppermute | solution.py:45
  956.9 62.6 %collective-permute-start.164 = (bf16[64,1024]{1,0:T(8,128)(2,1)S(1)}, bf16[64,1024]{1,0:T(8,128)(2,1)S(1)}, u32[]{:S(2)}, u32[]{:S(2)}) collective-permute-start(bf16[64,1024]{1,0:T(8,128)(2,1)S(1)} %copy-done.165), channel_id=1, source_target_pairs={{0,3},{1,2},{2,1},{3,0},{4,7},{5,6},{6,5},{7,4},{8,11},{9,10},{10,... | collective-permute-start | bytes 393224 | tf_op jit(solution)/shard_map/ppermute | solution.py:45
  962.7 57.3 %collective-permute-start.165 = (bf16[64,1024]{1,0:T(8,128)(2,1)S(1)}, bf16[64,1024]{1,0:T(8,128)(2,1)S(1)}, u32[]{:S(2)}, u32[]{:S(2)}) collective-permute-start(bf16[64,1024]{1,0:T(8,128)(2,1)S(1)} %copy-done.164), channel_id=1, source_target_pairs={{0,4},{1,5},{2,6},{3,7},{4,0},{5,1},{6,2},{7,3},{8,12},{9,13},{10,... | collective-permute-start | bytes 393224 | tf_op jit(solution)/shard_map/ppermute | solution.py:45
  (344 other events, 5908.6 us)

commit v2 on v1

v2 whole, which is shorter than its diff:
```python
import functools

import jax
import jax.numpy as jnp
from jax import lax
from jax.experimental import pallas as pl
from jax.experimental.pallas import tpu as pltpu
from jax.sharding import Mesh
from jax.sharding import PartitionSpec as P

H = 32
HD = 64
EPSILON = 1e-05
ROPE_BASE = 130000.0
MASKED_SCORE = -1e30
SCALE = HD ** (-0.5)
LANES = 128
MIB = 1 << 20
BF16 = jnp.bfloat16
F32 = jnp.float32
AXES = ("r", "zh", "zl", "y", "x", "c")
NT = (((1,), (1,)), ((), ()))
TN = (((0,), (0,)), ((), ()))


def dot_nn(a, b):
    return jnp.dot(a, b, preferred_element_type=F32)


def dot_nt(a, b):
    return lax.dot_general(a, b, NT, preferred_element_type=F32)


def dot_tn(a, b):
    return lax.dot_general(a, b, TN, preferred_element_type=F32)


def flip(x, axes, masks):
    return lax.ppermute(x, axes, [(i, i ^ masks[i & 1]) for i in range(8)])


def swap(x, axis):
    return lax.ppermute(x, axis, [(0, 1), (1, 0)])


PLACES = ((0, 1, 2, 3, 5, 4, 6, 7), (0, 1, 4, 5, 3, 2, 6, 7))


class Group:
    def __init__(self, d1, d2, half, spread):
        self.axes = (d1, d2, "c")
        self.half, self.spread = half, spread

    def column_order(self, outer):
        names = ("r", "zh", "zl", "y", "x")
        sizes = dict(zip(names, (outer, 2, 2, 2, 2)))
        sequence = ([self.half] if self.half else []) + list(self.spread) + list(self.axes[:2])
        order = [0]
        for name in sequence:
            step = 1
            for later in names[names.index(name) + 1 :]:
                step *= sizes[later]
            order = [base + step * i for base in order for i in range(sizes[name])]
        return order

    def reorder(self, x, order):
        if order == list(range(len(order))):
            return x
        width = x.shape[1] // len(order)
        return jnp.concatenate([x[:, i * width : (i + 1) * width] for i in order], axis=1)

    def flip_halves(self, x):
        if not self.half:
            return x
        width = x.shape[1] // 2
        at = lax.axis_index(self.half)
        first = lax.dynamic_slice_in_dim(x, at * width, width, axis=1)
        return jnp.concatenate([first, lax.dynamic_slice_in_dim(x, (1 - at) * width, width, axis=1)], axis=1)

    def to_slots(self, x, outer):
        return self.flip_halves(self.reorder(x, self.column_order(outer)))

    def from_slots(self, x, outer):
        order = self.column_order(outer)
        return self.reorder(self.flip_halves(x), [order.index(i) for i in range(len(order))])

    def other_core(self, x):
        return flip(x, self.axes, (1, 1))

    def near(self, x):
        return flip(x, self.axes, (2, 4))

    def far(self, x):
        return flip(x, self.axes, (4, 2))

    def gather_tokens(self, x):
        partner = self.other_core(x)
        near_one = self.near(x)
        near_two = self.near(partner)
        far_one = self.far(near_one)
        parts = [x, partner, near_one, near_two, self.other_core(near_one), self.other_core(near_two)]
        return jnp.concatenate(parts + [far_one, self.other_core(far_one)], axis=0)

    def scatter_tokens(self, partial):
        def cut(whole):
            size = whole.shape[0] // 2
            return whole[:size], whole[size:]

        six, seven = cut(partial(6, 8))
        six = six + self.other_core(seven.astype(BF16)).astype(F32)
        far_one = self.far(six.astype(BF16)).astype(F32)
        four, five = cut(partial(4, 6))
        four = self.other_core(four.astype(BF16)).astype(F32)
        five = self.other_core(five.astype(BF16)).astype(F32)
        two, three = cut(partial(2, 4))
        near_two = self.near((three + five).astype(BF16)).astype(F32)
        near_one = self.near((two + four + far_one).astype(BF16)).astype(F32)
        zero, one = cut(partial(0, 2))
        partner = self.other_core((one + near_two).astype(BF16)).astype(F32)
        return zero + near_one + partner

    def share_columns(self, weight):
        return lax.all_to_all(weight, self.axes, split_axis=1, concat_axis=0, tiled=True)

    def gather_weight(self, rows):
        rows = lax.all_gather(rows, self.spread, axis=0, tiled=True)
        if self.half:
            rows = jnp.concatenate([rows, swap(rows, self.half)], axis=0)
        return rows

    def scatter_weight(self, left, right):
        if self.half:
            width = left.shape[1] // 2
            away = swap(dot_tn(left[:, width:], right).astype(BF16), self.half)
            grad = (dot_tn(left[:, :width], right) + away.astype(F32)).astype(BF16)
        else:
            grad = dot_tn(left, right).astype(BF16)
        return lax.psum_scatter(grad, self.spread, scatter_dimension=0, tiled=True)

    def return_columns(self, grad):
        return lax.all_to_all(grad, self.axes, split_axis=0, concat_axis=1, tiled=True)


def scalars(values):
    return jnp.stack(values).astype(jnp.int32)


VMEM_SPEC = pl.BlockSpec(memory_space=pltpu.VMEM)


def cost(flops, moved):
    return pl.CostEstimate(flops=flops, bytes_accessed=moved, transcendentals=0)


def parts_of(width, count, unit):
    out = []
    at = 0
    for device in range(8):
        for p in range(width // unit):
            for i in range(count):
                out.append((i, device * width + p * unit, at))
                at += unit
    return out


def mix_columns(weights, gain, unit):
    rows, width = weights[0].shape[0], weights[0].shape[1] // 8
    parts = parts_of(width, len(weights), unit)

    def body(gain_ref, *refs):
        factor = gain_ref[...]
        for i, source, at in parts:
            refs[-1][:, at : at + unit] = (refs[i][:, source : source + unit].astype(F32) * factor).astype(BF16)

    total = 8 * width * len(weights)
    return pl.pallas_call(
        body,
        out_shape=jax.ShapeDtypeStruct((rows, total), BF16),
        in_specs=[VMEM_SPEC] * (1 + len(weights)),
        out_specs=VMEM_SPEC,
        cost_estimate=cost(rows * total, 4 * rows * total),
        name="mix_columns",
    )(gain, *weights)


def part_columns(mixed, weights, gain, unit):
    count = len(weights)
    rows, width = weights[0].shape[0], weights[0].shape[1] // 8
    parts = parts_of(width, count, unit)

    def body(mixed_ref, gain_ref, *refs):
        ins, outs = refs[:count], refs[count:-1]
        factor = gain_ref[...]
        acc = jnp.zeros((rows, LANES), F32)
        for i, source, at in parts:
            value = mixed_ref[:, at : at + unit].astype(F32)
            term = ins[i][:, source : source + unit].astype(F32) * value
            for p in range(unit // LANES):
                acc = acc + term[:, p * LANES : (p + 1) * LANES]
            outs[i][:, source : source + unit] = value * factor
        refs[-1][...] = jnp.sum(acc, axis=1, keepdims=True)

    return pl.pallas_call(
        body,
        out_shape=[jax.ShapeDtypeStruct(w.shape, F32) for w in weights] + [jax.ShapeDtypeStruct((rows, 1), F32)],
        in_specs=[VMEM_SPEC] * (2 + count),
        out_specs=[VMEM_SPEC] * (count + 1),
        cost_estimate=cost(4 * rows * width * 8 * count, 8 * rows * width * 8 * count),
        name="part_columns",
    )(mixed, gain, *weights)


def rope(x, cosine, sine):
    lane = lax.broadcasted_iota(jnp.int32, x.shape, 1)
    other = jnp.where(lane % HD < HD // 2, pltpu.roll(x, LANES - HD // 2, 1), pltpu.roll(x, HD // 2, 1))
    return x * cosine + other * sine


def head_masks(shape):
    lane = lax.broadcasted_iota(jnp.int32, shape, 1)
    return [lane < HD, lane >= HD]


def attend_body(place_ref, proj_ref, cos_ref, sin_ref, start_ref, saved_ref, mixed_ref, lse_ref, *, blocks, size):
    base = pl.program_id(1) * blocks

    def slot_rows(j):
        return pl.ds(pl.multiple_of(place_ref[base + j] * size, size), size)

    for j in range(blocks):
        rows = slot_rows(j)
        here = slice(j * size, (j + 1) * size)
        cosine, sine = cos_ref[rows, :], sin_ref[rows, :]
        for p in range(2):
            value = proj_ref[rows, p * LANES : (p + 1) * LANES]
            saved_ref[here, p * LANES : (p + 1) * LANES] = rope(value, cosine, sine).astype(BF16)
        saved_ref[here, 2 * LANES :] = proj_ref[rows, 2 * LANES :].astype(BF16)
    for j in range(blocks):
        here = slice(j * size, (j + 1) * size)
        upto = (j + 1) * size
        query = saved_ref[here, :LANES]
        keys = saved_ref[:upto, LANES : 2 * LANES]
        values = saved_ref[:upto, 2 * LANES :]
        row = lax.broadcasted_iota(jnp.int32, (size, upto), 0) + j * size
        col = lax.broadcasted_iota(jnp.int32, (size, upto), 1)
        visible = (col <= row) & (col >= start_ref[slot_rows(j), :])
        q_heads = head_masks(query.shape)
        v_heads = head_masks(values.shape)
        mixed, totals = [], []
        for h in range(2):
            scores = dot_nt(jnp.where(q_heads[h], query, jnp.zeros_like(query)), keys) * SCALE
            scores = jnp.where(visible, scores, MASKED_SCORE)
            top = jnp.max(scores, axis=1, keepdims=True)
            weights = jnp.exp(scores - top)
            total = jnp.sum(weights, axis=1, keepdims=True)
            probs = (weights * (1.0 / total)).astype(BF16)
            mixed.append(dot_nn(probs, jnp.where(v_heads[h], values, jnp.zeros_like(values))))
            totals.append(jnp.broadcast_to(top + jnp.log(total), query.shape))
        mixed_ref[slot_rows(j), :] = (mixed[0] + mixed[1]).astype(BF16)
        lse_ref[here, :] = jnp.where(q_heads[0], totals[0], totals[1])


def attend_back_body(place_ref, saved_ref, lse_ref, grad_ref, cos_ref, sin_ref, start_ref, out_ref, dk_ref, dv_ref, *, blocks, size):
    base = pl.program_id(1) * blocks

    def slot_rows(j):
        return pl.ds(pl.multiple_of(place_ref[base + j] * size, size), size)

    dk_ref[...] = jnp.zeros_like(dk_ref)
    dv_ref[...] = jnp.zeros_like(dv_ref)
    for j in range(blocks):
        here = slice(j * size, (j + 1) * size)
        upto = (j + 1) * size
        rows = slot_rows(j)
        query = saved_ref[here, :LANES]
        keys = saved_ref[:upto, LANES : 2 * LANES]
        values = saved_ref[:upto, 2 * LANES :]
        grad = grad_ref[rows, :]
        row = lax.broadcasted_iota(jnp.int32, (size, upto), 0) + j * size
        col = lax.broadcasted_iota(jnp.int32, (size, upto), 1)
        visible = (col <= row) & (col >= start_ref[rows, :])
        q_heads = head_masks(query.shape)
        k_heads = head_masks(keys.shape)
        dq = jnp.zeros(query.shape, F32)
        dk = jnp.zeros(keys.shape, F32)
        dv = jnp.zeros(keys.shape, F32)
        for h in range(2):
            q_head = jnp.where(q_heads[h], query, jnp.zeros_like(query))
            g_head = jnp.where(q_heads[h], grad, jnp.zeros_like(grad))
            scores = dot_nt(q_head, keys) * SCALE
            log_total = lse_ref[here, h * HD : h * HD + 1]
            probs = jnp.exp(jnp.where(visible, scores, MASKED_SCORE) - log_total)
            d_probs = dot_nt(g_head, values)
            inner = jnp.sum(probs * d_probs, axis=1, keepdims=True)
            d_scores = (probs * (d_probs - inner)).astype(BF16)
            dq += dot_nn(d_scores, jnp.where(k_heads[h], keys, jnp.zeros_like(keys)))
            dk += dot_tn(d_scores, q_head)
            dv += dot_tn(probs.astype(BF16), g_head)
        out_ref[rows, :LANES] = rope(dq * SCALE, cos_ref[rows, :], -sin_ref[rows, :]).astype(BF16)
        dk_ref[:upto, :] += dk
        dv_ref[:upto, :] += dv
    for j in range(blocks):
        here = slice(j * size, (j + 1) * size)
        rows = slot_rows(j)
        out_ref[rows, LANES : 2 * LANES] = rope(dk_ref[here, :] * SCALE, cos_ref[rows, :], -sin_ref[rows, :]).astype(BF16)
        out_ref[rows, 2 * LANES :] = dv_ref[here, :].astype(BF16)


def by_pair(tokens, width):
    return pl.BlockSpec((tokens, width), lambda p, s, places: (0, p))


def by_sequence(length, width):
    return pl.BlockSpec((length, width), lambda p, s, places: (s, p))


def table(tokens, width):
    return pl.BlockSpec((tokens, width), lambda p, s, places: (0, 0))


def attend(proj, cosine, sine, start, places, size, length):
    tokens = proj.shape[0]
    pairs = proj.shape[1] // (3 * LANES)
    body = functools.partial(attend_body, blocks=length // size, size=size)
    return pl.pallas_call(
        body,
        grid_spec=pltpu.PrefetchScalarGridSpec(
            num_scalar_prefetch=1,
            grid=(pairs, tokens // length),
            in_specs=[by_pair(tokens, 3 * LANES), table(tokens, LANES), table(tokens, LANES), table(tokens, 1)],
            out_specs=[by_sequence(length, 3 * LANES), by_pair(tokens, LANES), by_sequence(length, LANES)],
        ),
        out_shape=[
            jax.ShapeDtypeStruct(proj.shape, BF16),
            jax.ShapeDtypeStruct((tokens, pairs * LANES), BF16),
            jax.ShapeDtypeStruct((tokens, pairs * LANES), F32),
        ],
        compiler_params=pltpu.CompilerParams(vmem_limit_bytes=48 * MIB),
        cost_estimate=cost(16 * tokens * length * pairs * LANES, 16 * tokens * pairs * LANES),
        name="attend",
    )(places, proj, cosine, sine, start)


def attend_back(saved, lse, grad, cosine, sine, start, places, size, length):
    tokens = saved.shape[0]
    pairs = saved.shape[1] // (3 * LANES)
    body = functools.partial(attend_back_body, blocks=length // size, size=size)
    return pl.pallas_call(
        body,
        grid_spec=pltpu.PrefetchScalarGridSpec(
            num_scalar_prefetch=1,
            grid=(pairs, tokens // length),
            in_specs=[
                by_sequence(length, 3 * LANES),
                by_sequence(length, LANES),
                by_pair(tokens, LANES),
                table(tokens, LANES),
                table(tokens, LANES),
                table(tokens, 1),
            ],
            out_specs=by_pair(tokens, 3 * LANES),
            scratch_shapes=[pltpu.VMEM((length, LANES), F32), pltpu.VMEM((length, LANES), F32)],
        ),
        out_shape=jax.ShapeDtypeStruct(saved.shape, BF16),
        compiler_params=pltpu.CompilerParams(vmem_limit_bytes=48 * MIB),
        cost_estimate=cost(40 * tokens * length * pairs * LANES, 16 * tokens * pairs * LANES),
        name="attend_back",
    )(places, saved, lse, grad, cosine, sine, start)


def rms_rows(values):
    factor = lax.rsqrt(jnp.mean(values * values, axis=-1, keepdims=True) + EPSILON)
    return values * factor, factor


def norm_input(inner, normed, factor):
    return factor * (inner - normed * jnp.mean(inner * normed, axis=-1, keepdims=True))


def rope_tables(positions):
    inverse_freq = 1.0 / ROPE_BASE ** (jnp.arange(0, HD, 2, dtype=F32) / HD)
    angles = positions.astype(F32)[:, None] * inverse_freq
    cosine, sine = jnp.cos(angles), jnp.sin(angles)
    return (
        jnp.concatenate([cosine] * 4, axis=1),
        jnp.concatenate([-sine, sine, -sine, sine], axis=1),
    )


ATTN = Group("y", "x", None, ("r", "zh", "zl"))
MLP = Group("zl", "y", "x", ("r", "zh"))


def local(tokens, positions, attn_gain, w_query, w_key, w_value, w_out, mlp_gain, w_gate, w_up, w_down, out_grad):
    own = tokens.shape[1]
    model = tokens.shape[2]
    length = own * lax.axis_size("x") * lax.axis_size("c")
    outer = lax.axis_size("r")
    shape = tokens.shape
    gain_one = attn_gain.astype(F32)[:, None]
    gain_two = mlp_gain.astype(F32)[:, None]
    slice_width = w_gate.shape[1] // 8

    qkv_rows = ATTN.share_columns(mix_columns([w_query, w_key, w_value], gain_one, LANES))
    out_rows = ATTN.share_columns(jnp.transpose(w_out))
    gate_up_rows = MLP.share_columns(mix_columns([w_gate, w_up], gain_two, slice_width))
    down_rows = MLP.share_columns(jnp.transpose(w_down))
    qkv_all = ATTN.gather_weight(qkv_rows)
    out_all = ATTN.gather_weight(out_rows)
    gate_up_all = MLP.gather_weight(gate_up_rows)
    down_all = MLP.gather_weight(down_rows)

    inputs = tokens.reshape(own, model).astype(F32)
    normed_one, factor_one = rms_rows(inputs)
    one_all = ATTN.gather_tokens(ATTN.to_slots(normed_one.astype(BF16), outer))
    where = ATTN.gather_tokens(positions.reshape(own, 1)).reshape(-1)
    cosine, sine = rope_tables(where)
    place = lax.axis_index("x") * 2 + lax.axis_index("c")
    core = lax.axis_index("c")
    order = [jnp.where(core == 0, PLACES[0][i], PLACES[1][i]) for i in range(8)]
    slot_part = [jnp.where(core == 0, PLACES[0].index(i), PLACES[1].index(i)) for i in range(8)]
    parts = scalars(slot_part)
    places = parts[scalars([s * 4 + (j ^ place) for s in range(2) for j in range(4)])]
    first_row = (scalars(order) % 4 ^ place) * own
    start = (jnp.repeat(first_row, own) + jnp.tile(jnp.arange(own, dtype=jnp.int32), 8) - where)[:, None]
    proj = dot_nn(one_all, qkv_all)
    saved, mixed, lse = attend(proj, cosine, sine, start, places, own, length)

    def rows_of(array, begin, end):
        return array[begin * own : end * own]

    attn_out = ATTN.scatter_tokens(lambda i, j: dot_nt(rows_of(mixed, i, j), out_all))
    first_sum = inputs + ATTN.from_slots(attn_out, outer)

    grad_rows = out_grad.reshape(own, model)
    dy_all = MLP.gather_tokens(MLP.to_slots(grad_rows, outer))
    normed_two, factor_two = rms_rows(first_sum)
    two_all = MLP.gather_tokens(MLP.to_slots(normed_two.astype(BF16), outer))
    gate_up = dot_nn(two_all, gate_up_all)
    gate, up = gate_up[:, :slice_width], gate_up[:, slice_width:]
    sigmoid = jax.nn.sigmoid(gate)
    hidden = (gate * sigmoid * up).astype(BF16)
    down_grad = MLP.scatter_weight(dy_all, hidden)
    d_hidden = dot_nn(dy_all, down_all)
    d_up = (d_hidden * gate * sigmoid).astype(BF16)
    d_gate = (d_hidden * up * sigmoid * (1.0 + gate * (1.0 - sigmoid))).astype(BF16)
    d_gate_up = jnp.concatenate([d_gate, d_up], axis=1)
    inner_two = MLP.scatter_tokens(lambda i, j: dot_nt(rows_of(d_gate_up, i, j), gate_up_all))
    mlp_out = MLP.scatter_tokens(lambda i, j: dot_nt(rows_of(hidden, i, j), down_all))
    block_out = (first_sum + MLP.from_slots(mlp_out, outer)).astype(BF16)
    gate_up_grad = MLP.scatter_weight(two_all, d_gate_up)

    d_first = grad_rows.astype(F32) + norm_input(MLP.from_slots(inner_two, outer), normed_two, factor_two)
    d_attn_all = ATTN.gather_tokens(ATTN.to_slots(d_first.astype(BF16), outer))
    d_mixed = dot_nn(d_attn_all, out_all).astype(BF16)
    out_grad_rows = ATTN.scatter_weight(d_attn_all, mixed)
    d_qkv = attend_back(saved, lse, d_mixed, cosine, sine, start, places, own, length)
    inner_one = ATTN.scatter_tokens(lambda i, j: dot_nt(rows_of(d_qkv, i, j), qkv_all))
    qkv_grad = ATTN.scatter_weight(one_all, d_qkv)
    tokens_grad = d_first + norm_input(ATTN.from_slots(inner_one, outer), normed_one, factor_one)

    down_w = MLP.return_columns(down_grad)
    out_w = ATTN.return_columns(out_grad_rows)
    gate_w, up_w, gain_mlp = part_columns(MLP.return_columns(gate_up_grad), [w_gate, w_up], gain_two, slice_width)
    query_w, key_w, value_w, gain_attn = part_columns(ATTN.return_columns(qkv_grad), [w_query, w_key, w_value], gain_one, LANES)
    return (
        block_out.reshape(shape),
        tokens_grad.astype(BF16).reshape(shape),
        gain_attn.reshape(-1),
        query_w,
        key_w,
        value_w,
        jnp.transpose(out_w.astype(F32)),
        gain_mlp.reshape(-1),
        gate_w,
        up_w,
        jnp.transpose(down_w.astype(F32)),
    )


def solution(mesh):
    fsdp = mesh.shape["fsdp"]
    sizes = (fsdp // 8, 2, 2, 2, mesh.shape["ctx"] // 2, 2)
    fine = Mesh(mesh.devices.reshape(sizes), AXES)
    rows, cols = AXES[:4], AXES[4:]
    tokens, places, vector = P(rows, cols, None), P(rows, cols), P(AXES)
    first, second = P(AXES, None), P(None, AXES)
    in_specs = (tokens, places, vector, first, first, first, second, vector, first, first, second, tokens)
    out_specs = (tokens, tokens, vector, first, first, first, second, vector, first, first, second)
    return jax.shard_map(local, mesh=fine, in_specs=in_specs, out_specs=out_specs, check_vma=False)
```

time: 1190 us -> 931 us (0.78)
  the two profiles are of different devices: /device:TPU:0 before, /device:TPU:17 now
where the time goes in v2:
time: 931 us; the launch traced here: 921 us
  waiting for transfers between devices  355 us (38%)
  matrix products  189 us (20%)
  starting transfers between devices  135 us (15%)
  local copies, waits for them, and re-layouts  115 us (12%)
  Pallas kernels  60.7 us (7%)
  other arithmetic  50.1 us (5%)
  between operations  15.6 us (2%)
    ppermute x63, waiting for transfers between devices, flip(): return lax.ppermute(x, axes, [(i, i ^ masks[i & 1]) for i in range(8)])  168 us
    ppermute x4, waiting for transfers between devices, swap(): return lax.ppermute(x, axis, [(0, 1), (1, 0)])  95.2 us
    ppermute x63, starting transfers between devices, flip(): return lax.ppermute(x, axes, [(i, i ^ masks[i & 1]) for i in range(8)])  89 us
    unnamed x201, local copies, waits for them, and re-layouts  78.7 us
    all_gather x4, waiting for transfers between devices, gather_weight(): rows = lax.all_gather(rows, self.spread, axis=0, tiled=True)  73.2 us
    dot_general x16, matrix products, dot_nt(): return lax.dot_general(a, b, NT, preferred_element_type=F32)  66.2 us
    dot_general x4, matrix products, dot_nn(): return jnp.dot(a, b, preferred_element_type=F32)  63.1 us
    dot_general x6, matrix products, dot_tn(): return lax.dot_general(a, b, TN, preferred_element_type=F32)  59.6 us
  transfers between devices with their start and end apart: 83, of which 24 were waited for; matrix products, arithmetic and copies ran while one was open for 30% of the time, Pallas kernels for 6%

profile of v2, /device:TPU:17, one launch (start us, length us, event | category | flops | bytes accessed | tf_op | source)
XLA Modules:
  0.0 920.7 jit_solution(14607318922327102150)
XLA Ops:
  25.0 8.3 all-to-all-done
  33.3 6.7 all-to-all-start.1
  77.8 27.1 %collective-permute-done.2 = bf16[256,2048]{1,0:T(8,128)(2,1)} collective-permute-done((bf16[256,2048]{1,0:T(8,128)(2,1)S(1)}, bf16[256,2048]{1,0:T(8,128)(2,1)}, u32[]{:S(2)}, u32[]{:S(2)}) %collective-permute-start.2) | collective-permute-done | bytes 1048608 | tf_op jit(solution)/shard_map/ppermute | solution.py:39
  127.6 11.7 %fusion.103.proj_ref = f32[2048,768]{1,0:T(8,128)} fusion(bf16[2048,2048]{1,0:T(8,128)(2,1)} %constant_dynamic-update-slice_fusion, bf16[2048,768]{1,0:T(8,128)(2,1)} %all-gather.5.cloned.1.call-done), kind=kOutput, calls=%fused_computation.289 | convolution fusion | flops 6442450944 | bytes 17825792 | tf_op jit(solution)/shard_map/dot_general | solution.py:27
  139.4 21.2 %attend.1 = (bf16[2048,768]{1,0:T(8,128)(2,1)}, bf16[2048,256]{1,0:T(8,128)(2,1)S(1)}, f32[2048,256]{1,0:T(8,128)}) custom-call(s32[8]{0:T(128)S(1)} %gather_fusion, f32[2048,768]{1,0:T(8,128)} %fusion.103.proj_ref, f32[2048,128]{1,0:T(8,128)S(1)} %get-tuple-element.69.cos_ref, f32[2048,128]{1,0:T(8,128)S(1)} %get-tuple-element.70.sin_ref, ...), custom_call_target="tpu_custom_call" | custom-call | flops 8589934592 | bytes 8388608 | tf_op jit(solution)/shard_map/attend/pallas_call | solution.py:325
  191.1 23.7 %collective-permute-done.38 = bf16[256,2048]{1,0:T(8,128)(2,1)} collective-permute-done((bf16[256,2048]{1,0:T(8,128)(2,1)S(1)}, bf16[256,2048]{1,0:T(8,128)(2,1)}, u32[]{:S(2)}, u32[]{:S(2)}) %collective-permute-start.38) | collective-permute-done | bytes 1048608 | tf_op jit(solution)/shard_map/ppermute | solution.py:39
  221.8 14.7 %collective-permute-done.39 = bf16[256,2048]{1,0:T(8,128)(2,1)} collective-permute-done((bf16[256,2048]{1,0:T(8,128)(2,1)}, bf16[256,2048]{1,0:T(8,128)(2,1)}, u32[]{:S(2)}, u32[]{:S(2)}) %collective-permute-start.39) | collective-permute-done | bytes 1048608 | tf_op jit(solution)/shard_map/ppermute | solution.py:39
  242.8 73.2 %all-gather.9.cloned.1.call-done = bf16[1024,2048]{1,0:T(8,128)(2,1)} async-done(((bf16[512,2048]{1,0:T(8,128)(2,1)}), bf16[1024,2048]{1,0:T(8,128)(2,1)}) %all-gather.9.cloned.1.call-update) | async-done | bytes 4194320 | tf_op jit(solution)/shard_map/all_gather | solution.py:126
  349.0 10.6 %collective-permute-done.23 = bf16[256,2048]{1,0:T(8,128)(2,1)S(1)} collective-permute-done((bf16[256,2048]{1,0:T(8,128)(2,1)S(1)}, bf16[256,2048]{1,0:T(8,128)(2,1)S(1)}, u32[]{:S(2)}, u32[]{:S(2)}) %collective-permute-start.23) | collective-permute-done | bytes 1048608 | tf_op jit(solution)/shard_map/ppermute | solution.py:39
  365.9 41.8 %collective-permute-done.28 = bf16[1024,2048]{1,0:T(8,128)(2,1)S(1)} collective-permute-done((bf16[1024,2048]{1,0:T(8,128)(2,1)}, bf16[1024,2048]{1,0:T(8,128)(2,1)S(1)}, u32[]{:S(2)}, u32[]{:S(2)}) %collective-permute-start.28) | collective-permute-done | bytes 4194336 | tf_op jit(solution)/shard_map/ppermute | solution.py:43
  412.5 22.6 %fusion.104 = f32[2048,2048]{0,1:T(8,128)} fusion(bf16[2048,2048]{1,0:T(8,128)(2,1)} %constant_dynamic-update-slice_fusion.33, bf16[2048,2048]{1,0:T(8,128)(2,1)S(1)} %constant_dynamic-update-slice_fusion.41), kind=kOutput, calls=%fused_computation.290 | convolution fusion | flops 17179869184 | bytes 33554432 | tf_op jit(solution)/shard_map/dot_general | solution.py:27
  435.1 22.7 %multiply_convert_fusion = (bf16[2048,1024]{0,1:T(8,128)(2,1)}, bf16[2048,1024]{0,1:T(8,128)(2,1)}, bf16[2048,1024]{0,1:T(8,128)(2,1)}) fusion(f32[2048,2048]{0,1:T(8,128)} %fusion.104, bf16[2048,2048]{1,0:T(8,128)(2,1)} %constant_dynamic-update-slice_fusion.77, bf16[2048,1024]{1,0:T(8,128)(2,1)} %copy-done.27), kind=kOutput, calls=%fused_computation.11 | convolution fusion | flops 8623489024 | bytes 41943040 | tf_op jit(solution)/shard_map/dot_general | solution.py:27
  457.7 8.3 fusion.31
  468.7 6.5 convolution_convert_fusion.4
  486.2 6.5 collective-permute-done.46
  510.2 7.4 fusion.59
  529.6 35.2 %collective-permute-done.66 = bf16[1024,1024]{1,0:T(8,128)(2,1)S(1)} collective-permute-done((bf16[1024,1024]{1,0:T(8,128)(2,1)S(1)}, bf16[1024,1024]{1,0:T(8,128)(2,1)S(1)}, u32[]{:S(2)}, u32[]{:S(2)}) %collective-permute-start.66) | collective-permute-done | bytes 2097184 | tf_op jit(solution)/shard_map/ppermute | solution.py:43
  578.5 17.5 %collective-permute-start.55 = (bf16[256,2048]{1,0:T(8,128)(2,1)}, bf16[256,2048]{1,0:T(8,128)(2,1)S(1)}, u32[]{:S(2)}, u32[]{:S(2)}) collective-permute-start(bf16[256,2048]{1,0:T(8,128)(2,1)} %collective-permute-done.53), channel_id=1, source_target_pairs={{0,1},{1,0},{2,3},{3,2},{4,5},{5,4},{6,7},{7,6},{8,9},{9,8},{10,11... | collective-permute-start | bytes 3145736 | tf_op jit(solution)/shard_map/ppermute | solution.py:39
  596.0 14.8 %fusion.8 = bf16[1024,2048]{1,0:T(8,128)(2,1)} fusion(bf16[2048,1024]{0,1:T(8,128)(2,1)} %get-tuple-element.37, bf16[2048,1024]{0,1:T(8,128)(2,1)} %get-tuple-element.38, bf16[2048,2048]{1,0:T(8,128)(2,1)} %constant_dynamic-update-slice_fusion.33), kind=kOutput, calls=%fused_computation.24 | convolution fusion | flops 8608808960 | bytes 16777216 | tf_op jit(solution)/shard_map/dot_general | solution.py:35
  624.0 7.0 convolution_convert_fusion.5
  637.2 25.7 %attend_back.1 = bf16[2048,768]{1,0:T(8,128)(2,1)} custom-call(s32[8]{0:T(128)S(1)} %gather_fusion, bf16[2048,768]{1,0:T(8,128)(2,1)} %get-tuple-element.22.saved_ref, f32[2048,256]{1,0:T(8,128)} %get-tuple-element.23.lse_ref, bf16[2048,256]{1,0:T(8,128)(2,1)S(1)} %convolution_convert_fusion.6.grad_ref, f32[2048,128]{1,0:T(8,128)S(1)} %get-tuple-element.69.cos_ref, ...), custom_call_target="tpu_custom_call" | custom-call | flops 21474836480 | bytes 8388608 | tf_op jit(solution)/shard_map/attend_back/pallas_call | solution.py:348
  662.9 10.4 %convolution_convert_fusion = bf16[2048,768]{1,0:T(8,128)(2,1)} fusion(bf16[2048,2048]{1,0:T(8,128)(2,1)S(1)} %bitcast.175, bf16[2048,768]{1,0:T(8,128)(2,1)} %attend_back.1), kind=kOutput, calls=%fused_computation.25 | convolution fusion | flops 6444023808 | bytes 14680064 | tf_op jit(solution)/shard_map/dot_general | solution.py:35
  685.1 18.2 %collective-permute-done.65 = bf16[1024,2048]{1,0:T(8,128)(2,1)} collective-permute-done((bf16[1024,2048]{1,0:T(8,128)(2,1)}, bf16[1024,2048]{1,0:T(8,128)(2,1)}, u32[]{:S(2)}, u32[]{:S(2)}) %collective-permute-start.65) | collective-permute-done | bytes 4194336 | tf_op jit(solution)/shard_map/ppermute | solution.py:43
  703.3 14.3 %add_convert_fusion = bf16[1024,2048]{1,0:T(8,128)(2,1)} fusion(bf16[1024,2048]{1,0:T(8,128)(2,1)} %collective-permute-done.65, bf16[2048,1024]{0,1:T(8,128)(2,1)S(1)} %copy-done.45, bf16[2048,1024]{0,1:T(8,128)(2,1)} %get-tuple-element.38, bf16[2048,2048]{1,0:T(8,128)(2,1)} %constant_dynamic-update-slice_fusion.33), kind=kOutput, calls=%fused_computation.10 | convolution fusion | flops 8613003264 | bytes 20971520 | tf_op jit(solution)/shard_map/dot_general | solution.py:35
  726.8 9.0 collective-permute-done.32
  745.8 14.1 %collective-permute-start.59 = (bf16[256,2048]{1,0:T(8,128)(2,1)S(1)}, bf16[256,2048]{1,0:T(8,128)(2,1)}, u32[]{:S(2)}, u32[]{:S(2)}) collective-permute-start(bf16[256,2048]{1,0:T(8,128)(2,1)S(1)} %slice.759), channel_id=1, source_target_pairs={{0,1},{1,0},{2,3},{3,2},{4,5},{5,4},{6,7},{7,6},{8,9},{9,8},{10,11... | collective-permute-start | bytes 3145736 | tf_op jit(solution)/shard_map/ppermute | solution.py:39
  759.9 9.6 %collective-permute-done.35 = bf16[256,2048]{1,0:T(8,128)(2,1)S(1)} collective-permute-done((bf16[256,2048]{1,0:T(8,128)(2,1)S(1)}, bf16[256,2048]{1,0:T(8,128)(2,1)S(1)}, u32[]{:S(2)}, u32[]{:S(2)}) %collective-permute-start.35) | collective-permute-done | bytes 1048608 | tf_op jit(solution)/shard_map/ppermute | solution.py:39
  786.0 22.8 %collective-permute-done.33 = bf16[256,2048]{1,0:T(8,128)(2,1)} collective-permute-done((bf16[256,2048]{1,0:T(8,128)(2,1)S(1)}, bf16[256,2048]{1,0:T(8,128)(2,1)}, u32[]{:S(2)}, u32[]{:S(2)}) %collective-permute-start.33) | collective-permute-done | bytes 1048608 | tf_op jit(solution)/shard_map/ppermute | solution.py:39
  814.3 8.2 all-to-all-done.7
  847.0 7.6 all-to-all-start.6
  861.4 10.5 %collective-permute-done.63 = bf16[256,2048]{1,0:T(8,128)(2,1)} collective-permute-done((bf16[256,2048]{1,0:T(8,128)(2,1)}, bf16[256,2048]{1,0:T(8,128)(2,1)}, u32[]{:S(2)}, u32[]{:S(2)}) %collective-permute-start.63) | collective-permute-done | bytes 1048608 | tf_op jit(solution)/shard_map/ppermute | solution.py:39
  879.6 13.8 %collective-permute-done.61 = bf16[256,2048]{1,0:T(8,128)(2,1)S(1)} collective-permute-done((bf16[256,2048]{1,0:T(8,128)(2,1)S(1)}, bf16[256,2048]{1,0:T(8,128)(2,1)S(1)}, u32[]{:S(2)}, u32[]{:S(2)}) %collective-permute-start.61) | collective-permute-done | bytes 1048608 | tf_op jit(solution)/shard_map/ppermute | solution.py:39
  (458 shorter events, 353.7 us)
Async XLA Ops:
  11.6 57.3 %collective-permute-start = (bf16[256,2048]{1,0:T(8,128)(2,1)}, bf16[256,2048]{1,0:T(8,128)(2,1)S(1)}, u32[]{:S(2)}, u32[]{:S(2)}) collective-permute-start(bf16[256,2048]{1,0:T(8,128)(2,1)} %get-tuple-element.36), channel_id=1, source_target_pairs={{0,1},{1,0},{2,3},{3,2},{4,5},{5,4},{6,7},{7,6},{8,9},{9,8},{10,11... | collective-permute-start | bytes 3145736 | tf_op jit(solution)/shard_map/ppermute | solution.py:39
  12.2 58.0 %collective-permute-start.1 = (bf16[256,2048]{1,0:T(8,128)(2,1)}, bf16[256,2048]{1,0:T(8,128)(2,1)}, u32[]{:S(2)}, u32[]{:S(2)}) collective-permute-start(bf16[256,2048]{1,0:T(8,128)(2,1)} %get-tuple-element.36), channel_id=1, source_target_pairs={{0,2},{1,5},{2,0},{3,7},{4,6},{5,1},{6,4},{7,3},{8,10},{9,13},{10,... | collective-permute-start | bytes 3145736 | tf_op jit(solution)/shard_map/ppermute | solution.py:39
  13.5 45.4 %collective-permute-start.7 = (s32[256,1]{0,1:T(1,128)S(1)}, s32[256,1]{0,1:T(1,128)S(1)}, u32[]{:S(2)}, u32[]{:S(2)}) collective-permute-start(s32[256,1]{0,1:T(1,128)S(1)} %bitcast.177), channel_id=1, source_target_pairs={{0,1},{1,0},{2,3},{3,2},{4,5},{5,4},{6,7},{7,6},{8,9},{9,8},{10,11... | collective-permute-start | bytes 3080 | tf_op jit(solution)/shard_map/ppermute | solution.py:39
  40.1 87.6 %all-gather.5.cloned.1.call-start = ((), (), s32[]{:S(2)}) async-start(), calls=%async_computation.12 | async-start | bytes 3932160 | tf_op jit(solution)/shard_map/all_gather | solution.py:126
  64.6 45.9 %all-to-all-start.3 = ((bf16[64,8,1024]{2,0,1:T(8,128)(2,1)}), bf16[64,8,1024]{2,0,1:T(8,128)(2,1)}, u32[]{:S(2)}, u32[]{:S(2)}) async-start(bf16[64,8,1024]{2,0,1:T(8,128)(2,1)} %bitcast.138), calls=%async_computation.3 | async-start | bytes 2097152 | tf_op jit(solution)/shard_map/all_to_all | solution.py:123
  68.8 92.8 %all-gather.7.cloned.1.call-start = ((), (), s32[]{:S(2)}) async-start(), calls=%async_computation.13 | async-start | bytes 1310720 | tf_op jit(solution)/shard_map/all_gather | solution.py:126
  110.5 62.5 %all-to-all-start.2 = ((bf16[64,8,2048]{2,0,1:T(8,128)(2,1)}), bf16[64,8,2048]{2,0,1:T(8,128)(2,1)}, u32[]{:S(2)}, u32[]{:S(2)}) async-start(bf16[64,8,2048]{2,0,1:T(8,128)(2,1)} %bitcast.157), calls=%async_computation.2 | async-start | bytes 4194304 | tf_op jit(solution)/shard_map/all_to_all | solution.py:123
  114.8 122.3 %all-gather.11.cloned.1.call-start = ((), (), s32[]{:S(2)}) async-start(), calls=%async_computation.15 | async-start | bytes 3145728 | tf_op jit(solution)/shard_map/all_gather | solution.py:126
  115.5 200.5 %all-gather.9.cloned.1.call-start = ((), (), s32[]{:S(2)}) async-start(), calls=%async_computation.14 | async-start | bytes 6291456 | tf_op jit(solution)/shard_map/all_gather | solution.py:126
  173.0 597.9 %reduce-scatter.11.cloned.1.call-start = ((), (), s32[]{:S(2)}) async-start(), calls=%async_computation.19 | async-start | bytes 3145728 | tf_op jit(solution)/shard_map/reduce_scatter | solution.py:138
  189.9 46.7 %collective-permute-start.39 = (bf16[256,2048]{1,0:T(8,128)(2,1)}, bf16[256,2048]{1,0:T(8,128)(2,1)}, u32[]{:S(2)}, u32[]{:S(2)}) collective-permute-start(bf16[256,2048]{1,0:T(8,128)(2,1)} %collective-permute-done.37), channel_id=1, source_target_pairs={{0,4},{1,9},{4,0},{5,13},{8,12},{9,1},{12,8},{13,5},{2,6},{3,11},{... | collective-permute-start | bytes 3145736 | tf_op jit(solution)/shard_map/ppermute | solution.py:39
  219.0 97.1 %collective-permute-start.20 = (bf16[256,2048]{1,0:T(8,128)(2,1)}, bf16[256,2048]{1,0:T(8,128)(2,1)}, u32[]{:S(2)}, u32[]{:S(2)}) collective-permute-start(bf16[256,2048]{1,0:T(8,128)(2,1)} %fusion.52), channel_id=1, source_target_pairs={{0,1},{1,0},{2,3},{3,2},{4,5},{5,4},{6,7},{7,6},{8,9},{9,8},{10,11... | collective-permute-start | bytes 3145736 | tf_op jit(solution)/shard_map/ppermute | solution.py:39
  219.0 103.9 %collective-permute-start.40 = (bf16[256,2048]{1,0:T(8,128)(2,1)}, bf16[256,2048]{1,0:T(8,128)(2,1)}, u32[]{:S(2)}, u32[]{:S(2)}) collective-permute-start(bf16[256,2048]{1,0:T(8,128)(2,1)} %collective-permute-done.38), channel_id=1, source_target_pairs={{0,1},{1,0},{4,5},{5,4},{8,9},{9,8},{12,13},{13,12},{2,3},{3,2},{6... | collective-permute-start | bytes 3145736 | tf_op jit(solution)/shard_map/ppermute | solution.py:39
  236.5 89.6 %collective-permute-start.41 = (bf16[256,2048]{1,0:T(8,128)(2,1)}, bf16[256,2048]{1,0:T(8,128)(2,1)}, u32[]{:S(2)}, u32[]{:S(2)}) collective-permute-start(bf16[256,2048]{1,0:T(8,128)(2,1)} %collective-permute-done.39), channel_id=1, source_target_pairs={{0,1},{1,0},{4,5},{5,4},{8,9},{9,8},{12,13},{13,12},{2,3},{3,2},{6... | collective-permute-start | bytes 3145736 | tf_op jit(solution)/shard_map/ppermute | solution.py:39
  236.5 101.4 %collective-permute-start.43 = (bf16[256,2048]{1,0:T(8,128)(2,1)}, bf16[256,2048]{1,0:T(8,128)(2,1)}, u32[]{:S(2)}, u32[]{:S(2)}) collective-permute-start(bf16[256,2048]{1,0:T(8,128)(2,1)} %collective-permute-done.42), channel_id=1, source_target_pairs={{0,1},{1,0},{4,5},{5,4},{8,9},{9,8},{12,13},{13,12},{2,3},{3,2},{6... | collective-permute-start | bytes 3145736 | tf_op jit(solution)/shard_map/ppermute | solution.py:39
  241.7 100.5 %collective-permute-start.29 = (bf16[1024,1024]{1,0:T(8,128)(2,1)}, bf16[1024,1024]{1,0:T(8,128)(2,1)}, u32[]{:S(2)}, u32[]{:S(2)}) collective-permute-start(bf16[1024,1024]{1,0:T(8,128)(2,1)} %all-gather.11.cloned.1.call-done), channel_id=1, source_target_pairs={{0,2},{2,0},{1,3},{3,1},{4,6},{6,4},{5,7},{7,5},{8,10},{10,8},{9,1... | collective-permute-start | bytes 6291464 | tf_op jit(solution)/shard_map/ppermute | solution.py:43
  316.1 91.7 %collective-permute-start.28 = (bf16[1024,2048]{1,0:T(8,128)(2,1)}, bf16[1024,2048]{1,0:T(8,128)(2,1)S(1)}, u32[]{:S(2)}, u32[]{:S(2)}) collective-permute-start(bf16[1024,2048]{1,0:T(8,128)(2,1)} %all-gather.9.cloned.1.call-done), channel_id=1, source_target_pairs={{0,2},{2,0},{1,3},{3,1},{4,6},{6,4},{5,7},{7,5},{8,10},{10,8},{9,1... | collective-permute-start | bytes 12582920 | tf_op jit(solution)/shard_map/ppermute | solution.py:43
  359.6 48.5 %collective-permute-start.25 = (bf16[256,2048]{1,0:T(8,128)(2,1)S(1)}, bf16[256,2048]{1,0:T(8,128)(2,1)S(1)}, u32[]{:S(2)}, u32[]{:S(2)}) collective-permute-start(bf16[256,2048]{1,0:T(8,128)(2,1)S(1)} %collective-permute-done.23), channel_id=1, source_target_pairs={{0,1},{1,0},{4,5},{5,4},{8,9},{9,8},{12,13},{13,12},{2,3},{3,2},{6... | collective-permute-start | bytes 3145736 | tf_op jit(solution)/shard_map/ppermute | solution.py:39
  363.0 48.0 %collective-permute-start.27 = (bf16[256,2048]{1,0:T(8,128)(2,1)S(1)}, bf16[256,2048]{1,0:T(8,128)(2,1)S(1)}, u32[]{:S(2)}, u32[]{:S(2)}) collective-permute-start(bf16[256,2048]{1,0:T(8,128)(2,1)S(1)} %collective-permute-done.26), channel_id=1, source_target_pairs={{0,1},{1,0},{4,5},{5,4},{8,9},{9,8},{12,13},{13,12},{2,3},{3,2},{6... | collective-permute-start | bytes 3145736 | tf_op jit(solution)/shard_map/ppermute | solution.py:39
  517.6 47.3 %collective-permute-start.66 = (bf16[1024,1024]{1,0:T(8,128)(2,1)S(1)}, bf16[1024,1024]{1,0:T(8,128)(2,1)S(1)}, u32[]{:S(2)}, u32[]{:S(2)}) collective-permute-start(bf16[1024,1024]{1,0:T(8,128)(2,1)S(1)} %fusion.59), channel_id=1, source_target_pairs={{0,2},{2,0},{1,3},{3,1},{4,6},{6,4},{5,7},{7,5},{8,10},{10,8},{9,1... | collective-permute-start | bytes 6291464 | tf_op jit(solution)/shard_map/ppermute | solution.py:43
  528.2 50.3 %collective-permute-start.53 = (bf16[256,2048]{1,0:T(8,128)(2,1)}, bf16[256,2048]{1,0:T(8,128)(2,1)}, u32[]{:S(2)}, u32[]{:S(2)}) collective-permute-start(bf16[256,2048]{1,0:T(8,128)(2,1)} %collective-permute-done.51), channel_id=1, source_target_pairs={{0,2},{1,5},{2,0},{3,7},{4,6},{5,1},{6,4},{7,3},{8,10},{9,13},{10,... | collective-permute-start | bytes 3145736 | tf_op jit(solution)/shard_map/ppermute | solution.py:39
  570.7 251.7 %reduce-scatter.7.cloned.1.call-start = ((), (), s32[]{:S(2)}) async-start(), calls=%async_computation.17 | async-start | bytes 1310720 | tf_op jit(solution)/shard_map/reduce_scatter | solution.py:138
  570.8 48.7 %collective-permute-start.54 = (bf16[256,2048]{1,0:T(8,128)(2,1)}, bf16[256,2048]{1,0:T(8,128)(2,1)S(1)}, u32[]{:S(2)}, u32[]{:S(2)}) collective-permute-start(bf16[256,2048]{1,0:T(8,128)(2,1)} %collective-permute-done.52), channel_id=1, source_target_pairs={{0,1},{1,0},{2,3},{3,2},{4,5},{5,4},{6,7},{7,6},{8,9},{9,8},{10,11... | collective-permute-start | bytes 3145736 | tf_op jit(solution)/shard_map/ppermute | solution.py:39
  610.8 92.5 %collective-permute-start.65 = (bf16[1024,2048]{1,0:T(8,128)(2,1)}, bf16[1024,2048]{1,0:T(8,128)(2,1)}, u32[]{:S(2)}, u32[]{:S(2)}) collective-permute-start(bf16[1024,2048]{1,0:T(8,128)(2,1)} %fusion.8), channel_id=1, source_target_pairs={{0,2},{2,0},{1,3},{3,1},{4,6},{6,4},{5,7},{7,5},{8,10},{10,8},{9,1... | collective-permute-start | bytes 12582920 | tf_op jit(solution)/shard_map/ppermute | solution.py:43
  631.0 201.5 %reduce-scatter.5.cloned.1.call-start = ((), (), s32[]{:S(2)}) async-start(), calls=%async_computation.16 | async-start | bytes 3932160 | tf_op jit(solution)/shard_map/reduce_scatter | solution.py:138
  673.3 173.7 %reduce-scatter.9.cloned.1.call-start = ((), (), s32[]{:S(2)}) async-start(), calls=%async_computation.18 | async-start | bytes 6291456 | tf_op jit(solution)/shard_map/reduce_scatter | solution.py:138
  741.9 66.9 %collective-permute-start.33 = (bf16[256,2048]{1,0:T(8,128)(2,1)S(1)}, bf16[256,2048]{1,0:T(8,128)(2,1)}, u32[]{:S(2)}, u32[]{:S(2)}) collective-permute-start(bf16[256,2048]{1,0:T(8,128)(2,1)S(1)} %get-tuple-element.44), channel_id=1, source_target_pairs={{0,4},{1,9},{4,0},{5,13},{8,12},{9,1},{12,8},{13,5},{2,6},{3,11},{... | collective-permute-start | bytes 3145736 | tf_op jit(solution)/shard_map/ppermute | solution.py:39
  770.8 51.6 %all-to-all-start.7 = ((bf16[8,64,1024]{2,1,0:T(8,128)(2,1)}), bf16[8,64,1024]{2,1,0:T(8,128)(2,1)S(1)}, u32[]{:S(2)}, u32[]{:S(2)}) async-start(bf16[8,64,1024]{2,1,0:T(8,128)(2,1)} %bitcast.166), calls=%async_computation.11 | async-start | bytes 2097152 | tf_op jit(solution)/shard_map/all_to_all | solution.py:141
  780.3 57.2 %collective-permute-start.58 = (bf16[256,2048]{1,0:T(8,128)(2,1)}, bf16[256,2048]{1,0:T(8,128)(2,1)}, u32[]{:S(2)}, u32[]{:S(2)}) collective-permute-start(bf16[256,2048]{1,0:T(8,128)(2,1)} %get-tuple-element.50), channel_id=1, source_target_pairs={{0,1},{1,0},{2,3},{3,2},{4,5},{5,4},{6,7},{7,6},{8,9},{9,8},{10,11... | collective-permute-start | bytes 3145736 | tf_op jit(solution)/shard_map/ppermute | solution.py:39
  780.4 57.1 %collective-permute-start.62 = (bf16[256,2048]{1,0:T(8,128)(2,1)}, bf16[256,2048]{1,0:T(8,128)(2,1)}, u32[]{:S(2)}, u32[]{:S(2)}) collective-permute-start(bf16[256,2048]{1,0:T(8,128)(2,1)} %get-tuple-element.51), channel_id=1, source_target_pairs={{0,1},{1,0},{2,3},{3,2},{4,5},{5,4},{6,7},{7,6},{8,9},{9,8},{10,11... | collective-permute-start | bytes 3145736 | tf_op jit(solution)/shard_map/ppermute | solution.py:39
  784.6 52.9 %collective-permute-start.60 = (bf16[256,2048]{1,0:T(8,128)(2,1)}, bf16[256,2048]{1,0:T(8,128)(2,1)}, u32[]{:S(2)}, u32[]{:S(2)}) collective-permute-start(bf16[256,2048]{1,0:T(8,128)(2,1)} %fusion.35), channel_id=1, source_target_pairs={{0,4},{1,3},{2,6},{3,1},{4,0},{5,7},{6,2},{7,5},{8,12},{9,11},{10,... | collective-permute-start | bytes 3145736 | tf_op jit(solution)/shard_map/ppermute | solution.py:39
  847.0 57.1 %all-to-all-start.6 = ((bf16[8,64,2048]{2,1,0:T(8,128)(2,1)}), bf16[8,64,2048]{2,1,0:T(8,128)(2,1)}, u32[]{:S(2)}, u32[]{:S(2)}) async-start(bf16[8,64,2048]{2,1,0:T(8,128)(2,1)} %bitcast.163), calls=%async_computation.9 | async-start | bytes 4194304 | tf_op jit(solution)/shard_map/all_to_all | solution.py:141
  (101 other events, 1784.2 us)
Sparse Core Ops, SparseCore 0:
  43.0 73.9 all-gather.4
  119.2 38.6 all-gather.6
  159.4 53.4 all-gather.10
  214.3 101.6 all-gather.8
  570.8 52.9 reduce-scatter.10
  631.1 25.8 reduce-scatter.6
  673.4 63.8 reduce-scatter.4
  739.6 96.1 reduce-scatter.8

commit v3 on v2

v3 whole, which is shorter than its diff:
```python
import functools

import jax
import jax.numpy as jnp
from jax import lax
from jax.experimental import pallas as pl
from jax.experimental.pallas import tpu as pltpu
from jax.sharding import Mesh
from jax.sharding import PartitionSpec as P

H = 32
HD = 64
EPSILON = 1e-05
ROPE_BASE = 130000.0
MASKED_SCORE = -1e30
SCALE = HD ** (-0.5)
LANES = 128
MIB = 1 << 20
BF16 = jnp.bfloat16
F32 = jnp.float32
AXES = ("r", "zh", "zl", "y", "x", "c")
NT = (((1,), (1,)), ((), ()))
TN = (((0,), (0,)), ((), ()))


def dot_nn(a, b):
    return jnp.dot(a, b, preferred_element_type=F32)


def dot_nt(a, b):
    return lax.dot_general(a, b, NT, preferred_element_type=F32)


def dot_tn(a, b):
    return lax.dot_general(a, b, TN, preferred_element_type=F32)


def flip(x, axes, masks):
    return lax.ppermute(x, axes, [(i, i ^ masks[i & 1]) for i in range(8)])


def swap(x, axis):
    return lax.ppermute(x, axis, [(0, 1), (1, 0)])


def after(x, *others):
    return lax.optimization_barrier((x,) + others)[0]


PLACES = ((0, 1, 2, 3, 5, 4, 6, 7), (0, 1, 4, 5, 3, 2, 6, 7))


class Group:
    def __init__(self, d1, d2, half, spread):
        self.axes = (d1, d2, "c")
        self.half, self.spread = half, spread

    def column_order(self, outer):
        names = ("r", "zh", "zl", "y", "x")
        sizes = dict(zip(names, (outer, 2, 2, 2, 2)))
        sequence = ([self.half] if self.half else []) + list(self.spread) + list(self.axes[:2])
        order = [0]
        for name in sequence:
            step = 1
            for later in names[names.index(name) + 1 :]:
                step *= sizes[later]
            order = [base + step * i for base in order for i in range(sizes[name])]
        return order

    def reorder(self, x, order):
        if order == list(range(len(order))):
            return x
        width = x.shape[1] // len(order)
        return jnp.concatenate([x[:, i * width : (i + 1) * width] for i in order], axis=1)

    def flip_halves(self, x):
        if not self.half:
            return x
        width = x.shape[1] // 2
        at = lax.axis_index(self.half)
        first = lax.dynamic_slice_in_dim(x, at * width, width, axis=1)
        return jnp.concatenate([first, lax.dynamic_slice_in_dim(x, (1 - at) * width, width, axis=1)], axis=1)

    def to_slots(self, x, outer):
        return self.flip_halves(self.reorder(x, self.column_order(outer)))

    def from_slots(self, x, outer):
        order = self.column_order(outer)
        return self.reorder(self.flip_halves(x), [order.index(i) for i in range(len(order))])

    def other_core(self, x):
        return flip(x, self.axes, (1, 1))

    def near(self, x):
        return flip(x, self.axes, (2, 4))

    def far(self, x):
        return flip(x, self.axes, (4, 2))

    def gather_tokens(self, x):
        partner = self.other_core(x)
        near_one = self.near(x)
        near_two = self.near(partner)
        far_one = self.far(near_one)
        parts = [x, partner, near_one, near_two, self.other_core(near_one), self.other_core(near_two)]
        return parts + [far_one, self.other_core(far_one)]

    def scatter_begin(self, array, weights, at=0):
        six, seven = rows_product(array, weights, 6, (F32, BF16), at)
        four, five = rows_product(array, weights, 4, (BF16, BF16), at)
        six = six + self.other_core(seven).astype(F32)
        far_one = self.far(six.astype(BF16)).astype(F32)
        array = after(array, six)
        two, three = rows_product(array, weights, 2, (F32, F32), at)
        zero, one = rows_product(array, weights, 0, (F32, F32), at)
        three = (three + self.other_core(five).astype(F32)).astype(BF16)
        two = (two + self.other_core(four).astype(F32) + far_one).astype(BF16)
        return after((zero, one), two, three) + (two, three)

    def scatter_end(self, sums):
        zero, one, two, three = sums
        partner = self.other_core((one + self.near(three).astype(F32)).astype(BF16))
        return zero + self.near(two).astype(F32) + partner.astype(F32)

    def scatter_tokens(self, array, weights, at=0):
        return self.scatter_end(self.scatter_begin(array, weights, at))

    def share_columns(self, weight):
        return lax.all_to_all(weight, self.axes, split_axis=1, concat_axis=0, tiled=True)

    def gather_weight(self, rows):
        rows = lax.all_gather(rows, self.spread, axis=0, tiled=True)
        return [rows, swap(rows, self.half)] if self.half else [rows]

    def weight_terms(self, parts, right):
        if self.half:
            away = swap(parts_product(parts, right, 1, 2, None), self.half)
            return parts_product(parts, right, 0, 2, away)
        return parts_product(parts, right, 0, 1, None)

    def scatter_weight(self, terms):
        return lax.psum_scatter(terms, self.spread, scatter_dimension=0, tiled=True)

    def return_columns(self, grad):
        return lax.all_to_all(grad, self.axes, split_axis=0, concat_axis=1, tiled=True)


def scalars(values):
    return jnp.stack(values).astype(jnp.int32)


VMEM_SPEC = pl.BlockSpec(memory_space=pltpu.VMEM)


SMALL = pl.CostEstimate(flops=1024, bytes_accessed=1024, transcendentals=0)


def vmem(limit):
    return pltpu.CompilerParams(vmem_limit_bytes=limit * MIB)


def parts_of(widths, tails, unit):
    out = []
    at = 0
    for device in range(8):
        for p in range(widths[0] // unit):
            for i, width in enumerate(widths):
                out.append((i, device * width + p * unit, unit, at))
                at += unit
        for i, width in enumerate(tails):
            out.append((len(widths) + i, device * width, width, at))
            at += width
    return out


def mix_columns(weights, gain, unit, tails=()):
    arrays = list(weights) + list(tails)
    rows = arrays[0].shape[0]
    parts = parts_of([w.shape[1] // 8 for w in weights], [w.shape[1] // 8 for w in tails], unit)

    def body(gain_ref, *refs):
        factor = gain_ref[...]
        for i, source, width, at in parts:
            value = refs[i][:, source : source + width]
            if i < len(weights):
                value = (value.astype(F32) * factor).astype(BF16)
            refs[-1][:, at : at + width] = value

    return pl.pallas_call(
        body,
        out_shape=jax.ShapeDtypeStruct((rows, sum(w.shape[1] for w in arrays)), BF16),
        in_specs=[VMEM_SPEC] * (1 + len(arrays)),
        out_specs=VMEM_SPEC,
        cost_estimate=SMALL,
        name="mix_columns",
    )(gain, *arrays)


def part_columns(mixed, weights, gain, unit, tail=None):
    count = len(weights)
    rows = weights[0].shape[0]
    tails = [] if tail is None else [tail]
    parts = parts_of([w.shape[1] // 8 for w in weights], [w // 8 for w in tails], unit)

    def body(mixed_ref, gain_ref, *refs):
        ins, outs = refs[:count], refs[count:-1]
        factor = gain_ref[...]
        acc = jnp.zeros((rows, LANES), F32)
        for i, source, width, at in parts:
            value = mixed_ref[:, at : at + width].astype(F32)
            if i < count:
                term = ins[i][:, source : source + width].astype(F32) * value
                for p in range(width // LANES):
                    acc = acc + term[:, p * LANES : (p + 1) * LANES]
                value = value * factor
            outs[i][:, source : source + width] = value
        refs[-1][...] = jnp.sum(acc, axis=1, keepdims=True)

    shapes = [w.shape for w in weights] + [(rows, w) for w in tails] + [(rows, 1)]
    return pl.pallas_call(
        body,
        out_shape=[jax.ShapeDtypeStruct(shape, F32) for shape in shapes],
        in_specs=[VMEM_SPEC] * (2 + count),
        out_specs=[VMEM_SPEC] * len(shapes),
        cost_estimate=SMALL,
        name="part_columns",
    )(mixed, gain, *weights)


def rows_product(array, weights, first, types, at):
    size = array.shape[0] // 8
    depth = array.shape[1]
    count = len(weights)
    each = weights[0].shape[0]
    step = min(512, each)
    inner = each // step

    def body(array_ref, *refs):
        at = pl.program_id(0) // inner
        for i in range(count):

            @pl.when(at == i)
            def _():
                both = dot_nt(array_ref[...], refs[i][...])
                refs[count][...] = both[:size].astype(types[0])
                refs[count + 1][...] = both[size:].astype(types[1])

    def weight_spec(i):
        return pl.BlockSpec((step, depth), lambda j: (jnp.clip(j - i * inner, 0, inner - 1), at))

    return pl.pallas_call(
        body,
        grid=(count * inner,),
        out_shape=[jax.ShapeDtypeStruct((size, count * each), t) for t in types],
        in_specs=[pl.BlockSpec((2 * size, depth), lambda j: (first // 2, 0))] + [weight_spec(i) for i in range(count)],
        out_specs=[pl.BlockSpec((size, step), lambda j: (0, j))] * 2,
        compiler_params=vmem(40),
        cost_estimate=SMALL,
        name="rows_product",
    )(array, *weights)


def parts_product(parts, right, which, pieces, added):
    size = parts[0].shape[0]
    tokens, width = right.shape
    model = parts[0].shape[1] // pieces
    step = 512 if width <= 1024 else 256
    offset = which * (model // step)

    def body(*refs):
        ins, right_ref = refs[:8], refs[8]
        out_ref, stacked = refs[-2], refs[-1]
        for p in range(8):
            stacked[p * size : (p + 1) * size, :] = ins[p][...]
        total = dot_tn(stacked[...], right_ref[...])
        if added is not None:
            total = total + refs[9][...].astype(F32)
        out_ref[...] = total.astype(BF16)

    block = pl.BlockSpec((step, width), lambda j: (j, 0))
    return pl.pallas_call(
        body,
        grid=(model // step,),
        out_shape=jax.ShapeDtypeStruct((model, width), BF16),
        in_specs=[pl.BlockSpec((size, step), lambda j: (0, offset + j))] * 8
        + [pl.BlockSpec((tokens, width), lambda j: (0, 0))]
        + ([block] if added is not None else []),
        out_specs=block,
        scratch_shapes=[pltpu.VMEM((tokens, step), BF16)],
        compiler_params=vmem(48),
        cost_estimate=SMALL,
        name="parts_product",
    )(*parts, right, *([added] if added is not None else []))


def attention_terms(first, right, second, other):
    size, model = first[0].shape
    tokens, width = right.shape
    rest = other.shape[1]
    step = 512

    def body(*refs):
        right_ref, other_ref, out_ref, stacked = refs[16:]
        stack_parts(refs[:8], stacked)
        out_ref[:, :width] = dot_tn(stacked[...], right_ref[...]).astype(BF16)
        stack_parts(refs[8:16], stacked)
        out_ref[:, width:] = dot_tn(stacked[...], other_ref[...]).astype(BF16)

    return pl.pallas_call(
        body,
        grid=(model // step,),
        out_shape=jax.ShapeDtypeStruct((model, width + rest), BF16),
        in_specs=[pl.BlockSpec((size, step), lambda j: (0, j))] * 16 + [whole(right), whole(other)],
        out_specs=pl.BlockSpec((step, width + rest), lambda j: (j, 0)),
        scratch_shapes=[pltpu.VMEM((tokens, step), BF16)],
        compiler_params=vmem(48),
        cost_estimate=SMALL,
        name="attention_terms",
    )(*first, *second, right, other)


UNIT = 256
CHUNK = 512


def whole(part):
    return pl.BlockSpec(part.shape, lambda *at: (0, 0))


def stack_parts(ins, stacked):
    size = ins[0].shape[0]
    for p in range(8):
        stacked[p * size : (p + 1) * size, :] = ins[p][...]


def split_product(stacked, rows, weights):
    depth = weights[0].shape[0]
    total = dot_nn(stacked[rows, :depth], weights[0][...])
    for i in range(1, len(weights)):
        total += dot_nn(stacked[rows, i * depth : (i + 1) * depth], weights[i][...])
    return total


def feed_forward(parts, weights):
    size, model = parts[0].shape
    tokens = 8 * size
    width = weights[0].shape[1]
    count = len(weights)

    def body(*refs):
        ins, ws = refs[:8], refs[8 : 8 + count]
        hidden_ref, slope_ref, stacked = refs[8 + count :]

        @pl.when(pl.program_id(0) == 0)
        def _():
            stack_parts(ins, stacked)

        @pl.loop(0, tokens // CHUNK)
        def _(i):
            rows = pl.ds(pl.multiple_of(i * CHUNK, CHUNK), CHUNK)
            both = split_product(stacked, rows, ws)
            gate, up = both[:, :UNIT], both[:, UNIT:]
            sigmoid = 1.0 / (1.0 + jnp.exp(-gate))
            silu = gate * sigmoid
            hidden_ref[rows, :] = (silu * up).astype(BF16)
            slope_ref[rows, :UNIT] = up * sigmoid * (1.0 + gate * (1.0 - sigmoid))
            slope_ref[rows, UNIT:] = silu

    return pl.pallas_call(
        body,
        grid=(width // (2 * UNIT),),
        out_shape=[jax.ShapeDtypeStruct((tokens, width // 2), BF16), jax.ShapeDtypeStruct((tokens, width), F32)],
        in_specs=[whole(p) for p in parts] + [pl.BlockSpec((w.shape[0], 2 * UNIT), lambda j: (0, j)) for w in weights],
        out_specs=[pl.BlockSpec((tokens, UNIT), lambda j: (0, j)), pl.BlockSpec((tokens, 2 * UNIT), lambda j: (0, j))],
        scratch_shapes=[pltpu.VMEM((tokens, model), BF16)],
        compiler_params=vmem(56),
        cost_estimate=SMALL,
        name="feed_forward",
    )(*parts, *weights)


def feed_back(parts, weights, slope):
    size, model = parts[0].shape
    tokens = 8 * size
    width = slope.shape[1]
    count = len(weights)

    def body(*refs):
        ins, ws = refs[:8], refs[8 : 8 + count]
        slope_ref, out_ref, stacked = refs[8 + count :]

        @pl.when(pl.program_id(0) == 0)
        def _():
            stack_parts(ins, stacked)

        @pl.loop(0, tokens // CHUNK)
        def _(i):
            rows = pl.ds(pl.multiple_of(i * CHUNK, CHUNK), CHUNK)
            grad = split_product(stacked, rows, ws)
            out_ref[rows, :UNIT] = (grad * slope_ref[rows, :UNIT]).astype(BF16)
            out_ref[rows, UNIT:] = (grad * slope_ref[rows, UNIT:]).astype(BF16)

    return pl.pallas_call(
        body,
        grid=(width // (2 * UNIT),),
        out_shape=jax.ShapeDtypeStruct((tokens, width), BF16),
        in_specs=[whole(p) for p in parts]
        + [pl.BlockSpec((w.shape[0], UNIT), lambda j: (0, j)) for w in weights]
        + [pl.BlockSpec((tokens, 2 * UNIT), lambda j: (0, j))],
        out_specs=pl.BlockSpec((tokens, 2 * UNIT), lambda j: (0, j)),
        scratch_shapes=[pltpu.VMEM((tokens, model), BF16)],
        compiler_params=vmem(56),
        cost_estimate=SMALL,
        name="feed_back",
    )(*parts, *weights, slope)


def rope(x, cosine, sine):
    lane = lax.broadcasted_iota(jnp.int32, x.shape, 1)
    other = jnp.where(lane % HD < HD // 2, pltpu.roll(x, LANES - HD // 2, 1), pltpu.roll(x, HD // 2, 1))
    return x * cosine + other * sine


def head_masks(shape):
    lane = lax.broadcasted_iota(jnp.int32, shape, 1)
    return [lane < HD, lane >= HD]


def attend_body(place_ref, *refs, blocks, size):
    ins = refs[:8]
    weight_ref, cos_ref, sin_ref, start_ref, saved_ref, mixed_ref, lse_ref, stacked, proj_ref = refs[8:]

    @pl.when((pl.program_id(0) == 0) & (pl.program_id(1) == 0))
    def _():
        stack_parts(ins, stacked)

    @pl.when(pl.program_id(1) == 0)
    def _():
        @pl.loop(0, stacked.shape[0] // CHUNK)
        def _(i):
            rows = pl.ds(pl.multiple_of(i * CHUNK, CHUNK), CHUNK)
            proj_ref[rows, :] = dot_nn(stacked[rows, :], weight_ref[...])

    base = pl.program_id(1) * blocks

    def token_rows(j):
        return pl.ds(pl.multiple_of(place_ref[base + j] * size, size), size)

    def table_rows(j):
        return pl.ds(pl.multiple_of(place_ref[8 + base + j] * size, size), size)

    for j in range(blocks):
        rows = token_rows(j)
        here = slice(j * size, (j + 1) * size)
        cosine, sine = cos_ref[table_rows(j), :], sin_ref[table_rows(j), :]
        for p in range(2):
            value = proj_ref[rows, p * LANES : (p + 1) * LANES]
            saved_ref[here, p * LANES : (p + 1) * LANES] = rope(value, cosine, sine).astype(BF16)
        saved_ref[here, 2 * LANES :] = proj_ref[rows, 2 * LANES :].astype(BF16)
    for j in range(blocks):
        here = slice(j * size, (j + 1) * size)
        upto = (j + 1) * size
        query = saved_ref[here, :LANES]
        keys = saved_ref[:upto, LANES : 2 * LANES]
        values = saved_ref[:upto, 2 * LANES :]
        row = lax.broadcasted_iota(jnp.int32, (size, upto), 0) + j * size
        col = lax.broadcasted_iota(jnp.int32, (size, upto), 1)
        visible = (col <= row) & (col >= start_ref[table_rows(j), :])
        q_heads = head_masks(query.shape)
        v_heads = head_masks(values.shape)
        mixed, totals = [], []
        for h in range(2):
            scores = dot_nt(jnp.where(q_heads[h], query, jnp.zeros_like(query)), keys) * SCALE
            scores = jnp.where(visible, scores, MASKED_SCORE)
            top = jnp.max(scores, axis=1, keepdims=True)
            weights = jnp.exp(scores - top)
            total = jnp.sum(weights, axis=1, keepdims=True)
            probs = (weights * (1.0 / total)).astype(BF16)
            mixed.append(dot_nn(probs, jnp.where(v_heads[h], values, jnp.zeros_like(values))))
            totals.append(jnp.broadcast_to(top + jnp.log(total), query.shape))
        mixed_ref[token_rows(j), :] = (mixed[0] + mixed[1]).astype(BF16)
        lse_ref[here, :] = jnp.where(q_heads[0], totals[0], totals[1])


def attend_back_body(place_ref, *refs, blocks, size):
    ins = refs[:8]
    weight_ref, saved_ref, lse_ref, cos_ref, sin_ref, start_ref, out_ref, dk_ref, dv_ref, stacked, grad_ref = refs[8:]

    @pl.when((pl.program_id(0) == 0) & (pl.program_id(1) == 0))
    def _():
        stack_parts(ins, stacked)

    @pl.when(pl.program_id(1) == 0)
    def _():
        @pl.loop(0, stacked.shape[0] // CHUNK)
        def _(i):
            rows = pl.ds(pl.multiple_of(i * CHUNK, CHUNK), CHUNK)
            grad_ref[rows, :] = dot_nn(stacked[rows, :], weight_ref[...]).astype(BF16)

    base = pl.program_id(1) * blocks

    def token_rows(j):
        return pl.ds(pl.multiple_of(place_ref[base + j] * size, size), size)

    def table_rows(j):
        return pl.ds(pl.multiple_of(place_ref[8 + base + j] * size, size), size)

    dk_ref[...] = jnp.zeros_like(dk_ref)
    dv_ref[...] = jnp.zeros_like(dv_ref)
    for j in range(blocks):
        here = slice(j * size, (j + 1) * size)
        upto = (j + 1) * size
        rows = token_rows(j)
        query = saved_ref[here, :LANES]
        keys = saved_ref[:upto, LANES : 2 * LANES]
        values = saved_ref[:upto, 2 * LANES :]
        grad = grad_ref[rows, :]
        row = lax.broadcasted_iota(jnp.int32, (size, upto), 0) + j * size
        col = lax.broadcasted_iota(jnp.int32, (size, upto), 1)
        visible = (col <= row) & (col >= start_ref[table_rows(j), :])
        q_heads = head_masks(query.shape)
        k_heads = head_masks(keys.shape)
        dq = jnp.zeros(query.shape, F32)
        dk = jnp.zeros(keys.shape, F32)
        dv = jnp.zeros(keys.shape, F32)
        for h in range(2):
            q_head = jnp.where(q_heads[h], query, jnp.zeros_like(query))
            g_head = jnp.where(q_heads[h], grad, jnp.zeros_like(grad))
            scores = dot_nt(q_head, keys) * SCALE
            log_total = lse_ref[here, h * HD : h * HD + 1]
            probs = jnp.exp(jnp.where(visible, scores, MASKED_SCORE) - log_total)
            d_probs = dot_nt(g_head, values)
            inner = jnp.sum(probs * d_probs, axis=1, keepdims=True)
            d_scores = (probs * (d_probs - inner)).astype(BF16)
            dq += dot_nn(d_scores, jnp.where(k_heads[h], keys, jnp.zeros_like(keys)))
            dk += dot_tn(d_scores, q_head)
            dv += dot_tn(probs.astype(BF16), g_head)
        out_ref[rows, :LANES] = rope(dq * SCALE, cos_ref[table_rows(j), :], -sin_ref[table_rows(j), :]).astype(BF16)
        dk_ref[:upto, :] += dk
        dv_ref[:upto, :] += dv
    for j in range(blocks):
        here = slice(j * size, (j + 1) * size)
        rows = token_rows(j)
        out_ref[rows, LANES : 2 * LANES] = rope(dk_ref[here, :] * SCALE, cos_ref[table_rows(j), :], -sin_ref[table_rows(j), :]).astype(BF16)
        out_ref[rows, 2 * LANES :] = dv_ref[here, :].astype(BF16)


def by_pair(tokens, width):
    return pl.BlockSpec((tokens, width), lambda p, s, places: (0, p))


def by_sequence(length, width):
    return pl.BlockSpec((length, width), lambda p, s, places: (s, p))


def attend(parts, weight, cosine, sine, start, places, length):
    size, model = parts[0].shape
    tokens = 8 * size
    width = weight.shape[1] * 3 // 4
    pairs = width // (3 * LANES)
    return pl.pallas_call(
        functools.partial(attend_body, blocks=length // size, size=size),
        grid_spec=pltpu.PrefetchScalarGridSpec(
            num_scalar_prefetch=1,
            grid=(pairs, tokens // length),
            in_specs=[whole(p) for p in parts] + [by_pair(model, 3 * LANES)] + [whole(t) for t in (cosine, sine, start)],
            out_specs=[by_sequence(length, 3 * LANES), by_pair(tokens, LANES), by_sequence(length, LANES)],
            scratch_shapes=[pltpu.VMEM((tokens, model), BF16), pltpu.VMEM((tokens, 3 * LANES), F32)],
        ),
        out_shape=[
            jax.ShapeDtypeStruct((tokens, width), BF16),
            jax.ShapeDtypeStruct((tokens, pairs * LANES), BF16),
            jax.ShapeDtypeStruct((tokens, pairs * LANES), F32),
        ],
        compiler_params=vmem(56),
        cost_estimate=SMALL,
        name="attend",
    )(places, *parts, weight, cosine, sine, start)


def attend_back(parts, weight, saved, lse, cosine, sine, start, places, length):
    size, model = parts[0].shape
    tokens = 8 * size
    pairs = weight.shape[1] // (4 * LANES)
    return pl.pallas_call(
        functools.partial(attend_back_body, blocks=length // size, size=size),
        grid_spec=pltpu.PrefetchScalarGridSpec(
            num_scalar_prefetch=1,
            grid=(pairs, tokens // length),
            in_specs=[whole(p) for p in parts]
            + [pl.BlockSpec((model, LANES), lambda p, s, places: (0, 3 * pairs + p)), by_sequence(length, 3 * LANES), by_sequence(length, LANES)]
            + [whole(t) for t in (cosine, sine, start)],
            out_specs=by_pair(tokens, 3 * LANES),
            scratch_shapes=[
                pltpu.VMEM((length, LANES), F32),
                pltpu.VMEM((length, LANES), F32),
                pltpu.VMEM((tokens, model), BF16),
                pltpu.VMEM((tokens, LANES), BF16),
            ],
        ),
        out_shape=jax.ShapeDtypeStruct(saved.shape, BF16),
        compiler_params=vmem(56),
        cost_estimate=SMALL,
        name="attend_back",
    )(places, *parts, weight, saved, lse, cosine, sine, start)


def rms_rows(values):
    factor = lax.rsqrt(jnp.mean(values * values, axis=-1, keepdims=True) + EPSILON)
    return values * factor, factor


def norm_input(inner, normed, factor):
    return factor * (inner - normed * jnp.mean(inner * normed, axis=-1, keepdims=True))


def rope_tables(positions):
    inverse_freq = 1.0 / ROPE_BASE ** (jnp.arange(0, HD, 2, dtype=F32) / HD)
    angles = positions.astype(F32)[:, None] * inverse_freq
    cosine, sine = jnp.cos(angles), jnp.sin(angles)
    return (
        jnp.concatenate([cosine] * 4, axis=1),
        jnp.concatenate([-sine, sine, -sine, sine], axis=1),
    )


ATTN = Group("y", "x", None, ("r", "zh", "zl"))
MLP = Group("y", "x", None, ("r", "zh", "zl"))


def local(tokens, positions, attn_gain, w_query, w_key, w_value, w_out, mlp_gain, w_gate, w_up, w_down, out_grad):
    own = tokens.shape[1]
    model = tokens.shape[2]
    length = own * lax.axis_size("x") * lax.axis_size("c")
    outer = lax.axis_size("r")
    shape = tokens.shape
    gain_one = attn_gain.astype(F32)[:, None]
    gain_two = mlp_gain.astype(F32)[:, None]

    attn_mixed = mix_columns([w_query, w_key, w_value], gain_one, LANES, [jnp.transpose(w_out)])
    attn_all = ATTN.gather_weight(ATTN.share_columns(attn_mixed))
    inputs = after(tokens, attn_mixed).reshape(own, model).astype(F32)
    normed_one, factor_one = rms_rows(inputs)
    one_low = normed_one.astype(BF16)
    gate_up_rows = MLP.share_columns(mix_columns([after(w_gate, one_low), w_up], gain_two, UNIT))
    gate_up_all = MLP.gather_weight(gate_up_rows)

    one_all = ATTN.gather_tokens(ATTN.to_slots(one_low, outer))
    where = positions.reshape(own, 1)
    for axis in ("c", "x", "y"):
        where = jnp.concatenate([where, swap(where, axis)], axis=0)
    where = where.reshape(-1)
    cosine, sine = rope_tables(where)
    place = lax.axis_index("x") * 2 + lax.axis_index("c")
    core = lax.axis_index("c")
    slot_part = scalars([jnp.where(core == 0, PLACES[0].index(i), PLACES[1].index(i)) for i in range(8)])
    slots = scalars([s * 4 + (j ^ place) for s in range(2) for j in range(4)])
    places = jnp.concatenate([slot_part[slots], slots])
    row = jnp.arange(2 * length, dtype=jnp.int32)
    start = (((row // own % 4) ^ place) * own + row % own - where)[:, None]
    saved, mixed, lse = attend(after(one_all, gate_up_rows), attn_all[0], cosine, sine, start, places, length)
    down_rows = MLP.share_columns(jnp.transpose(after(w_down, mixed)))
    down_all = MLP.gather_weight(after(down_rows, gate_up_rows))

    attn_out = ATTN.scatter_tokens(mixed, attn_all, 3)
    first_sum = inputs + ATTN.from_slots(attn_out, outer)

    grad_rows = out_grad.reshape(own, model)
    normed_two, factor_two = rms_rows(first_sum)
    two_low = MLP.to_slots(normed_two.astype(BF16), outer)
    two_all = MLP.gather_tokens(two_low)
    dy_all = MLP.gather_tokens(MLP.to_slots(after(grad_rows, one_all), outer))
    hidden, slope = feed_forward(two_all, gate_up_all)
    down_terms = MLP.weight_terms(dy_all, hidden)
    down_grad = MLP.scatter_weight(down_terms)
    d_gate_up = feed_back(after(dy_all, down_terms), down_all, slope)
    inner_sums = MLP.scatter_begin(d_gate_up, gate_up_all)
    gate_up_terms = after(MLP.weight_terms(two_all, after(d_gate_up, *inner_sums)), down_grad)
    gate_up_grad = MLP.scatter_weight(gate_up_terms)
    inner_two = MLP.scatter_end(after(inner_sums[:2], gate_up_terms) + inner_sums[2:])

    d_first = grad_rows.astype(F32) + norm_input(MLP.from_slots(inner_two, outer), normed_two, factor_two)
    d_attn_all = ATTN.gather_tokens(ATTN.to_slots(d_first.astype(BF16), outer))
    zero, one, two, three = MLP.scatter_begin(after(hidden, d_first), down_all)
    d_attn_all = after(d_attn_all, zero, one, two, three)
    d_qkv = attend_back(d_attn_all, attn_all[0], saved, lse, cosine, sine, start, places, length)
    zero, one = after((zero, one), d_qkv)
    attn_terms = after(attention_terms(one_all, d_qkv, d_attn_all, mixed), gate_up_grad)
    attn_grad = ATTN.scatter_weight(attn_terms)
    inner_one = ATTN.scatter_tokens(d_qkv, attn_all)
    tokens_grad = d_first + norm_input(ATTN.from_slots(inner_one, outer), normed_one, factor_one)
    mlp_out = MLP.scatter_end((zero, one, two, three))
    block_out = (first_sum + MLP.from_slots(mlp_out, outer)).astype(BF16)

    down_w = MLP.return_columns(down_grad)
    gate_w, up_w, gain_mlp = part_columns(MLP.return_columns(gate_up_grad), [w_gate, w_up], gain_two, UNIT)
    query_w, key_w, value_w, out_w, gain_attn = part_columns(
        ATTN.return_columns(attn_grad), [w_query, w_key, w_value], gain_one, LANES, w_out.shape[0]
    )
    return (
        block_out.reshape(shape),
        tokens_grad.astype(BF16).reshape(shape),
        gain_attn.reshape(-1),
        query_w,
        key_w,
        value_w,
        jnp.transpose(out_w),
        gain_mlp.reshape(-1),
        gate_w,
        up_w,
        jnp.transpose(down_w.astype(F32)),
    )


def solution(mesh):
    fsdp = mesh.shape["fsdp"]
    sizes = (fsdp // 8, 2, 2, 2, mesh.shape["ctx"] // 2, 2)
    fine = Mesh(mesh.devices.reshape(sizes), AXES)
    rows, cols = AXES[:4], AXES[4:]
    tokens, places, vector = P(rows, cols, None), P(rows, cols), P(AXES)
    first, second = P(AXES, None), P(None, AXES)
    in_specs = (tokens, places, vector, first, first, first, second, vector, first, first, second, tokens)
    out_specs = (tokens, tokens, vector, first, first, first, second, vector, first, first, second)
    return jax.shard_map(local, mesh=fine, in_specs=in_specs, out_specs=out_specs, check_vma=False)
```

time: 931 us -> 720 us (0.77)
  the two profiles are of different devices: /device:TPU:17 before, /device:TPU:0 now
where the time goes in v3:
time: 720 us; the launch traced here: 709 us
  Pallas kernels  251 us (35%)
  waiting for transfers between devices  231 us (32%)
  starting transfers between devices  59.4 us (8%)
  other arithmetic  57.8 us (8%)
  blocking collectives  50.3 us (7%)
  local copies, waits for them, and re-layouts  44.1 us (6%)
  between operations  15.4 us (2%)
    ppermute x56, waiting for transfers between devices, flip(): return lax.ppermute(x, axes, [(i, i ^ masks[i & 1]) for i in range(8)])  177 us
    pallas_call x16, Pallas kernels, rows_product(): pl.pallas_call(body, grid=(count * inner,), out_shape=[jax.ShapeDtypeStru...  64 us
    all_to_all x2, blocking collectives, share_columns(): lax.all_to_all(weight, self.axes, split_axis=1, concat_axis=0, tiled=True)  50.3 us
    ppermute x56, starting transfers between devices, flip(): return lax.ppermute(x, axes, [(i, i ^ masks[i & 1]) for i in range(8)])  39.8 us
    pallas_call x2, Pallas kernels, parts_product(): pl.pallas_call(body, grid=(model // step,), out_shape=jax.ShapeDtypeStruc...  37.9 us
    pallas_call x1, Pallas kernels, attend(): pl.pallas_call(functools.partial(attend_body, blocks=length // size, size...  36.1 us
    pallas_call x1, Pallas kernels, attend_back(): pl.pallas_call(functools.partial(attend_back_body, blocks=length // size,...  35.7 us
    pallas_call x1, Pallas kernels, feed_forward(): pl.pallas_call(body, grid=(width // (2 * UNIT),), out_shape=[jax.ShapeDty...  29.1 us
  transfers between devices with their start and end apart: 69, of which 22 were waited for; matrix products, arithmetic and copies ran while one was open for 9% of the time, Pallas kernels for 35%

profile of v3, /device:TPU:0, one launch (start us, length us, event | category | flops | bytes accessed | tf_op | source)
XLA Modules:
  0.0 708.8 jit_solution(13667446702334270057)
XLA Ops:
  12.3 20.6 %all_to_all.108 = bf16[64,8,1024]{2,0,1:T(8,128)(2,1)} all-to-all(bf16[64,8,1024]{2,0,1:T(8,128)(2,1)S(1)} %bitcast.97), channel_id=1, replica_groups=mesh['r'=1,'zh'=2,'zl'=2,'y'=2,'x'=2,'c'=2] {'y','x','c'}, dimensions={1} | all-to-all | bytes 2097152 | tf_op jit(solution)/shard_map/all_to_all | solution.py:129
  39.9 29.8 %all_to_all.109 = bf16[64,8,2048]{2,0,1:T(8,128)(2,1)} all-to-all(bf16[64,8,2048]{2,0,1:T(8,128)(2,1)S(1)} %bitcast.93), channel_id=1, replica_groups=mesh['r'=1,'zh'=2,'zl'=2,'y'=2,'x'=2,'c'=2] {'y','x','c'}, dimensions={1} | all-to-all | bytes 4194304 | tf_op jit(solution)/shard_map/all_to_all | solution.py:129
  70.3 14.2 %collective-permute-done.1.refs_2_ = bf16[256,2048]{1,0:T(8,128)(2,1)S(1)} collective-permute-done((bf16[256,2048]{1,0:T(8,128)(2,1)S(1)}, bf16[256,2048]{1,0:T(8,128)(2,1)S(1)}, u32[]{:S(2)}, u32[]{:S(2)}) %collective-permute-start.1) | collective-permute-done | bytes 1048608 | tf_op jit(solution)/shard_map/ppermute | solution.py:39
  88.3 19.8 %collective-permute-done.8 = s32[512,1]{0,1:T(1,128)S(1)} collective-permute-done((s32[512,1]{0,1:T(1,128)S(1)}, s32[512,1]{0,1:T(1,128)S(1)}, u32[]{:S(2)}, u32[]{:S(2)}) %collective-permute-start.8) | collective-permute-done | bytes 2080 | tf_op jit(solution)/shard_map/ppermute | solution.py:43
  123.7 36.1 %attend.1 = (bf16[2048,768]{1,0:T(8,128)(2,1)}, bf16[2048,256]{1,0:T(8,128)(2,1)}, f32[2048,256]{1,0:T(8,128)}) custom-call(s32[16]{0:T(128)} %concatenate.59.place_ref, bf16[256,2048]{1,0:T(8,128)(2,1)} %copy-done.13, bf16[256,2048]{1,0:T(8,128)(2,1)} %copy-done.21, bf16[256,2048]{1,0:T(8,128)(2,1)} %copy-done.19, bf16[256,2048]{1,0:T(8,128)(2,1)} %copy-done.23, ...), custom_call_target="tpu_custom_call" | custom-call | flops 1024 | bytes 1024 | tf_op jit(solution)/shard_map/attend/pallas_call | solution.py:561
  182.5 17.4 %all-to-all-done.2 = bf16[64,8,1024]{2,0,1:T(8,128)(2,1)} async-done(((bf16[64,8,1024]{2,0,1:T(8,128)(2,1)}), bf16[64,8,1024]{2,0,1:T(8,128)(2,1)}, u32[]{:S(2)}, u32[]{:S(2)}) %all-to-all-start.2) | async-done | bytes 1048608 | tf_op jit(solution)/shard_map/all_to_all | solution.py:129
  209.1 11.9 %collective-permute-done.14 = bf16[256,2048]{1,0:T(8,128)(2,1)S(1)} collective-permute-done((bf16[256,2048]{1,0:T(8,128)(2,1)S(1)}, bf16[256,2048]{1,0:T(8,128)(2,1)S(1)}, u32[]{:S(2)}, u32[]{:S(2)}) %collective-permute-start.14) | collective-permute-done | bytes 1048608 | tf_op jit(solution)/shard_map/ppermute | solution.py:39
  225.0 12.6 %collective-permute-done.18.refs_2_ = bf16[256,2048]{1,0:T(8,128)(2,1)S(1)} collective-permute-done((bf16[256,2048]{1,0:T(8,128)(2,1)S(1)}, bf16[256,2048]{1,0:T(8,128)(2,1)S(1)}, u32[]{:S(2)}, u32[]{:S(2)}) %collective-permute-start.18) | collective-permute-done | bytes 1048608 | tf_op jit(solution)/shard_map/ppermute | solution.py:39
  240.4 19.8 %collective-permute-done.25.refs_2_ = bf16[256,2048]{1,0:T(8,128)(2,1)} collective-permute-done((bf16[256,2048]{1,0:T(8,128)(2,1)S(1)}, bf16[256,2048]{1,0:T(8,128)(2,1)}, u32[]{:S(2)}, u32[]{:S(2)}) %collective-permute-start.25) | collective-permute-done | bytes 1048608 | tf_op jit(solution)/shard_map/ppermute | solution.py:39
  264.4 17.3 %collective-permute-done.19.refs_3_ = bf16[256,2048]{1,0:T(8,128)(2,1)S(1)} collective-permute-done((bf16[256,2048]{1,0:T(8,128)(2,1)S(1)}, bf16[256,2048]{1,0:T(8,128)(2,1)S(1)}, u32[]{:S(2)}, u32[]{:S(2)}) %collective-permute-start.19) | collective-permute-done | bytes 1048608 | tf_op jit(solution)/shard_map/ppermute | solution.py:39
  286.6 6.5 collective-permute-done.26.refs_3_
  295.1 29.1 %feed_forward.1 = (bf16[2048,1024]{1,0:T(8,128)(2,1)}, f32[2048,2048]{1,0:T(8,128)}) custom-call(bf16[256,2048]{1,0:T(8,128)(2,1)} %copy-done.11, bf16[256,2048]{1,0:T(8,128)(2,1)} %copy-done.29, bf16[256,2048]{1,0:T(8,128)(2,1)} %copy-done.27, bf16[256,2048]{1,0:T(8,128)(2,1)} %copy-done.31, bf16[256,2048]{1,0:T(8,128)(2,1)} %copy-done.33, ...), custom_call_target="tpu_custom_call" | custom-call | flops 1024 | bytes 1024 | tf_op jit(solution)/shard_map/feed_forward/pallas_call | solution.py:369
  324.3 13.4 %parts_product.2 = bf16[2048,1024]{1,0:T(8,128)(2,1)} custom-call(bf16[256,2048]{1,0:T(8,128)(2,1)S(1)} %bitcast.90, bf16[256,2048]{1,0:T(8,128)(2,1)S(1)} %copy-done.36, bf16[256,2048]{1,0:T(8,128)(2,1)} %collective-permute-done.25.refs_2_, bf16[256,2048]{1,0:T(8,128)(2,1)} %collective-permute-done.26.refs_3_, ...), custom_call_target="tpu_custom_call" | custom-call | flops 1024 | bytes 1024 | tf_op jit(solution)/shard_map/parts_product/pallas_call | solution.py:281
  337.7 5.9 all-gather.8.cloned.1.call-done.refs_8_.refs_0_
  343.6 19.3 %feed_back.1.array_ref.refs_8_ = bf16[2048,2048]{1,0:T(8,128)(2,1)} custom-call(bf16[256,2048]{1,0:T(8,128)(2,1)} %bitcast.87, bf16[256,2048]{1,0:T(8,128)(2,1)} %copy-done.35, bf16[256,2048]{1,0:T(8,128)(2,1)} %collective-permute-done.25.refs_2_, bf16[256,2048]{1,0:T(8,128)(2,1)} %collective-permute-done.26.refs_3_, ...), custom_call_target="tpu_custom_call" | custom-call | flops 1024 | bytes 1024 | tf_op jit(solution)/shard_map/feed_back/pallas_call | solution.py:403
  366.4 7.3 %rows_product.20 = (f32[256,2048]{1,0:T(8,128)S(1)}, bf16[256,2048]{1,0:T(8,128)(2,1)S(1)}) custom-call(bf16[2048,2048]{1,0:T(8,128)(2,1)S(1)} %copy-done.5, bf16[2048,2048]{1,0:T(8,128)(2,1)} %all-gather.6.cloned.1.call-done.refs_8_.refs_0_), custom_call_target="tpu_custom_call" | custom-call | flops 1024 | bytes 1024 | tf_op jit(solution)/shard_map/rows_product/pallas_call | solution.py:251
  373.8 7.3 %rows_product.23 = (bf16[256,2048]{1,0:T(8,128)(2,1)S(1)}, bf16[256,2048]{1,0:T(8,128)(2,1)S(1)}) custom-call(bf16[2048,2048]{1,0:T(8,128)(2,1)S(1)} %copy-done.5, bf16[2048,2048]{1,0:T(8,128)(2,1)} %all-gather.6.cloned.1.call-done.refs_8_.refs_0_), custom_call_target="tpu_custom_call" | custom-call | flops 1024 | bytes 1024 | tf_op jit(solution)/shard_map/rows_product/pallas_call | solution.py:251
  383.6 7.4 %rows_product.22 = (f32[256,2048]{1,0:T(8,128)S(1)}, f32[256,2048]{1,0:T(8,128)S(1)}) custom-call(bf16[2048,2048]{1,0:T(8,128)(2,1)S(1)} %copy-done.5, bf16[2048,2048]{1,0:T(8,128)(2,1)} %all-gather.6.cloned.1.call-done.refs_8_.refs_0_), custom_call_target="tpu_custom_call" | custom-call | flops 1024 | bytes 1024 | tf_op jit(solution)/shard_map/rows_product/pallas_call | solution.py:251
  391.0 7.4 %rows_product.21 = (f32[256,2048]{1,0:T(8,128)S(1)}, f32[256,2048]{1,0:T(8,128)S(1)}) custom-call(bf16[2048,2048]{1,0:T(8,128)(2,1)S(1)} %copy-done.5, bf16[2048,2048]{1,0:T(8,128)(2,1)} %all-gather.6.cloned.1.call-done.refs_8_.refs_0_), custom_call_target="tpu_custom_call" | custom-call | flops 1024 | bytes 1024 | tf_op jit(solution)/shard_map/rows_product/pallas_call | solution.py:251
  402.6 24.6 %parts_product.3 = bf16[2048,2048]{1,0:T(8,128)(2,1)} custom-call(bf16[256,2048]{1,0:T(8,128)(2,1)S(1)} %copy-done.12, bf16[256,2048]{1,0:T(8,128)(2,1)S(1)} %copy-done.30, bf16[256,2048]{1,0:T(8,128)(2,1)S(1)} %copy-done.28, bf16[256,2048]{1,0:T(8,128)(2,1)S(1)} %copy-done.32, bf16[256,2048]{1,0:T(8,128)(2,1)S(1)} %copy-done.34, ...), custom_call_target="tpu_custom_call" | custom-call | flops 1024 | bytes 1024 | tf_op jit(solution)/shard_map/parts_product/pallas_call | solution.py:281
  429.3 13.0 %collective-permute-done.36 = bf16[256,2048]{1,0:T(8,128)(2,1)S(1)} collective-permute-done((bf16[256,2048]{1,0:T(8,128)(2,1)}, bf16[256,2048]{1,0:T(8,128)(2,1)S(1)}, u32[]{:S(2)}, u32[]{:S(2)}) %collective-permute-start.36) | collective-permute-done | bytes 1048608 | tf_op jit(solution)/shard_map/ppermute | solution.py:39
  444.3 9.3 %collective-permute-done.35 = bf16[256,2048]{1,0:T(8,128)(2,1)S(1)} collective-permute-done((bf16[256,2048]{1,0:T(8,128)(2,1)S(1)}, bf16[256,2048]{1,0:T(8,128)(2,1)S(1)}, u32[]{:S(2)}, u32[]{:S(2)}) %collective-permute-start.35) | collective-permute-done | bytes 1048608 | tf_op jit(solution)/shard_map/ppermute | solution.py:39
  466.0 5.3 collective-permute-done.43.refs_2_.refs_10_
  482.8 12.4 %collective-permute-done.47.refs_6_.refs_14_ = bf16[256,2048]{1,0:T(8,128)(2,1)S(1)} collective-permute-done((bf16[256,2048]{1,0:T(8,128)(2,1)S(1)}, bf16[256,2048]{1,0:T(8,128)(2,1)S(1)}, u32[]{:S(2)}, u32[]{:S(2)}) %collective-permute-start.47) | collective-permute-done | bytes 1048608 | tf_op jit(solution)/shard_map/ppermute | solution.py:39
  500.8 5.8 collective-permute-done.40
  511.4 35.7 %attend_back.1.array_ref.refs_16_ = bf16[2048,768]{1,0:T(8,128)(2,1)} custom-call(s32[16]{0:T(128)} %concatenate.59.place_ref, bf16[256,2048]{1,0:T(8,128)(2,1)} %copy-done.54, bf16[256,2048]{1,0:T(8,128)(2,1)} %copy-done.61, bf16[256,2048]{1,0:T(8,128)(2,1)} %copy-done.60, bf16[256,2048]{1,0:T(8,128)(2,1)} %copy-done.63, bf16[256,2048]{1,0:T(8,128)(2,1)} %copy-done.64, ...), custom_call_target="tpu_custom_call" | custom-call | flops 1024 | bytes 1024 | tf_op jit(solution)/shard_map/attend_back/pallas_call | solution.py:585
  547.1 14.2 %attention_terms.1 = bf16[2048,1024]{1,0:T(8,128)(2,1)} custom-call(bf16[256,2048]{1,0:T(8,128)(2,1)S(1)} %copy-done.14, bf16[256,2048]{1,0:T(8,128)(2,1)S(1)} %copy-done.22, bf16[256,2048]{1,0:T(8,128)(2,1)S(1)} %copy-done.20, bf16[256,2048]{1,0:T(8,128)(2,1)S(1)} %copy-done.24, bf16[256,2048]{1,0:T(8,128)(2,1)S(1)} %copy-done.26, ...), custom_call_target="tpu_custom_call" | custom-call | flops 1024 | bytes 1024 | tf_op jit(solution)/shard_map/attention_terms/pallas_call | solution.py:309
  561.3 7.9 %reduce-scatter.6.cloned.1.call-done = bf16[512,2048]{1,0:T(8,128)(2,1)} async-done(((bf16[2048,2048]{1,0:T(8,128)(2,1)}), bf16[512,2048]{1,0:T(8,128)(2,1)}) %reduce-scatter.6.cloned.1.call-update) | async-done | bytes 2097168 | tf_op jit(solution)/shard_map/reduce_scatter | solution.py:142
  601.3 21.2 %collective-permute-done.50 = bf16[256,2048]{1,0:T(8,128)(2,1)S(1)} collective-permute-done((bf16[256,2048]{1,0:T(8,128)(2,1)}, bf16[256,2048]{1,0:T(8,128)(2,1)S(1)}, u32[]{:S(2)}, u32[]{:S(2)}) %collective-permute-start.50) | collective-permute-done | bytes 1048608 | tf_op jit(solution)/shard_map/ppermute | solution.py:39
  637.1 15.8 %collective-permute-done.57 = bf16[256,2048]{1,0:T(8,128)(2,1)} collective-permute-done((bf16[256,2048]{1,0:T(8,128)(2,1)}, bf16[256,2048]{1,0:T(8,128)(2,1)}, u32[]{:S(2)}, u32[]{:S(2)}) %collective-permute-start.57) | collective-permute-done | bytes 1048608 | tf_op jit(solution)/shard_map/ppermute | solution.py:39
  656.1 6.8 collective-permute-start.56
  688.4 5.0 part_columns.3
  (338 shorter events, 213.3 us)
Async XLA Ops:
  7.2 116.5 %all-gather.4.cloned.1.call-start = ((), (), s32[]{:S(2)}) async-start(), calls=%async_computation.9 | async-start | bytes 5242880 | tf_op jit(solution)/shard_map/all_gather | solution.py:132
  32.9 262.2 %all-gather.6.cloned.1.call-start = ((), (), s32[]{:S(2)}) async-start(), calls=%async_computation.10 | async-start | bytes 10485760 | tf_op jit(solution)/shard_map/all_gather | solution.py:132
  84.5 28.5 %collective-permute-start.5 = (bf16[256,2048]{1,0:T(8,128)(2,1)S(1)}, bf16[256,2048]{1,0:T(8,128)(2,1)}, u32[]{:S(2)}, u32[]{:S(2)}) collective-permute-start(bf16[256,2048]{1,0:T(8,128)(2,1)S(1)} %collective-permute-done.1.refs_2_), channel_id=1, source_target_pairs={{0,4},{1,3},{2,6},{3,1},{4,0},{5,7},{6,2},{7,5},{8,12},{9,11},{10,... | collective-permute-start | bytes 3145736 | tf_op jit(solution)/shard_map/ppermute | solution.py:39
  85.1 28.5 %collective-permute-start.2 = (bf16[256,2048]{1,0:T(8,128)(2,1)S(1)}, bf16[256,2048]{1,0:T(8,128)(2,1)S(1)}, u32[]{:S(2)}, u32[]{:S(2)}) collective-permute-start(bf16[256,2048]{1,0:T(8,128)(2,1)S(1)} %collective-permute-done.refs_1_), channel_id=1, source_target_pairs={{0,2},{1,5},{2,0},{3,7},{4,6},{5,1},{6,4},{7,3},{8,10},{9,13},{10,... | collective-permute-start | bytes 3145736 | tf_op jit(solution)/shard_map/ppermute | solution.py:39
  166.1 37.9 %collective-permute-start.11 = (bf16[256,2048]{1,0:T(8,128)(2,1)}, bf16[256,2048]{1,0:T(8,128)(2,1)}, u32[]{:S(2)}, u32[]{:S(2)}) collective-permute-start(bf16[256,2048]{1,0:T(8,128)(2,1)} %get-tuple-element.122), channel_id=1, source_target_pairs={{0,1},{1,0},{2,3},{3,2},{4,5},{5,4},{6,7},{7,6},{8,9},{9,8},{10,11... | collective-permute-start | bytes 3145736 | tf_op jit(solution)/shard_map/ppermute | solution.py:39
  167.9 36.2 %collective-permute-start.12 = (bf16[256,2048]{1,0:T(8,128)(2,1)}, bf16[256,2048]{1,0:T(8,128)(2,1)}, u32[]{:S(2)}, u32[]{:S(2)}) collective-permute-start(bf16[256,2048]{1,0:T(8,128)(2,1)} %convert_add_fusion.6), channel_id=1, source_target_pairs={{0,4},{1,3},{2,6},{3,1},{4,0},{5,7},{6,2},{7,5},{8,12},{9,11},{10,... | collective-permute-start | bytes 3145736 | tf_op jit(solution)/shard_map/ppermute | solution.py:39
  169.7 30.2 %all-to-all-start.2 = ((bf16[64,8,1024]{2,0,1:T(8,128)(2,1)}), bf16[64,8,1024]{2,0,1:T(8,128)(2,1)}, u32[]{:S(2)}, u32[]{:S(2)}) async-start(bf16[64,8,1024]{2,0,1:T(8,128)(2,1)} %bitcast.85), calls=%async_computation.2 | async-start | bytes 2097152 | tf_op jit(solution)/shard_map/all_to_all | solution.py:129
  174.0 169.6 %all-gather.8.cloned.1.call-start = ((), (), s32[]{:S(2)}) async-start(), calls=%async_computation.11 | async-start | bytes 5242880 | tf_op jit(solution)/shard_map/all_gather | solution.py:132
  180.6 26.8 %collective-permute-start.15 = (bf16[256,2048]{1,0:T(8,128)(2,1)}, bf16[256,2048]{1,0:T(8,128)(2,1)}, u32[]{:S(2)}, u32[]{:S(2)}) collective-permute-start(bf16[256,2048]{1,0:T(8,128)(2,1)} %add_convert_fusion.11), channel_id=1, source_target_pairs={{0,2},{1,5},{2,0},{3,7},{4,6},{5,1},{6,4},{7,3},{8,10},{9,13},{10,... | collective-permute-start | bytes 3145736 | tf_op jit(solution)/shard_map/ppermute | solution.py:39
  199.9 227.2 %reduce-scatter.4.cloned.1.call-start = ((), (), s32[]{:S(2)}) async-start(), calls=%async_computation.12 | async-start | bytes 5242880 | tf_op jit(solution)/shard_map/reduce_scatter | solution.py:142
  223.7 36.4 %collective-permute-start.25 = (bf16[256,2048]{1,0:T(8,128)(2,1)S(1)}, bf16[256,2048]{1,0:T(8,128)(2,1)}, u32[]{:S(2)}, u32[]{:S(2)}) collective-permute-start(bf16[256,2048]{1,0:T(8,128)(2,1)S(1)} %bitcast.88), channel_id=1, source_target_pairs={{0,2},{1,5},{2,0},{3,7},{4,6},{5,1},{6,4},{7,3},{8,10},{9,13},{10,... | collective-permute-start | bytes 3145736 | tf_op jit(solution)/shard_map/ppermute | solution.py:39
  225.0 35.4 %collective-permute-start.24 = (bf16[256,2048]{1,0:T(8,128)(2,1)S(1)}, bf16[256,2048]{1,0:T(8,128)(2,1)S(1)}, u32[]{:S(2)}, u32[]{:S(2)}) collective-permute-start(bf16[256,2048]{1,0:T(8,128)(2,1)S(1)} %bitcast.89), channel_id=1, source_target_pairs={{0,1},{1,0},{2,3},{3,2},{4,5},{5,4},{6,7},{7,6},{8,9},{9,8},{10,11... | collective-permute-start | bytes 3145736 | tf_op jit(solution)/shard_map/ppermute | solution.py:39
  237.9 43.9 %collective-permute-start.19 = (bf16[256,2048]{1,0:T(8,128)(2,1)S(1)}, bf16[256,2048]{1,0:T(8,128)(2,1)S(1)}, u32[]{:S(2)}, u32[]{:S(2)}) collective-permute-start(bf16[256,2048]{1,0:T(8,128)(2,1)S(1)} %collective-permute-done.17.refs_1_), channel_id=1, source_target_pairs={{0,2},{1,5},{2,0},{3,7},{4,6},{5,1},{6,4},{7,3},{8,10},{9,13},{10,... | collective-permute-start | bytes 3145736 | tf_op jit(solution)/shard_map/ppermute | solution.py:39
  260.4 32.7 %collective-permute-start.26 = (bf16[256,2048]{1,0:T(8,128)(2,1)S(1)}, bf16[256,2048]{1,0:T(8,128)(2,1)}, u32[]{:S(2)}, u32[]{:S(2)}) collective-permute-start(bf16[256,2048]{1,0:T(8,128)(2,1)S(1)} %collective-permute-done.24.refs_1_), channel_id=1, source_target_pairs={{0,2},{1,5},{2,0},{3,7},{4,6},{5,1},{6,4},{7,3},{8,10},{9,13},{10,... | collective-permute-start | bytes 3145736 | tf_op jit(solution)/shard_map/ppermute | solution.py:39
  263.9 29.2 %collective-permute-start.20 = (bf16[256,2048]{1,0:T(8,128)(2,1)S(1)}, bf16[256,2048]{1,0:T(8,128)(2,1)S(1)}, u32[]{:S(2)}, u32[]{:S(2)}) collective-permute-start(bf16[256,2048]{1,0:T(8,128)(2,1)S(1)} %collective-permute-done.18.refs_2_), channel_id=1, source_target_pairs={{0,1},{1,0},{2,3},{3,2},{4,5},{5,4},{6,7},{7,6},{8,9},{9,8},{10,11... | collective-permute-start | bytes 3145736 | tf_op jit(solution)/shard_map/ppermute | solution.py:39
  263.9 29.8 %collective-permute-start.23 = (bf16[256,2048]{1,0:T(8,128)(2,1)S(1)}, bf16[256,2048]{1,0:T(8,128)(2,1)S(1)}, u32[]{:S(2)}, u32[]{:S(2)}) collective-permute-start(bf16[256,2048]{1,0:T(8,128)(2,1)S(1)} %collective-permute-done.22.refs_6_), channel_id=1, source_target_pairs={{0,1},{1,0},{2,3},{3,2},{4,5},{5,4},{6,7},{7,6},{8,9},{9,8},{10,11... | collective-permute-start | bytes 3145736 | tf_op jit(solution)/shard_map/ppermute | solution.py:39
  286.6 37.7 %collective-permute-start.27 = (bf16[256,2048]{1,0:T(8,128)(2,1)}, bf16[256,2048]{1,0:T(8,128)(2,1)}, u32[]{:S(2)}, u32[]{:S(2)}) collective-permute-start(bf16[256,2048]{1,0:T(8,128)(2,1)} %collective-permute-done.25.refs_2_), channel_id=1, source_target_pairs={{0,1},{1,0},{2,3},{3,2},{4,5},{5,4},{6,7},{7,6},{8,9},{9,8},{10,11... | collective-permute-start | bytes 3145736 | tf_op jit(solution)/shard_map/ppermute | solution.py:39
  293.1 31.1 %collective-permute-start.30 = (bf16[256,2048]{1,0:T(8,128)(2,1)}, bf16[256,2048]{1,0:T(8,128)(2,1)}, u32[]{:S(2)}, u32[]{:S(2)}) collective-permute-start(bf16[256,2048]{1,0:T(8,128)(2,1)} %collective-permute-done.29.refs_6_), channel_id=1, source_target_pairs={{0,1},{1,0},{2,3},{3,2},{4,5},{5,4},{6,7},{7,6},{8,9},{9,8},{10,11... | collective-permute-start | bytes 3145736 | tf_op jit(solution)/shard_map/ppermute | solution.py:39
  293.1 31.1 %collective-permute-start.28 = (bf16[256,2048]{1,0:T(8,128)(2,1)}, bf16[256,2048]{1,0:T(8,128)(2,1)}, u32[]{:S(2)}, u32[]{:S(2)}) collective-permute-start(bf16[256,2048]{1,0:T(8,128)(2,1)} %collective-permute-done.26.refs_3_), channel_id=1, source_target_pairs={{0,1},{1,0},{2,3},{3,2},{4,5},{5,4},{6,7},{7,6},{8,9},{9,8},{10,11... | collective-permute-start | bytes 3145736 | tf_op jit(solution)/shard_map/ppermute | solution.py:39
  337.6 231.6 %reduce-scatter.6.cloned.1.call-start = ((), (), s32[]{:S(2)}) async-start(), calls=%async_computation.13 | async-start | bytes 10485760 | tf_op jit(solution)/shard_map/reduce_scatter | solution.py:142
  427.2 243.3 %reduce-scatter.8.cloned.1.call-start = ((), (), s32[]{:S(2)}) async-start(), calls=%async_computation.14 | async-start | bytes 5242880 | tf_op jit(solution)/shard_map/reduce_scatter | solution.py:142
  473.3 27.5 %collective-permute-start.39 = (bf16[256,2048]{1,0:T(8,128)(2,1)S(1)}, bf16[256,2048]{1,0:T(8,128)(2,1)}, u32[]{:S(2)}, u32[]{:S(2)}) collective-permute-start(bf16[256,2048]{1,0:T(8,128)(2,1)S(1)} %get-tuple-element.162), channel_id=1, source_target_pairs={{0,1},{1,0},{2,3},{3,2},{4,5},{5,4},{6,7},{7,6},{8,9},{9,8},{10,11... | collective-permute-start | bytes 3145736 | tf_op jit(solution)/shard_map/ppermute | solution.py:39
  474.6 32.0 %collective-permute-start.40 = (bf16[256,2048]{1,0:T(8,128)(2,1)}, bf16[256,2048]{1,0:T(8,128)(2,1)}, u32[]{:S(2)}, u32[]{:S(2)}) collective-permute-start(bf16[256,2048]{1,0:T(8,128)(2,1)} %convert_add_fusion.3), channel_id=1, source_target_pairs={{0,4},{1,3},{2,6},{3,1},{4,0},{5,7},{6,2},{7,5},{8,12},{9,11},{10,... | collective-permute-start | bytes 3145736 | tf_op jit(solution)/shard_map/ppermute | solution.py:39
  482.7 26.9 %collective-permute-start.45 = (bf16[256,2048]{1,0:T(8,128)(2,1)S(1)}, bf16[256,2048]{1,0:T(8,128)(2,1)S(1)}, u32[]{:S(2)}, u32[]{:S(2)}) collective-permute-start(bf16[256,2048]{1,0:T(8,128)(2,1)S(1)} %collective-permute-done.43.refs_2_.refs_10_), channel_id=1, source_target_pairs={{0,1},{1,0},{2,3},{3,2},{4,5},{5,4},{6,7},{7,6},{8,9},{9,8},{10,11... | collective-permute-start | bytes 3145736 | tf_op jit(solution)/shard_map/ppermute | solution.py:39
  581.3 48.1 %all-to-all-start.5 = ((bf16[8,64,1024]{2,1,0:T(8,128)(2,1)}), bf16[8,64,1024]{2,1,0:T(8,128)(2,1)}, u32[]{:S(2)}, u32[]{:S(2)}) async-start(bf16[8,64,1024]{2,1,0:T(8,128)(2,1)} %bitcast.102), calls=%async_computation.8 | async-start | bytes 2097152 | tf_op jit(solution)/shard_map/all_to_all | solution.py:145
  585.6 36.9 %collective-permute-start.50 = (bf16[256,2048]{1,0:T(8,128)(2,1)}, bf16[256,2048]{1,0:T(8,128)(2,1)S(1)}, u32[]{:S(2)}, u32[]{:S(2)}) collective-permute-start(bf16[256,2048]{1,0:T(8,128)(2,1)} %add_convert_fusion.5), channel_id=1, source_target_pairs={{0,2},{1,5},{2,0},{3,7},{4,6},{5,1},{6,4},{7,3},{8,10},{9,13},{10,... | collective-permute-start | bytes 3145736 | tf_op jit(solution)/shard_map/ppermute | solution.py:39
  587.5 78.3 %collective-permute-start.49 = (bf16[256,2048]{1,0:T(8,128)(2,1)}, bf16[256,2048]{1,0:T(8,128)(2,1)}, u32[]{:S(2)}, u32[]{:S(2)}) collective-permute-start(bf16[256,2048]{1,0:T(8,128)(2,1)} %add_convert_fusion.6), channel_id=1, source_target_pairs={{0,2},{1,5},{2,0},{3,7},{4,6},{5,1},{6,4},{7,3},{8,10},{9,13},{10,... | collective-permute-start | bytes 3145736 | tf_op jit(solution)/shard_map/ppermute | solution.py:39
  587.7 46.3 %collective-permute-start.53 = (bf16[256,2048]{1,0:T(8,128)(2,1)}, bf16[256,2048]{1,0:T(8,128)(2,1)}, u32[]{:S(2)}, u32[]{:S(2)}) collective-permute-start(bf16[256,2048]{1,0:T(8,128)(2,1)} %copy-done.47), channel_id=1, source_target_pairs={{0,1},{1,0},{2,3},{3,2},{4,5},{5,4},{6,7},{7,6},{8,9},{9,8},{10,11... | collective-permute-start | bytes 3145736 | tf_op jit(solution)/shard_map/ppermute | solution.py:39
  591.0 43.0 %collective-permute-start.54 = (bf16[256,2048]{1,0:T(8,128)(2,1)}, bf16[256,2048]{1,0:T(8,128)(2,1)}, u32[]{:S(2)}, u32[]{:S(2)}) collective-permute-start(bf16[256,2048]{1,0:T(8,128)(2,1)} %convert_add_fusion.2), channel_id=1, source_target_pairs={{0,4},{1,3},{2,6},{3,1},{4,0},{5,7},{6,2},{7,5},{8,12},{9,11},{10,... | collective-permute-start | bytes 3145736 | tf_op jit(solution)/shard_map/ppermute | solution.py:39
  599.8 53.1 %collective-permute-start.57 = (bf16[256,2048]{1,0:T(8,128)(2,1)}, bf16[256,2048]{1,0:T(8,128)(2,1)}, u32[]{:S(2)}, u32[]{:S(2)}) collective-permute-start(bf16[256,2048]{1,0:T(8,128)(2,1)} %add_convert_fusion.1), channel_id=1, source_target_pairs={{0,2},{1,5},{2,0},{3,7},{4,6},{5,1},{6,4},{7,3},{8,10},{9,13},{10,... | collective-permute-start | bytes 3145736 | tf_op jit(solution)/shard_map/ppermute | solution.py:39
  623.7 42.1 %collective-permute-start.51 = (bf16[256,2048]{1,0:T(8,128)(2,1)}, bf16[256,2048]{1,0:T(8,128)(2,1)}, u32[]{:S(2)}, u32[]{:S(2)}) collective-permute-start(bf16[256,2048]{1,0:T(8,128)(2,1)} %add_convert_fusion.4), channel_id=1, source_target_pairs={{0,1},{1,0},{2,3},{3,2},{4,5},{5,4},{6,7},{7,6},{8,9},{9,8},{10,11... | collective-permute-start | bytes 3145736 | tf_op jit(solution)/shard_map/ppermute | solution.py:39
  629.4 41.1 %all-to-all-start.4 = ((bf16[8,64,2048]{2,1,0:T(8,128)(2,1)}), bf16[8,64,2048]{2,1,0:T(8,128)(2,1)}, u32[]{:S(2)}, u32[]{:S(2)}) async-start(bf16[8,64,2048]{2,1,0:T(8,128)(2,1)} %bitcast.99), calls=%async_computation.7 | async-start | bytes 4194304 | tf_op jit(solution)/shard_map/all_to_all | solution.py:145
  (107 other events, 1557.2 us)
Sparse Core Ops, SparseCore 0:
  33.0 80.1 all-gather.3
  114.8 148.1 all-gather.5
  264.6 78.9 all-gather.7
  345.7 75.2 reduce-scatter.3
  427.3 141.8 reduce-scatter.5
  571.5 77.4 reduce-scatter.7

commit v4 on v3

--- a/solution.py
+++ b/solution.py
@@ -117,13 +117,17 @@
         two = (two + self.other_core(four).astype(F32) + far_one).astype(BF16)
         return after((zero, one), two, three) + (two, three)
 
+    def scatter_near(self, sums):
+        zero, one, two, three = sums
+        return zero, one, self.near(two), self.near(three)
+
     def scatter_end(self, sums):
         zero, one, two, three = sums
-        partner = self.other_core((one + self.near(three).astype(F32)).astype(BF16))
-        return zero + self.near(two).astype(F32) + partner.astype(F32)
+        partner = self.other_core((one + three.astype(F32)).astype(BF16))
+        return zero + two.astype(F32) + partner.astype(F32)
 
     def scatter_tokens(self, array, weights, at=0):
-        return self.scatter_end(self.scatter_begin(array, weights, at))
+        return self.scatter_end(self.scatter_near(self.scatter_begin(array, weights, at)))
 
     def share_columns(self, weight):
         return lax.all_to_all(weight, self.axes, split_axis=1, concat_axis=0, tiled=True)
@@ -153,6 +157,10 @@
 
 
 SMALL = pl.CostEstimate(flops=1024, bytes_accessed=1024, transcendentals=0)
+
+
+def cost(microseconds):
+    return pl.CostEstimate(flops=int(microseconds * 1.1e9), bytes_accessed=int(microseconds * 3e6), transcendentals=0)
 
 
 def vmem(limit):
@@ -288,7 +296,7 @@
         out_specs=block,
         scratch_shapes=[pltpu.VMEM((tokens, step), BF16)],
         compiler_params=vmem(48),
-        cost_estimate=SMALL,
+        cost_estimate=cost(model * width / 175000),
         name="parts_product",
     )(*parts, right, *([added] if added is not None else []))
 
@@ -314,7 +322,7 @@
         out_specs=pl.BlockSpec((step, width + rest), lambda j: (j, 0)),
         scratch_shapes=[pltpu.VMEM((tokens, step), BF16)],
         compiler_params=vmem(48),
-        cost_estimate=SMALL,
+        cost_estimate=cost(14),
         name="attention_terms",
     )(*first, *second, right, other)
 
@@ -600,7 +608,7 @@
         ),
         out_shape=jax.ShapeDtypeStruct(saved.shape, BF16),
         compiler_params=vmem(56),
-        cost_estimate=SMALL,
+        cost_estimate=cost(36),
         name="attend_back",
     )(places, *parts, weight, saved, lse, cosine, sine, start)
 
@@ -675,31 +683,35 @@
     down_grad = MLP.scatter_weight(down_terms)
     d_gate_up = feed_back(after(dy_all, down_terms), down_all, slope)
     inner_sums = MLP.scatter_begin(d_gate_up, gate_up_all)
-    gate_up_terms = after(MLP.weight_terms(two_all, after(d_gate_up, *inner_sums)), down_grad)
-    gate_up_grad = MLP.scatter_weight(gate_up_terms)
-    inner_two = MLP.scatter_end(after(inner_sums[:2], gate_up_terms) + inner_sums[2:])
+    gate_up_terms = MLP.weight_terms(two_all, after(d_gate_up, *inner_sums))
+    inner_sums = MLP.scatter_near(inner_sums)
+    gate_up_grad = MLP.scatter_weight(after(gate_up_terms, down_grad, *inner_sums))
+    inner_two = MLP.scatter_end(inner_sums)
 
     d_first = grad_rows.astype(F32) + norm_input(MLP.from_slots(inner_two, outer), normed_two, factor_two)
     d_attn_all = ATTN.gather_tokens(ATTN.to_slots(d_first.astype(BF16), outer))
-    zero, one, two, three = MLP.scatter_begin(after(hidden, d_first), down_all)
-    d_attn_all = after(d_attn_all, zero, one, two, three)
+    mlp_sums = MLP.scatter_begin(after(hidden, d_first), down_all)
+    d_attn_all = after(d_attn_all, *mlp_sums)
     d_qkv = attend_back(d_attn_all, attn_all[0], saved, lse, cosine, sine, start, places, length)
-    zero, one = after((zero, one), d_qkv)
-    attn_terms = after(attention_terms(one_all, d_qkv, d_attn_all, mixed), gate_up_grad)
-    attn_grad = ATTN.scatter_weight(attn_terms)
-    inner_one = ATTN.scatter_tokens(d_qkv, attn_all)
-    tokens_grad = d_first + norm_input(ATTN.from_slots(inner_one, outer), normed_one, factor_one)
-    mlp_out = MLP.scatter_end((zero, one, two, three))
+    terms = attention_terms(one_all, d_qkv, d_attn_all, mixed)
+    inner_sums = ATTN.scatter_begin(after(d_qkv, terms), attn_all)
+    attn_grad = ATTN.scatter_weight(after(terms, gate_up_grad, inner_sums[0]))
+    mlp_sums = MLP.scatter_near(after(mlp_sums, *inner_sums))
+    gate_up_grad, down_grad = after((gate_up_grad, down_grad), *inner_sums)
+    inner_one = ATTN.scatter_end(ATTN.scatter_near(inner_sums))
+    tokens_grad = (d_first + norm_input(ATTN.from_slots(inner_one, outer), normed_one, factor_one)).astype(BF16)
+    mlp_out = MLP.scatter_end(mlp_sums)
     block_out = (first_sum + MLP.from_slots(mlp_out, outer)).astype(BF16)
 
-    down_w = MLP.return_columns(down_grad)
+    down_w = jnp.transpose(MLP.return_columns(down_grad).astype(F32))
     gate_w, up_w, gain_mlp = part_columns(MLP.return_columns(gate_up_grad), [w_gate, w_up], gain_two, UNIT)
+    attn_grad = after(attn_grad, tokens_grad, block_out, down_w)
     query_w, key_w, value_w, out_w, gain_attn = part_columns(
         ATTN.return_columns(attn_grad), [w_query, w_key, w_value], gain_one, LANES, w_out.shape[0]
     )
     return (
         block_out.reshape(shape),
-        tokens_grad.astype(BF16).reshape(shape),
+        tokens_grad.reshape(shape),
         gain_attn.reshape(-1),
         query_w,
         key_w,
@@ -708,7 +720,7 @@
         gain_mlp.reshape(-1),
         gate_w,
         up_w,
-        jnp.transpose(down_w.astype(F32)),
+        down_w,
     )
 
 

time: 720 us -> 698 us (0.969)
  other arithmetic: 57.8 us -> 49.2 us
  starting transfers between devices: 59.4 us -> 51.7 us
    all_to_all x3, waiting for transfers between devices: 0.01 us -> 28.6 us  [return_columns(): lax.all_to_all(grad, self.axes, split_axis=0, concat_axis=1, tiled=True)]
    ppermute x56, waiting for transfers between devices: 177 us -> 154 us  [flip(): return lax.ppermute(x, axes, [(i, i ^ masks[i & 1]) for i in range(8)])]
    all_to_all x1, waiting for transfers between devices: 17.4 us -> 2.53 us  [share_columns(): lax.all_to_all(weight, self.axes, split_axis=1, concat_axis=0, tiled=True)]
    convert_element_type x4 -> x6, other arithmetic: 7.27 us -> 15.6 us  [the longest x4 8.63 us: scatter_end(): partner = self.other_core((one + three.astype(F32)).astype(BF16))]
    unnamed x140 -> x134, local copies, waits for them, and re-layouts: 28.7 us -> 23.7 us
  transfers between devices with their start and end apart: 69 -> 69, of which waited for: 22 -> 29; matrix products, arithmetic and copies ran while one was open for 9% -> 8% of each run, Pallas kernels for 35% -> 36%
where the time goes in v4:
time: 698 us; the launch traced here: 687 us
  Pallas kernels  250 us (36%)
  waiting for transfers between devices  232 us (33%)
  starting transfers between devices  51.7 us (7%)
  blocking collectives  50.3 us (7%)
  other arithmetic  49.2 us (7%)
  local copies, waits for them, and re-layouts  37.9 us (5%)
  between operations  15.4 us (2%)
    ppermute x56, waiting for transfers between devices, flip(): return lax.ppermute(x, axes, [(i, i ^ masks[i & 1]) for i in range(8)])  154 us
    pallas_call x16, Pallas kernels, rows_product(): pl.pallas_call(body, grid=(count * inner,), out_shape=[jax.ShapeDtypeStru...  62.6 us
    all_to_all x2, blocking collectives, share_columns(): lax.all_to_all(weight, self.axes, split_axis=1, concat_axis=0, tiled=True)  50.3 us
    pallas_call x2, Pallas kernels, parts_product(): pl.pallas_call(body, grid=(model // step,), out_shape=jax.ShapeDtypeStruc...  37.9 us
    pallas_call x1, Pallas kernels, attend(): pl.pallas_call(functools.partial(attend_body, blocks=length // size, size...  36 us
    pallas_call x1, Pallas kernels, attend_back(): pl.pallas_call(functools.partial(attend_back_body, blocks=length // size,...  35.9 us
    ppermute x56, starting transfers between devices, flip(): return lax.ppermute(x, axes, [(i, i ^ masks[i & 1]) for i in range(8)])  33.5 us
    pallas_call x1, Pallas kernels, feed_forward(): pl.pallas_call(body, grid=(width // (2 * UNIT),), out_shape=[jax.ShapeDty...  29.1 us
  transfers between devices with their start and end apart: 69, of which 29 were waited for; matrix products, arithmetic and copies ran while one was open for 8% of the time, Pallas kernels for 36%

profile of v4, /device:TPU:0, one launch (start us, length us, event | category | flops | bytes accessed | tf_op | source)
XLA Modules:
  0.0 686.6 jit_solution(4498806866580608041)
XLA Ops:
  12.3 20.6 %all_to_all.108 = bf16[64,8,1024]{2,0,1:T(8,128)(2,1)} all-to-all(bf16[64,8,1024]{2,0,1:T(8,128)(2,1)S(1)} %bitcast.97), channel_id=1, replica_groups=mesh['r'=1,'zh'=2,'zl'=2,'y'=2,'x'=2,'c'=2] {'y','x','c'}, dimensions={1} | all-to-all | bytes 2097152 | tf_op jit(solution)/shard_map/all_to_all | solution.py:133
  40.4 29.8 %all_to_all.109 = bf16[64,8,2048]{2,0,1:T(8,128)(2,1)} all-to-all(bf16[64,8,2048]{2,0,1:T(8,128)(2,1)S(1)} %bitcast.91), channel_id=1, replica_groups=mesh['r'=1,'zh'=2,'zl'=2,'y'=2,'x'=2,'c'=2] {'y','x','c'}, dimensions={1} | all-to-all | bytes 4194304 | tf_op jit(solution)/shard_map/all_to_all | solution.py:133
  70.8 14.2 %collective-permute-done.1.refs_2_ = bf16[256,2048]{1,0:T(8,128)(2,1)S(1)} collective-permute-done((bf16[256,2048]{1,0:T(8,128)(2,1)S(1)}, bf16[256,2048]{1,0:T(8,128)(2,1)S(1)}, u32[]{:S(2)}, u32[]{:S(2)}) %collective-permute-start.1) | collective-permute-done | bytes 1048608 | tf_op jit(solution)/shard_map/ppermute | solution.py:39
  88.8 19.8 %collective-permute-done.8 = s32[512,1]{0,1:T(1,128)S(1)} collective-permute-done((s32[512,1]{0,1:T(1,128)S(1)}, s32[512,1]{0,1:T(1,128)S(1)}, u32[]{:S(2)}, u32[]{:S(2)}) %collective-permute-start.8) | collective-permute-done | bytes 2080 | tf_op jit(solution)/shard_map/ppermute | solution.py:43
  124.2 36.0 %attend.1 = (bf16[2048,768]{1,0:T(8,128)(2,1)}, bf16[2048,256]{1,0:T(8,128)(2,1)}, f32[2048,256]{1,0:T(8,128)}) custom-call(s32[16]{0:T(128)} %concatenate.59.place_ref, bf16[256,2048]{1,0:T(8,128)(2,1)} %copy-done.13, bf16[256,2048]{1,0:T(8,128)(2,1)} %copy-done.28, bf16[256,2048]{1,0:T(8,128)(2,1)} %copy-done.26, bf16[256,2048]{1,0:T(8,128)(2,1)} %copy-done.30, ...), custom_call_target="tpu_custom_call" | custom-call | flops 1024 | bytes 1024 | tf_op jit(solution)/shard_map/attend/pallas_call | solution.py:569
  182.8 8.2 %collective-permute-done.12 = bf16[256,2048]{1,0:T(8,128)(2,1)} collective-permute-done((bf16[256,2048]{1,0:T(8,128)(2,1)}, bf16[256,2048]{1,0:T(8,128)(2,1)}, u32[]{:S(2)}, u32[]{:S(2)}) %collective-permute-start.12) | collective-permute-done | bytes 1048608 | tf_op jit(solution)/shard_map/ppermute | solution.py:39
  205.3 10.9 %collective-permute-done.14 = bf16[256,2048]{1,0:T(8,128)(2,1)} collective-permute-done((bf16[256,2048]{1,0:T(8,128)(2,1)}, bf16[256,2048]{1,0:T(8,128)(2,1)}, u32[]{:S(2)}, u32[]{:S(2)}) %collective-permute-start.14) | collective-permute-done | bytes 1048608 | tf_op jit(solution)/shard_map/ppermute | solution.py:39
  221.8 11.7 %collective-permute-done.18.refs_2_ = bf16[256,2048]{1,0:T(8,128)(2,1)S(1)} collective-permute-done((bf16[256,2048]{1,0:T(8,128)(2,1)S(1)}, bf16[256,2048]{1,0:T(8,128)(2,1)S(1)}, u32[]{:S(2)}, u32[]{:S(2)}) %collective-permute-start.18) | collective-permute-done | bytes 1048608 | tf_op jit(solution)/shard_map/ppermute | solution.py:39
  235.5 17.7 %collective-permute-done.25.refs_2_ = bf16[256,2048]{1,0:T(8,128)(2,1)} collective-permute-done((bf16[256,2048]{1,0:T(8,128)(2,1)S(1)}, bf16[256,2048]{1,0:T(8,128)(2,1)}, u32[]{:S(2)}, u32[]{:S(2)}) %collective-permute-start.25) | collective-permute-done | bytes 1048608 | tf_op jit(solution)/shard_map/ppermute | solution.py:39
  259.5 16.0 %collective-permute-done.19.refs_3_ = bf16[256,2048]{1,0:T(8,128)(2,1)S(1)} collective-permute-done((bf16[256,2048]{1,0:T(8,128)(2,1)S(1)}, bf16[256,2048]{1,0:T(8,128)(2,1)S(1)}, u32[]{:S(2)}, u32[]{:S(2)}) %collective-permute-start.19) | collective-permute-done | bytes 1048608 | tf_op jit(solution)/shard_map/ppermute | solution.py:39
  275.6 6.5 collective-permute-done.29.refs_6_
  282.1 7.6 %collective-permute-done.26.refs_3_ = bf16[256,2048]{1,0:T(8,128)(2,1)} collective-permute-done((bf16[256,2048]{1,0:T(8,128)(2,1)S(1)}, bf16[256,2048]{1,0:T(8,128)(2,1)}, u32[]{:S(2)}, u32[]{:S(2)}) %collective-permute-start.26) | collective-permute-done | bytes 1048608 | tf_op jit(solution)/shard_map/ppermute | solution.py:39
  291.8 29.1 %feed_forward.1 = (bf16[2048,1024]{1,0:T(8,128)(2,1)}, f32[2048,2048]{1,0:T(8,128)}) custom-call(bf16[256,2048]{1,0:T(8,128)(2,1)} %copy-done.11, bf16[256,2048]{1,0:T(8,128)(2,1)} %copy-done.36, bf16[256,2048]{1,0:T(8,128)(2,1)} %copy-done.34, bf16[256,2048]{1,0:T(8,128)(2,1)} %copy-done.38, bf16[256,2048]{1,0:T(8,128)(2,1)} %copy-done.40, ...), custom_call_target="tpu_custom_call" | custom-call | flops 1024 | bytes 1024 | tf_op jit(solution)/shard_map/feed_forward/pallas_call | solution.py:377
  320.9 13.4 %parts_product.2 = bf16[2048,1024]{1,0:T(8,128)(2,1)} custom-call(bf16[256,2048]{1,0:T(8,128)(2,1)S(1)} %bitcast.88, bf16[256,2048]{1,0:T(8,128)(2,1)S(1)} %copy-done.43, bf16[256,2048]{1,0:T(8,128)(2,1)} %collective-permute-done.25.refs_2_, bf16[256,2048]{1,0:T(8,128)(2,1)} %collective-permute-done.26.refs_3_, ...), custom_call_target="tpu_custom_call" | custom-call | flops 13182098432 | bytes 35951176 | tf_op jit(solution)/shard_map/parts_product/pallas_call | solution.py:289
  334.4 9.2 %all-gather.8.cloned.1.call-done.refs_8_.refs_0_ = bf16[2048,1024]{1,0:T(8,128)(2,1)} async-done(((bf16[512,1024]{1,0:T(8,128)(2,1)}), bf16[2048,1024]{1,0:T(8,128)(2,1)}) %all-gather.8.cloned.1.call-update) | async-done | bytes 4194320 | tf_op jit(solution)/shard_map/all_gather | solution.py:136
  343.6 19.3 %feed_back.1.array_ref.refs_8_ = bf16[2048,2048]{1,0:T(8,128)(2,1)} custom-call(bf16[256,2048]{1,0:T(8,128)(2,1)} %bitcast.85, bf16[256,2048]{1,0:T(8,128)(2,1)} %copy-done.42, bf16[256,2048]{1,0:T(8,128)(2,1)} %collective-permute-done.25.refs_2_, bf16[256,2048]{1,0:T(8,128)(2,1)} %collective-permute-done.26.refs_3_, ...), custom_call_target="tpu_custom_call" | custom-call | flops 1024 | bytes 1024 | tf_op jit(solution)/shard_map/feed_back/pallas_call | solution.py:411
  366.4 7.3 %rows_product.20 = (f32[256,2048]{1,0:T(8,128)S(1)}, bf16[256,2048]{1,0:T(8,128)(2,1)S(1)}) custom-call(bf16[2048,2048]{1,0:T(8,128)(2,1)S(1)} %copy-done.3, bf16[2048,2048]{1,0:T(8,128)(2,1)} %all-gather.6.cloned.1.call-done.refs_8_.refs_0_), custom_call_target="tpu_custom_call" | custom-call | flops 1024 | bytes 1024 | tf_op jit(solution)/shard_map/rows_product/pallas_call | solution.py:259
  373.8 7.3 %rows_product.23 = (bf16[256,2048]{1,0:T(8,128)(2,1)S(1)}, bf16[256,2048]{1,0:T(8,128)(2,1)S(1)}) custom-call(bf16[2048,2048]{1,0:T(8,128)(2,1)S(1)} %copy-done.3, bf16[2048,2048]{1,0:T(8,128)(2,1)} %all-gather.6.cloned.1.call-done.refs_8_.refs_0_), custom_call_target="tpu_custom_call" | custom-call | flops 1024 | bytes 1024 | tf_op jit(solution)/shard_map/rows_product/pallas_call | solution.py:259
  383.6 7.4 %rows_product.22 = (f32[256,2048]{1,0:T(8,128)S(1)}, f32[256,2048]{1,0:T(8,128)S(1)}) custom-call(bf16[2048,2048]{1,0:T(8,128)(2,1)S(1)} %copy-done.3, bf16[2048,2048]{1,0:T(8,128)(2,1)} %all-gather.6.cloned.1.call-done.refs_8_.refs_0_), custom_call_target="tpu_custom_call" | custom-call | flops 1024 | bytes 1024 | tf_op jit(solution)/shard_map/rows_product/pallas_call | solution.py:259
  393.7 7.3 %rows_product.21 = (f32[256,2048]{1,0:T(8,128)S(1)}, f32[256,2048]{1,0:T(8,128)S(1)}) custom-call(bf16[2048,2048]{1,0:T(8,128)(2,1)S(1)} %copy-done.3, bf16[2048,2048]{1,0:T(8,128)(2,1)} %all-gather.6.cloned.1.call-done.refs_8_.refs_0_), custom_call_target="tpu_custom_call" | custom-call | flops 1024 | bytes 1024 | tf_op jit(solution)/shard_map/rows_product/pallas_call | solution.py:259
  405.4 24.5 %parts_product.3 = bf16[2048,2048]{1,0:T(8,128)(2,1)} custom-call(bf16[256,2048]{1,0:T(8,128)(2,1)S(1)} %copy-done.12, bf16[256,2048]{1,0:T(8,128)(2,1)S(1)} %copy-done.37, bf16[256,2048]{1,0:T(8,128)(2,1)S(1)} %copy-done.35, bf16[256,2048]{1,0:T(8,128)(2,1)S(1)} %copy-done.39, bf16[256,2048]{1,0:T(8,128)(2,1)S(1)} %copy-done.41, ...), custom_call_target="tpu_custom_call" | custom-call | flops 26364196864 | bytes 71902352 | tf_op jit(solution)/shard_map/parts_product/pallas_call | solution.py:289
  447.5 5.3 collective-permute-done.43.refs_2_.refs_10_
  462.7 15.3 %collective-permute-done.47.refs_6_.refs_14_ = bf16[256,2048]{1,0:T(8,128)(2,1)} collective-permute-done((bf16[256,2048]{1,0:T(8,128)(2,1)S(1)}, bf16[256,2048]{1,0:T(8,128)(2,1)}, u32[]{:S(2)}, u32[]{:S(2)}) %collective-permute-start.47) | collective-permute-done | bytes 1048608 | tf_op jit(solution)/shard_map/ppermute | solution.py:39
  481.1 8.1 %collective-permute-done.40 = bf16[256,2048]{1,0:T(8,128)(2,1)S(1)} collective-permute-done((bf16[256,2048]{1,0:T(8,128)(2,1)S(1)}, bf16[256,2048]{1,0:T(8,128)(2,1)S(1)}, u32[]{:S(2)}, u32[]{:S(2)}) %collective-permute-start.40) | collective-permute-done | bytes 1048608 | tf_op jit(solution)/shard_map/ppermute | solution.py:39
  492.4 35.9 %attend_back.1.refs_16_.array_ref = bf16[2048,768]{1,0:T(8,128)(2,1)} custom-call(s32[16]{0:T(128)} %concatenate.59.place_ref, bf16[256,2048]{1,0:T(8,128)(2,1)} %copy-done.58, bf16[256,2048]{1,0:T(8,128)(2,1)} %collective-permute-done.42.refs_1_.refs_9_, bf16[256,2048]{1,0:T(8,128)(2,1)} %copy-done.62, ...), custom_call_target="tpu_custom_call" | custom-call | flops 39600001024 | bytes 108000000 | tf_op jit(solution)/shard_map/attend_back/pallas_call | solution.py:593
  529.5 14.9 %attention_terms.1 = bf16[2048,1024]{1,0:T(8,128)(2,1)} custom-call(bf16[256,2048]{1,0:T(8,128)(2,1)S(1)} %copy-done.14, bf16[256,2048]{1,0:T(8,128)(2,1)S(1)} %copy-done.29, bf16[256,2048]{1,0:T(8,128)(2,1)S(1)} %copy-done.27, bf16[256,2048]{1,0:T(8,128)(2,1)S(1)} %copy-done.31, bf16[256,2048]{1,0:T(8,128)(2,1)S(1)} %copy-done.33, ...), custom_call_target="tpu_custom_call" | custom-call | flops 15399999488 | bytes 42000000 | tf_op jit(solution)/shard_map/attention_terms/pallas_call | solution.py:317
  562.2 6.1 collective-permute-done.51
  573.6 12.8 %collective-permute-done.57 = bf16[256,2048]{1,0:T(8,128)(2,1)S(1)} collective-permute-done((bf16[256,2048]{1,0:T(8,128)(2,1)S(1)}, bf16[256,2048]{1,0:T(8,128)(2,1)S(1)}, u32[]{:S(2)}, u32[]{:S(2)}) %collective-permute-start.57) | collective-permute-done | bytes 1048608 | tf_op jit(solution)/shard_map/ppermute | solution.py:39
  602.0 19.1 %all-to-all-done.3 = bf16[8,64,1024]{2,1,0:T(8,128)(2,1)S(1)} async-done(((bf16[8,64,1024]{2,1,0:T(8,128)(2,1)}), bf16[8,64,1024]{2,1,0:T(8,128)(2,1)S(1)}, u32[]{:S(2)}, u32[]{:S(2)}) %all-to-all-start.3) | async-done | bytes 1048608 | tf_op jit(solution)/shard_map/all_to_all | solution.py:149
  638.1 13.1 %reduce-scatter.8.cloned.1.call-done = bf16[512,1024]{1,0:T(8,128)(2,1)} async-done(((bf16[2048,1024]{1,0:T(8,128)(2,1)}), bf16[512,1024]{1,0:T(8,128)(2,1)}) %reduce-scatter.8.cloned.1.call-update) | async-done | bytes 1048592 | tf_op jit(solution)/shard_map/reduce_scatter | solution.py:146
  661.7 5.0 part_columns.3
  668.0 5.8 all-to-all-done.4
  (332 shorter events, 205.8 us)
Async XLA Ops:
  7.2 117.1 %all-gather.4.cloned.1.call-start = ((), (), s32[]{:S(2)}) async-start(), calls=%async_computation.9 | async-start | bytes 5242880 | tf_op jit(solution)/shard_map/all_gather | solution.py:136
  32.9 258.8 %all-gather.6.cloned.1.call-start = ((), (), s32[]{:S(2)}) async-start(), calls=%async_computation.10 | async-start | bytes 10485760 | tf_op jit(solution)/shard_map/all_gather | solution.py:136
  85.1 28.5 %collective-permute-start.5 = (bf16[256,2048]{1,0:T(8,128)(2,1)S(1)}, bf16[256,2048]{1,0:T(8,128)(2,1)}, u32[]{:S(2)}, u32[]{:S(2)}) collective-permute-start(bf16[256,2048]{1,0:T(8,128)(2,1)S(1)} %collective-permute-done.1.refs_2_), channel_id=1, source_target_pairs={{0,4},{1,3},{2,6},{3,1},{4,0},{5,7},{6,2},{7,5},{8,12},{9,11},{10,... | collective-permute-start | bytes 3145736 | tf_op jit(solution)/shard_map/ppermute | solution.py:39
  85.6 28.5 %collective-permute-start.2 = (bf16[256,2048]{1,0:T(8,128)(2,1)S(1)}, bf16[256,2048]{1,0:T(8,128)(2,1)S(1)}, u32[]{:S(2)}, u32[]{:S(2)}) collective-permute-start(bf16[256,2048]{1,0:T(8,128)(2,1)S(1)} %collective-permute-done.refs_1_), channel_id=1, source_target_pairs={{0,2},{1,5},{2,0},{3,7},{4,6},{5,1},{6,4},{7,3},{8,10},{9,13},{10,... | collective-permute-start | bytes 3145736 | tf_op jit(solution)/shard_map/ppermute | solution.py:39
  172.1 26.4 %collective-permute-start.15 = (bf16[256,2048]{1,0:T(8,128)(2,1)}, bf16[256,2048]{1,0:T(8,128)(2,1)}, u32[]{:S(2)}, u32[]{:S(2)}) collective-permute-start(bf16[256,2048]{1,0:T(8,128)(2,1)} %add_convert_fusion.11), channel_id=1, source_target_pairs={{0,2},{1,5},{2,0},{3,7},{4,6},{5,1},{6,4},{7,3},{8,10},{9,13},{10,... | collective-permute-start | bytes 3145736 | tf_op jit(solution)/shard_map/ppermute | solution.py:39
  174.4 30.9 %all-to-all-start.2 = ((bf16[64,8,1024]{2,0,1:T(8,128)(2,1)}), bf16[64,8,1024]{2,0,1:T(8,128)(2,1)}, u32[]{:S(2)}, u32[]{:S(2)}) async-start(bf16[64,8,1024]{2,0,1:T(8,128)(2,1)} %bitcast.95), calls=%async_computation.2 | async-start | bytes 2097152 | tf_op jit(solution)/shard_map/all_to_all | solution.py:133
  178.6 164.9 %all-gather.8.cloned.1.call-start = ((), (), s32[]{:S(2)}) async-start(), calls=%async_computation.11 | async-start | bytes 5242880 | tf_op jit(solution)/shard_map/all_gather | solution.py:136
  205.3 224.6 %reduce-scatter.4.cloned.1.call-start = ((), (), s32[]{:S(2)}) async-start(), calls=%async_computation.12 | async-start | bytes 5242880 | tf_op jit(solution)/shard_map/reduce_scatter | solution.py:146
  220.4 32.8 %collective-permute-start.25 = (bf16[256,2048]{1,0:T(8,128)(2,1)S(1)}, bf16[256,2048]{1,0:T(8,128)(2,1)}, u32[]{:S(2)}, u32[]{:S(2)}) collective-permute-start(bf16[256,2048]{1,0:T(8,128)(2,1)S(1)} %bitcast.86), channel_id=1, source_target_pairs={{0,2},{1,5},{2,0},{3,7},{4,6},{5,1},{6,4},{7,3},{8,10},{9,13},{10,... | collective-permute-start | bytes 3145736 | tf_op jit(solution)/shard_map/ppermute | solution.py:39
  221.7 32.3 %collective-permute-start.24 = (bf16[256,2048]{1,0:T(8,128)(2,1)S(1)}, bf16[256,2048]{1,0:T(8,128)(2,1)S(1)}, u32[]{:S(2)}, u32[]{:S(2)}) collective-permute-start(bf16[256,2048]{1,0:T(8,128)(2,1)S(1)} %bitcast.87), channel_id=1, source_target_pairs={{0,1},{1,0},{2,3},{3,2},{4,5},{5,4},{6,7},{7,6},{8,9},{9,8},{10,11... | collective-permute-start | bytes 3145736 | tf_op jit(solution)/shard_map/ppermute | solution.py:39
  234.2 41.3 %collective-permute-start.19 = (bf16[256,2048]{1,0:T(8,128)(2,1)S(1)}, bf16[256,2048]{1,0:T(8,128)(2,1)S(1)}, u32[]{:S(2)}, u32[]{:S(2)}) collective-permute-start(bf16[256,2048]{1,0:T(8,128)(2,1)S(1)} %collective-permute-done.17.refs_1_), channel_id=1, source_target_pairs={{0,2},{1,5},{2,0},{3,7},{4,6},{5,1},{6,4},{7,3},{8,10},{9,13},{10,... | collective-permute-start | bytes 3145736 | tf_op jit(solution)/shard_map/ppermute | solution.py:39
  253.2 28.9 %collective-permute-start.29 = (bf16[256,2048]{1,0:T(8,128)(2,1)}, bf16[256,2048]{1,0:T(8,128)(2,1)}, u32[]{:S(2)}, u32[]{:S(2)}) collective-permute-start(bf16[256,2048]{1,0:T(8,128)(2,1)} %collective-permute-done.25.refs_2_), channel_id=1, source_target_pairs={{0,4},{1,3},{2,6},{3,1},{4,0},{5,7},{6,2},{7,5},{8,12},{9,11},{10,... | collective-permute-start | bytes 3145736 | tf_op jit(solution)/shard_map/ppermute | solution.py:39
  254.0 35.7 %collective-permute-start.26 = (bf16[256,2048]{1,0:T(8,128)(2,1)S(1)}, bf16[256,2048]{1,0:T(8,128)(2,1)}, u32[]{:S(2)}, u32[]{:S(2)}) collective-permute-start(bf16[256,2048]{1,0:T(8,128)(2,1)S(1)} %collective-permute-done.24.refs_1_), channel_id=1, source_target_pairs={{0,2},{1,5},{2,0},{3,7},{4,6},{5,1},{6,4},{7,3},{8,10},{9,13},{10,... | collective-permute-start | bytes 3145736 | tf_op jit(solution)/shard_map/ppermute | solution.py:39
  256.2 33.5 %collective-permute-start.20 = (bf16[256,2048]{1,0:T(8,128)(2,1)S(1)}, bf16[256,2048]{1,0:T(8,128)(2,1)S(1)}, u32[]{:S(2)}, u32[]{:S(2)}) collective-permute-start(bf16[256,2048]{1,0:T(8,128)(2,1)S(1)} %collective-permute-done.18.refs_2_), channel_id=1, source_target_pairs={{0,1},{1,0},{2,3},{3,2},{4,5},{5,4},{6,7},{7,6},{8,9},{9,8},{10,11... | collective-permute-start | bytes 3145736 | tf_op jit(solution)/shard_map/ppermute | solution.py:39
  259.5 30.8 %collective-permute-start.23 = (bf16[256,2048]{1,0:T(8,128)(2,1)S(1)}, bf16[256,2048]{1,0:T(8,128)(2,1)S(1)}, u32[]{:S(2)}, u32[]{:S(2)}) collective-permute-start(bf16[256,2048]{1,0:T(8,128)(2,1)S(1)} %collective-permute-done.22.refs_6_), channel_id=1, source_target_pairs={{0,1},{1,0},{2,3},{3,2},{4,5},{5,4},{6,7},{7,6},{8,9},{9,8},{10,11... | collective-permute-start | bytes 3145736 | tf_op jit(solution)/shard_map/ppermute | solution.py:39
  282.1 38.8 %collective-permute-start.27 = (bf16[256,2048]{1,0:T(8,128)(2,1)}, bf16[256,2048]{1,0:T(8,128)(2,1)}, u32[]{:S(2)}, u32[]{:S(2)}) collective-permute-start(bf16[256,2048]{1,0:T(8,128)(2,1)} %collective-permute-done.25.refs_2_), channel_id=1, source_target_pairs={{0,1},{1,0},{2,3},{3,2},{4,5},{5,4},{6,7},{7,6},{8,9},{9,8},{10,11... | collective-permute-start | bytes 3145736 | tf_op jit(solution)/shard_map/ppermute | solution.py:39
  289.7 31.2 %collective-permute-start.30 = (bf16[256,2048]{1,0:T(8,128)(2,1)}, bf16[256,2048]{1,0:T(8,128)(2,1)}, u32[]{:S(2)}, u32[]{:S(2)}) collective-permute-start(bf16[256,2048]{1,0:T(8,128)(2,1)} %collective-permute-done.29.refs_6_), channel_id=1, source_target_pairs={{0,1},{1,0},{2,3},{3,2},{4,5},{5,4},{6,7},{7,6},{8,9},{9,8},{10,11... | collective-permute-start | bytes 3145736 | tf_op jit(solution)/shard_map/ppermute | solution.py:39
  289.8 31.1 %collective-permute-start.28 = (bf16[256,2048]{1,0:T(8,128)(2,1)}, bf16[256,2048]{1,0:T(8,128)(2,1)}, u32[]{:S(2)}, u32[]{:S(2)}) collective-permute-start(bf16[256,2048]{1,0:T(8,128)(2,1)} %collective-permute-done.26.refs_3_), channel_id=1, source_target_pairs={{0,1},{1,0},{2,3},{3,2},{4,5},{5,4},{6,7},{7,6},{8,9},{9,8},{10,11... | collective-permute-start | bytes 3145736 | tf_op jit(solution)/shard_map/ppermute | solution.py:39
  334.3 237.1 %reduce-scatter.6.cloned.1.call-start = ((), (), s32[]{:S(2)}) async-start(), calls=%async_computation.13 | async-start | bytes 10485760 | tf_op jit(solution)/shard_map/reduce_scatter | solution.py:146
  392.3 37.6 %collective-permute-start.36 = (bf16[256,2048]{1,0:T(8,128)(2,1)}, bf16[256,2048]{1,0:T(8,128)(2,1)}, u32[]{:S(2)}, u32[]{:S(2)}) collective-permute-start(bf16[256,2048]{1,0:T(8,128)(2,1)} %add_convert_fusion.8), channel_id=1, source_target_pairs={{0,2},{1,5},{2,0},{3,7},{4,6},{5,1},{6,4},{7,3},{8,10},{9,13},{10,... | collective-permute-start | bytes 3145736 | tf_op jit(solution)/shard_map/ppermute | solution.py:39
  429.9 221.3 %reduce-scatter.8.cloned.1.call-start = ((), (), s32[]{:S(2)}) async-start(), calls=%async_computation.14 | async-start | bytes 5242880 | tf_op jit(solution)/shard_map/reduce_scatter | solution.py:146
  453.4 26.4 %collective-permute-start.44 = (bf16[256,2048]{1,0:T(8,128)(2,1)}, bf16[256,2048]{1,0:T(8,128)(2,1)}, u32[]{:S(2)}, u32[]{:S(2)}) collective-permute-start(bf16[256,2048]{1,0:T(8,128)(2,1)} %collective-permute-done.42.refs_1_.refs_9_), channel_id=1, source_target_pairs={{0,2},{1,5},{2,0},{3,7},{4,6},{5,1},{6,4},{7,3},{8,10},{9,13},{10,... | collective-permute-start | bytes 3145736 | tf_op jit(solution)/shard_map/ppermute | solution.py:39
  454.2 26.9 %collective-permute-start.39 = (bf16[256,2048]{1,0:T(8,128)(2,1)S(1)}, bf16[256,2048]{1,0:T(8,128)(2,1)S(1)}, u32[]{:S(2)}, u32[]{:S(2)}) collective-permute-start(bf16[256,2048]{1,0:T(8,128)(2,1)S(1)} %get-tuple-element.162), channel_id=1, source_target_pairs={{0,1},{1,0},{2,3},{3,2},{4,5},{5,4},{6,7},{7,6},{8,9},{9,8},{10,11... | collective-permute-start | bytes 3145736 | tf_op jit(solution)/shard_map/ppermute | solution.py:39
  454.5 34.7 %collective-permute-start.40 = (bf16[256,2048]{1,0:T(8,128)(2,1)S(1)}, bf16[256,2048]{1,0:T(8,128)(2,1)S(1)}, u32[]{:S(2)}, u32[]{:S(2)}) collective-permute-start(bf16[256,2048]{1,0:T(8,128)(2,1)S(1)} %convert_add_fusion.3), channel_id=1, source_target_pairs={{0,4},{1,3},{2,6},{3,1},{4,0},{5,7},{6,2},{7,5},{8,12},{9,11},{10,... | collective-permute-start | bytes 3145736 | tf_op jit(solution)/shard_map/ppermute | solution.py:39
  462.7 28.0 %collective-permute-start.45 = (bf16[256,2048]{1,0:T(8,128)(2,1)S(1)}, bf16[256,2048]{1,0:T(8,128)(2,1)S(1)}, u32[]{:S(2)}, u32[]{:S(2)}) collective-permute-start(bf16[256,2048]{1,0:T(8,128)(2,1)S(1)} %collective-permute-done.43.refs_2_.refs_10_), channel_id=1, source_target_pairs={{0,1},{1,0},{2,3},{3,2},{4,5},{5,4},{6,7},{7,6},{8,9},{9,8},{10,11... | collective-permute-start | bytes 3145736 | tf_op jit(solution)/shard_map/ppermute | solution.py:39
  573.0 26.5 %collective-permute-start.54 = (bf16[256,2048]{1,0:T(8,128)(2,1)}, bf16[256,2048]{1,0:T(8,128)(2,1)}, u32[]{:S(2)}, u32[]{:S(2)}) collective-permute-start(bf16[256,2048]{1,0:T(8,128)(2,1)} %add_convert_fusion.5), channel_id=1, source_target_pairs={{0,2},{1,5},{2,0},{3,7},{4,6},{5,1},{6,4},{7,3},{8,10},{9,13},{10,... | collective-permute-start | bytes 3145736 | tf_op jit(solution)/shard_map/ppermute | solution.py:39
  587.6 39.1 %collective-permute-start.58 = (bf16[256,2048]{1,0:T(8,128)(2,1)}, bf16[256,2048]{1,0:T(8,128)(2,1)}, u32[]{:S(2)}, u32[]{:S(2)}) collective-permute-start(bf16[256,2048]{1,0:T(8,128)(2,1)} %add_convert_fusion), channel_id=1, source_target_pairs={{0,1},{1,0},{2,3},{3,2},{4,5},{5,4},{6,7},{7,6},{8,9},{9,8},{10,11... | collective-permute-start | bytes 3145736 | tf_op jit(solution)/shard_map/ppermute | solution.py:39
  587.6 39.1 %collective-permute-start.56 = (bf16[256,2048]{1,0:T(8,128)(2,1)}, bf16[256,2048]{1,0:T(8,128)(2,1)}, u32[]{:S(2)}, u32[]{:S(2)}) collective-permute-start(bf16[256,2048]{1,0:T(8,128)(2,1)} %add_convert_fusion.4), channel_id=1, source_target_pairs={{0,2},{1,5},{2,0},{3,7},{4,6},{5,1},{6,4},{7,3},{8,10},{9,13},{10,... | collective-permute-start | bytes 3145736 | tf_op jit(solution)/shard_map/ppermute | solution.py:39
  589.1 32.0 %all-to-all-start.3 = ((bf16[8,64,1024]{2,1,0:T(8,128)(2,1)}), bf16[8,64,1024]{2,1,0:T(8,128)(2,1)S(1)}, u32[]{:S(2)}, u32[]{:S(2)}) async-start(bf16[8,64,1024]{2,1,0:T(8,128)(2,1)} %bitcast.104), calls=%async_computation.6 | async-start | bytes 2097152 | tf_op jit(solution)/shard_map/all_to_all | solution.py:149
  592.7 40.4 %collective-permute-start.53 = (bf16[256,2048]{1,0:T(8,128)(2,1)}, bf16[256,2048]{1,0:T(8,128)(2,1)}, u32[]{:S(2)}, u32[]{:S(2)}) collective-permute-start(bf16[256,2048]{1,0:T(8,128)(2,1)} %add_convert_fusion.6), channel_id=1, source_target_pairs={{0,2},{1,5},{2,0},{3,7},{4,6},{5,1},{6,4},{7,3},{8,10},{9,13},{10,... | collective-permute-start | bytes 3145736 | tf_op jit(solution)/shard_map/ppermute | solution.py:39
  602.0 31.1 %collective-permute-start.55 = (bf16[256,2048]{1,0:T(8,128)(2,1)}, bf16[256,2048]{1,0:T(8,128)(2,1)}, u32[]{:S(2)}, u32[]{:S(2)}) collective-permute-start(bf16[256,2048]{1,0:T(8,128)(2,1)} %add_convert_fusion.2), channel_id=1, source_target_pairs={{0,1},{1,0},{2,3},{3,2},{4,5},{5,4},{6,7},{7,6},{8,9},{9,8},{10,11... | collective-permute-start | bytes 3145736 | tf_op jit(solution)/shard_map/ppermute | solution.py:39
  622.1 32.8 %all-to-all-start.5 = ((bf16[8,64,2048]{2,1,0:T(8,128)(2,1)}), bf16[8,64,2048]{2,1,0:T(8,128)(2,1)}, u32[]{:S(2)}, u32[]{:S(2)}) async-start(bf16[8,64,2048]{2,1,0:T(8,128)(2,1)} %bitcast.99), calls=%async_computation.8 | async-start | bytes 4194304 | tf_op jit(solution)/shard_map/all_to_all | solution.py:149
  (104 other events, 1418.8 us)
Sparse Core Ops, SparseCore 0:
  33.0 80.1 all-gather.3
  114.8 148.1 all-gather.5
  264.6 78.9 all-gather.7
  345.7 75.2 reduce-scatter.3
  430.0 141.3 reduce-scatter.5
  573.7 77.4 reduce-scatter.7

commit v5 on v4

--- a/solution.py
+++ b/solution.py
@@ -97,13 +97,18 @@
     def far(self, x):
         return flip(x, self.axes, (4, 2))
 
-    def gather_tokens(self, x):
+    def gather_near(self, x):
         partner = self.other_core(x)
-        near_one = self.near(x)
-        near_two = self.near(partner)
+        return x, partner, self.near(x), self.near(partner)
+
+    def gather_far(self, parts):
+        x, partner, near_one, near_two = parts
         far_one = self.far(near_one)
         parts = [x, partner, near_one, near_two, self.other_core(near_one), self.other_core(near_two)]
         return parts + [far_one, self.other_core(far_one)]
+
+    def gather_tokens(self, x):
+        return self.gather_far(self.gather_near(x))
 
     def scatter_begin(self, array, weights, at=0):
         six, seven = rows_product(array, weights, 6, (F32, BF16), at)
@@ -564,7 +569,7 @@
 def attend(parts, weight, cosine, sine, start, places, length):
     size, model = parts[0].shape
     tokens = 8 * size
-    width = weight.shape[1] * 3 // 4
+    width = weight.shape[1]
     pairs = width // (3 * LANES)
     return pl.pallas_call(
         functools.partial(attend_body, blocks=length // size, size=size),
@@ -589,14 +594,14 @@
 def attend_back(parts, weight, saved, lse, cosine, sine, start, places, length):
     size, model = parts[0].shape
     tokens = 8 * size
-    pairs = weight.shape[1] // (4 * LANES)
+    pairs = weight.shape[1] // LANES
     return pl.pallas_call(
         functools.partial(attend_back_body, blocks=length // size, size=size),
         grid_spec=pltpu.PrefetchScalarGridSpec(
             num_scalar_prefetch=1,
             grid=(pairs, tokens // length),
             in_specs=[whole(p) for p in parts]
-            + [pl.BlockSpec((model, LANES), lambda p, s, places: (0, 3 * pairs + p)), by_sequence(length, 3 * LANES), by_sequence(length, LANES)]
+            + [by_pair(model, LANES), by_sequence(length, 3 * LANES), by_sequence(length, LANES)]
             + [whole(t) for t in (cosine, sine, start)],
             out_specs=by_pair(tokens, 3 * LANES),
             scratch_shapes=[
@@ -645,15 +650,6 @@
     gain_one = attn_gain.astype(F32)[:, None]
     gain_two = mlp_gain.astype(F32)[:, None]
 
-    attn_mixed = mix_columns([w_query, w_key, w_value], gain_one, LANES, [jnp.transpose(w_out)])
-    attn_all = ATTN.gather_weight(ATTN.share_columns(attn_mixed))
-    inputs = after(tokens, attn_mixed).reshape(own, model).astype(F32)
-    normed_one, factor_one = rms_rows(inputs)
-    one_low = normed_one.astype(BF16)
-    gate_up_rows = MLP.share_columns(mix_columns([after(w_gate, one_low), w_up], gain_two, UNIT))
-    gate_up_all = MLP.gather_weight(gate_up_rows)
-
-    one_all = ATTN.gather_tokens(ATTN.to_slots(one_low, outer))
     where = positions.reshape(own, 1)
     for axis in ("c", "x", "y"):
         where = jnp.concatenate([where, swap(where, axis)], axis=0)
@@ -666,18 +662,44 @@
     places = jnp.concatenate([slot_part[slots], slots])
     row = jnp.arange(2 * length, dtype=jnp.int32)
     start = (((row // own % 4) ^ place) * own + row % own - where)[:, None]
-    saved, mixed, lse = attend(after(one_all, gate_up_rows), attn_all[0], cosine, sine, start, places, length)
+
+    out_rows = jnp.transpose(w_out)
+    (out_all,) = ATTN.gather_weight(out_rows)
+    qkv_mixed = mix_columns([w_query, w_key, w_value], gain_one, LANES)
+    qkv_all = ATTN.gather_weight(after(ATTN.share_columns(qkv_mixed), out_all))
+    inputs = after(tokens, qkv_mixed).reshape(own, model).astype(F32)
+    normed_one, factor_one = rms_rows(inputs)
+    one_low = normed_one.astype(BF16)
+    count = w_gate.shape[0]
+    out_blocks = [out_all[i * count : (i + 1) * count] for i in range(out_all.shape[0] // count)]
+    rows_mixed = mix_columns(
+        [after(w_gate, one_low, cosine, sine, start, places), w_up], gain_two, UNIT, out_blocks
+    )
+
+    one_all = ATTN.gather_tokens(ATTN.to_slots(one_low, outer))
+    rows_shared = MLP.share_columns(rows_mixed)
+    split = w_gate.shape[1] // 4
+    width = w_out.shape[0] // 8
+    gate_up_rows = rows_shared[:, :split]
+    out_all = [
+        jnp.concatenate(
+            [rows_shared[:, split + i * width : split + (i + 1) * width] for i in range(len(out_blocks))], axis=0
+        )
+    ]
+    gate_up_all = MLP.gather_weight(gate_up_rows)
+    saved, mixed, lse = attend(after(one_all, gate_up_rows), qkv_all[0], cosine, sine, start, places, length)
+    grad_rows = out_grad.reshape(own, model)
+    dy_near = MLP.gather_near(MLP.to_slots(after(grad_rows, gate_up_rows), outer))
+    dy_all = MLP.gather_far(after(dy_near, mixed))
     down_rows = MLP.share_columns(jnp.transpose(after(w_down, mixed)))
     down_all = MLP.gather_weight(after(down_rows, gate_up_rows))
 
-    attn_out = ATTN.scatter_tokens(mixed, attn_all, 3)
+    attn_out = ATTN.scatter_tokens(after(mixed, *dy_near), out_all)
     first_sum = inputs + ATTN.from_slots(attn_out, outer)
 
-    grad_rows = out_grad.reshape(own, model)
     normed_two, factor_two = rms_rows(first_sum)
     two_low = MLP.to_slots(normed_two.astype(BF16), outer)
-    two_all = MLP.gather_tokens(two_low)
-    dy_all = MLP.gather_tokens(MLP.to_slots(after(grad_rows, one_all), outer))
+    two_all = MLP.gather_tokens(after(two_low, *dy_all))
     hidden, slope = feed_forward(two_all, gate_up_all)
     down_terms = MLP.weight_terms(dy_all, hidden)
     down_grad = MLP.scatter_weight(down_terms)
@@ -692,9 +714,9 @@
     d_attn_all = ATTN.gather_tokens(ATTN.to_slots(d_first.astype(BF16), outer))
     mlp_sums = MLP.scatter_begin(after(hidden, d_first), down_all)
     d_attn_all = after(d_attn_all, *mlp_sums)
-    d_qkv = attend_back(d_attn_all, attn_all[0], saved, lse, cosine, sine, start, places, length)
+    d_qkv = attend_back(d_attn_all, out_all[0], saved, lse, cosine, sine, start, places, length)
     terms = attention_terms(one_all, d_qkv, d_attn_all, mixed)
-    inner_sums = ATTN.scatter_begin(after(d_qkv, terms), attn_all)
+    inner_sums = ATTN.scatter_begin(after(d_qkv, terms), qkv_all)
     attn_grad = ATTN.scatter_weight(after(terms, gate_up_grad, inner_sums[0]))
     mlp_sums = MLP.scatter_near(after(mlp_sums, *inner_sums))
     gate_up_grad, down_grad = after((gate_up_grad, down_grad), *inner_sums)

time: 698 us -> 689 us (0.987)
  blocking collectives: 50.3 us -> 41.3 us
    ppermute x3, waiting for transfers between devices: 22.5 us -> 8.67 us  [swap(): return lax.ppermute(x, axis, [(0, 1), (1, 0)])]
    ppermute x56, waiting for transfers between devices: 154 us -> 164 us  [flip(): return lax.ppermute(x, axes, [(i, i ^ masks[i & 1]) for i in range(8)])]
    all_to_all x2 -> x1, blocking collectives: 50.3 us -> 41.3 us  [share_columns(): lax.all_to_all(weight, self.axes, split_axis=1, concat_axis=0, tiled=True)]
    unnamed x134 -> x148, local copies, waits for them, and re-layouts: 23.7 us -> 20.7 us
  transfers between devices with their start and end apart: 69 -> 71, of which waited for: 29 -> 28; matrix products, arithmetic and copies ran while one was open for 8% -> 9% of each run, Pallas kernels for 36% -> 36%
where the time goes in v5:
time: 689 us; the launch traced here: 681 us
  Pallas kernels  246 us (36%)
  waiting for transfers between devices  234 us (34%)
  starting transfers between devices  57.2 us (8%)
  other arithmetic  49.2 us (7%)
  blocking collectives  41.3 us (6%)
  local copies, waits for them, and re-layouts  38.6 us (6%)
  between operations  15.4 us (2%)
    ppermute x56, waiting for transfers between devices, flip(): return lax.ppermute(x, axes, [(i, i ^ masks[i & 1]) for i in range(8)])  164 us
    pallas_call x16, Pallas kernels, rows_product(): pl.pallas_call(body, grid=(count * inner,), out_shape=[jax.ShapeDtypeStru...  59.9 us
    all_to_all x1, blocking collectives, share_columns(): lax.all_to_all(weight, self.axes, split_axis=1, concat_axis=0, tiled=True)  41.3 us
    pallas_call x2, Pallas kernels, parts_product(): pl.pallas_call(body, grid=(model // step,), out_shape=jax.ShapeDtypeStruc...  37.8 us
    pallas_call x1, Pallas kernels, attend_back(): pl.pallas_call(functools.partial(attend_back_body, blocks=length // size,...  35.8 us
    pallas_call x1, Pallas kernels, attend(): pl.pallas_call(functools.partial(attend_body, blocks=length // size, size...  34.8 us
    ppermute x56, starting transfers between devices, flip(): return lax.ppermute(x, axes, [(i, i ^ masks[i & 1]) for i in range(8)])  31.5 us
    pallas_call x1, Pallas kernels, feed_forward(): pl.pallas_call(body, grid=(width // (2 * UNIT),), out_shape=[jax.ShapeDty...  29.1 us
  transfers between devices with their start and end apart: 71, of which 28 were waited for; matrix products, arithmetic and copies ran while one was open for 9% of the time, Pallas kernels for 36%

profile of v5, /device:TPU:0, one launch (start us, length us, event | category | flops | bytes accessed | tf_op | source)
XLA Modules:
  0.0 681.4 jit_solution(5230730648354096424)
XLA Ops:
  14.2 5.0 all-to-all-start.1
  22.2 8.7 %collective-permute-done.8 = s32[512,1]{0,1:T(1,128)S(1)} collective-permute-done((s32[512,1]{0,1:T(1,128)S(1)}, s32[512,1]{0,1:T(1,128)S(1)}, u32[]{:S(2)}, u32[]{:S(2)}) %collective-permute-start.8) | collective-permute-done | bytes 2080 | tf_op jit(solution)/shard_map/ppermute | solution.py:43
  34.4 5.8 all-gather.5.cloned.1.call-done
  56.3 41.3 %all_to_all.108 = bf16[64,8,3072]{2,0,1:T(8,128)(2,1)S(1)} all-to-all(bf16[64,8,3072]{2,0,1:T(8,128)(2,1)S(1)} %bitcast.92), channel_id=1, replica_groups=mesh['r'=1,'zh'=2,'zl'=2,'y'=2,'x'=2,'c'=2] {'y','x','c'}, dimensions={1} | all-to-all | bytes 6291456 | tf_op jit(solution)/shard_map/all_to_all | solution.py:138
  101.4 14.2 %collective-permute-done.1.refs_2_ = bf16[256,2048]{1,0:T(8,128)(2,1)S(1)} collective-permute-done((bf16[256,2048]{1,0:T(8,128)(2,1)S(1)}, bf16[256,2048]{1,0:T(8,128)(2,1)S(1)}, u32[]{:S(2)}, u32[]{:S(2)}) %collective-permute-start.1) | collective-permute-done | bytes 1048608 | tf_op jit(solution)/shard_map/ppermute | solution.py:39
  117.3 22.9 %collective-permute-done.5.refs_6_ = bf16[256,2048]{1,0:T(8,128)(2,1)S(1)} collective-permute-done((bf16[256,2048]{1,0:T(8,128)(2,1)S(1)}, bf16[256,2048]{1,0:T(8,128)(2,1)S(1)}, u32[]{:S(2)}, u32[]{:S(2)}) %collective-permute-start.5) | collective-permute-done | bytes 1048608 | tf_op jit(solution)/shard_map/ppermute | solution.py:39
  146.2 34.8 %attend.1 = (bf16[2048,768]{1,0:T(8,128)(2,1)}, bf16[2048,256]{1,0:T(8,128)(2,1)}, f32[2048,256]{1,0:T(8,128)}) custom-call(s32[16]{0:T(128)} %concatenate.62.place_ref, bf16[256,2048]{1,0:T(8,128)(2,1)} %copy-done.12, bf16[256,2048]{1,0:T(8,128)(2,1)} %copy-done.30, bf16[256,2048]{1,0:T(8,128)(2,1)} %copy-done.28, bf16[256,2048]{1,0:T(8,128)(2,1)} %copy-done.32, ...), custom_call_target="tpu_custom_call" | custom-call | flops 1024 | bytes 1024 | tf_op jit(solution)/shard_map/attend/pallas_call | solution.py:574
  201.3 10.8 %collective-permute-done.15 = bf16[256,2048]{1,0:T(8,128)(2,1)} collective-permute-done((bf16[256,2048]{1,0:T(8,128)(2,1)}, bf16[256,2048]{1,0:T(8,128)(2,1)}, u32[]{:S(2)}, u32[]{:S(2)}) %collective-permute-start.15) | collective-permute-done | bytes 1048608 | tf_op jit(solution)/shard_map/ppermute | solution.py:39
  222.5 7.7 %all-to-all-done.2 = bf16[64,8,1024]{2,0,1:T(8,128)(2,1)} async-done(((bf16[64,8,1024]{2,0,1:T(8,128)(2,1)}), bf16[64,8,1024]{2,0,1:T(8,128)(2,1)}, u32[]{:S(2)}, u32[]{:S(2)}) %all-to-all-start.2) | async-done | bytes 1048608 | tf_op jit(solution)/shard_map/all_to_all | solution.py:138
  230.9 14.0 %collective-permute-done.22.refs_6_ = bf16[256,2048]{1,0:T(8,128)(2,1)} collective-permute-done((bf16[256,2048]{1,0:T(8,128)(2,1)}, bf16[256,2048]{1,0:T(8,128)(2,1)}, u32[]{:S(2)}, u32[]{:S(2)}) %collective-permute-start.22) | collective-permute-done | bytes 1048608 | tf_op jit(solution)/shard_map/ppermute | solution.py:39
  251.5 13.7 %collective-permute-done.25.refs_2_ = bf16[256,2048]{1,0:T(8,128)(2,1)S(1)} collective-permute-done((bf16[256,2048]{1,0:T(8,128)(2,1)S(1)}, bf16[256,2048]{1,0:T(8,128)(2,1)S(1)}, u32[]{:S(2)}, u32[]{:S(2)}) %collective-permute-start.25) | collective-permute-done | bytes 1048608 | tf_op jit(solution)/shard_map/ppermute | solution.py:39
  266.5 24.3 %collective-permute-done.29.refs_6_ = bf16[256,2048]{1,0:T(8,128)(2,1)S(1)} collective-permute-done((bf16[256,2048]{1,0:T(8,128)(2,1)S(1)}, bf16[256,2048]{1,0:T(8,128)(2,1)S(1)}, u32[]{:S(2)}, u32[]{:S(2)}) %collective-permute-start.29) | collective-permute-done | bytes 1048608 | tf_op jit(solution)/shard_map/ppermute | solution.py:39
  295.2 29.1 %feed_forward.1 = (bf16[2048,1024]{1,0:T(8,128)(2,1)}, f32[2048,2048]{1,0:T(8,128)}) custom-call(bf16[256,2048]{1,0:T(8,128)(2,1)} %copy-done.10, bf16[256,2048]{1,0:T(8,128)(2,1)} %copy-done.38, bf16[256,2048]{1,0:T(8,128)(2,1)} %copy-done.36, bf16[256,2048]{1,0:T(8,128)(2,1)} %copy-done.40, bf16[256,2048]{1,0:T(8,128)(2,1)} %copy-done.42, ...), custom_call_target="tpu_custom_call" | custom-call | flops 1024 | bytes 1024 | tf_op jit(solution)/shard_map/feed_forward/pallas_call | solution.py:382
  324.3 13.3 %parts_product.2 = bf16[2048,1024]{1,0:T(8,128)(2,1)} custom-call(bf16[256,2048]{1,0:T(8,128)(2,1)S(1)} %bitcast.88, bf16[256,2048]{1,0:T(8,128)(2,1)} %collective-permute-done.10.refs_1_, bf16[256,2048]{1,0:T(8,128)(2,1)} %collective-permute-done.11.refs_2_, bf16[256,2048]{1,0:T(8,128)(2,1)} %collective-permute-done.12.refs_3_, ...), custom_call_target="tpu_custom_call" | custom-call | flops 13182098432 | bytes 35951176 | tf_op jit(solution)/shard_map/parts_product/pallas_call | solution.py:294
  338.1 19.7 %feed_back.1.array_ref.refs_8_ = bf16[2048,2048]{1,0:T(8,128)(2,1)} custom-call(bf16[256,2048]{1,0:T(8,128)(2,1)} %bitcast.85, bf16[256,2048]{1,0:T(8,128)(2,1)} %collective-permute-done.10.refs_1_, bf16[256,2048]{1,0:T(8,128)(2,1)} %collective-permute-done.11.refs_2_, bf16[256,2048]{1,0:T(8,128)(2,1)} %collective-permute-done.12.refs_3_, ...), custom_call_target="tpu_custom_call" | custom-call | flops 1024 | bytes 1024 | tf_op jit(solution)/shard_map/feed_back/pallas_call | solution.py:416
  361.2 7.3 %rows_product.20 = (f32[256,2048]{1,0:T(8,128)S(1)}, bf16[256,2048]{1,0:T(8,128)(2,1)S(1)}) custom-call(bf16[2048,2048]{1,0:T(8,128)(2,1)S(1)} %copy-done, bf16[2048,2048]{1,0:T(8,128)(2,1)} %all-gather.9.cloned.1.call-done.refs_8_.refs_0_), custom_call_target="tpu_custom_call" | custom-call | flops 1024 | bytes 1024 | tf_op jit(solution)/shard_map/rows_product/pallas_call | solution.py:264
  368.6 7.3 %rows_product.23 = (bf16[256,2048]{1,0:T(8,128)(2,1)S(1)}, bf16[256,2048]{1,0:T(8,128)(2,1)S(1)}) custom-call(bf16[2048,2048]{1,0:T(8,128)(2,1)S(1)} %copy-done, bf16[2048,2048]{1,0:T(8,128)(2,1)} %all-gather.9.cloned.1.call-done.refs_8_.refs_0_), custom_call_target="tpu_custom_call" | custom-call | flops 1024 | bytes 1024 | tf_op jit(solution)/shard_map/rows_product/pallas_call | solution.py:264
  376.9 7.4 %rows_product.22 = (f32[256,2048]{1,0:T(8,128)S(1)}, f32[256,2048]{1,0:T(8,128)S(1)}) custom-call(bf16[2048,2048]{1,0:T(8,128)(2,1)S(1)} %copy-done, bf16[2048,2048]{1,0:T(8,128)(2,1)} %all-gather.9.cloned.1.call-done.refs_8_.refs_0_), custom_call_target="tpu_custom_call" | custom-call | flops 1024 | bytes 1024 | tf_op jit(solution)/shard_map/rows_product/pallas_call | solution.py:264
  386.7 7.3 %rows_product.21 = (f32[256,2048]{1,0:T(8,128)S(1)}, f32[256,2048]{1,0:T(8,128)S(1)}) custom-call(bf16[2048,2048]{1,0:T(8,128)(2,1)S(1)} %copy-done, bf16[2048,2048]{1,0:T(8,128)(2,1)} %all-gather.9.cloned.1.call-done.refs_8_.refs_0_), custom_call_target="tpu_custom_call" | custom-call | flops 1024 | bytes 1024 | tf_op jit(solution)/shard_map/rows_product/pallas_call | solution.py:264
  398.3 24.5 %parts_product.3 = bf16[2048,2048]{1,0:T(8,128)(2,1)} custom-call(bf16[256,2048]{1,0:T(8,128)(2,1)S(1)} %copy-done.11, bf16[256,2048]{1,0:T(8,128)(2,1)S(1)} %copy-done.39, bf16[256,2048]{1,0:T(8,128)(2,1)S(1)} %copy-done.37, bf16[256,2048]{1,0:T(8,128)(2,1)S(1)} %copy-done.41, bf16[256,2048]{1,0:T(8,128)(2,1)S(1)} %copy-done.43, ...), custom_call_target="tpu_custom_call" | custom-call | flops 26364196864 | bytes 71902352 | tf_op jit(solution)/shard_map/parts_product/pallas_call | solution.py:294
  440.5 5.4 collective-permute-done.43.refs_2_.refs_10_
  456.8 14.7 %collective-permute-done.47.refs_6_.refs_14_ = bf16[256,2048]{1,0:T(8,128)(2,1)} collective-permute-done((bf16[256,2048]{1,0:T(8,128)(2,1)S(1)}, bf16[256,2048]{1,0:T(8,128)(2,1)}, u32[]{:S(2)}, u32[]{:S(2)}) %collective-permute-start.47) | collective-permute-done | bytes 1048608 | tf_op jit(solution)/shard_map/ppermute | solution.py:39
  475.1 7.6 %collective-permute-done.40 = bf16[256,2048]{1,0:T(8,128)(2,1)S(1)} collective-permute-done((bf16[256,2048]{1,0:T(8,128)(2,1)S(1)}, bf16[256,2048]{1,0:T(8,128)(2,1)S(1)}, u32[]{:S(2)}, u32[]{:S(2)}) %collective-permute-start.40) | collective-permute-done | bytes 1048608 | tf_op jit(solution)/shard_map/ppermute | solution.py:39
  486.0 35.8 %attend_back.1.refs_16_.array_ref = bf16[2048,768]{1,0:T(8,128)(2,1)} custom-call(s32[16]{0:T(128)} %concatenate.62.place_ref, bf16[256,2048]{1,0:T(8,128)(2,1)} %copy-done.65, bf16[256,2048]{1,0:T(8,128)(2,1)} %collective-permute-done.42.refs_1_.refs_9_, bf16[256,2048]{1,0:T(8,128)(2,1)} %copy-done.69, ...), custom_call_target="tpu_custom_call" | custom-call | flops 39600001024 | bytes 108000000 | tf_op jit(solution)/shard_map/attend_back/pallas_call | solution.py:598
  523.0 14.4 %attention_terms.1 = bf16[2048,1024]{1,0:T(8,128)(2,1)} custom-call(bf16[256,2048]{1,0:T(8,128)(2,1)S(1)} %copy-done.13, bf16[256,2048]{1,0:T(8,128)(2,1)S(1)} %copy-done.31, bf16[256,2048]{1,0:T(8,128)(2,1)S(1)} %copy-done.29, bf16[256,2048]{1,0:T(8,128)(2,1)S(1)} %copy-done.33, bf16[256,2048]{1,0:T(8,128)(2,1)S(1)} %copy-done.35, ...), custom_call_target="tpu_custom_call" | custom-call | flops 15399999488 | bytes 42000000 | tf_op jit(solution)/shard_map/attention_terms/pallas_call | solution.py:322
  555.1 5.5 collective-permute-done.51
  568.5 12.8 %collective-permute-done.57 = bf16[256,2048]{1,0:T(8,128)(2,1)S(1)} collective-permute-done((bf16[256,2048]{1,0:T(8,128)(2,1)S(1)}, bf16[256,2048]{1,0:T(8,128)(2,1)S(1)}, u32[]{:S(2)}, u32[]{:S(2)}) %collective-permute-start.57) | collective-permute-done | bytes 1048608 | tf_op jit(solution)/shard_map/ppermute | solution.py:39
  589.6 4.9 collective-permute-done.54
  596.9 19.2 %all-to-all-done.3 = bf16[8,64,1024]{2,1,0:T(8,128)(2,1)S(1)} async-done(((bf16[8,64,1024]{2,1,0:T(8,128)(2,1)}), bf16[8,64,1024]{2,1,0:T(8,128)(2,1)S(1)}, u32[]{:S(2)}, u32[]{:S(2)}) %all-to-all-start.3) | async-done | bytes 1048608 | tf_op jit(solution)/shard_map/all_to_all | solution.py:154
  633.0 13.3 %reduce-scatter.8.cloned.1.call-done = bf16[512,1024]{1,0:T(8,128)(2,1)} async-done(((bf16[2048,1024]{1,0:T(8,128)(2,1)}), bf16[512,1024]{1,0:T(8,128)(2,1)}) %reduce-scatter.8.cloned.1.call-update) | async-done | bytes 1048592 | tf_op jit(solution)/shard_map/reduce_scatter | solution.py:151
  656.6 5.0 part_columns.3
  663.0 5.8 all-to-all-done.4
  (354 shorter events, 202.7 us)
Async XLA Ops:
  7.2 33.1 %all-gather.5.cloned.1.call-start = ((), (), s32[]{:S(2)}) async-start(), calls=%async_computation.9 | async-start | bytes 1310720 | tf_op jit(solution)/shard_map/all_gather | solution.py:141
  19.2 127.0 %all-gather.7.cloned.1.call-start = ((), (), s32[]{:S(2)}) async-start(), calls=%async_computation.10 | async-start | bytes 3932160 | tf_op jit(solution)/shard_map/all_gather | solution.py:141
  40.3 254.9 %all-gather.9.cloned.1.call-start = ((), (), s32[]{:S(2)}) async-start(), calls=%async_computation.11 | async-start | bytes 10485760 | tf_op jit(solution)/shard_map/all_gather | solution.py:141
  116.8 25.9 %collective-permute-start.3 = (bf16[256,2048]{1,0:T(8,128)(2,1)S(1)}, bf16[256,2048]{1,0:T(8,128)(2,1)S(1)}, u32[]{:S(2)}, u32[]{:S(2)}) collective-permute-start(bf16[256,2048]{1,0:T(8,128)(2,1)S(1)} %collective-permute-done.1.refs_2_), channel_id=1, source_target_pairs={{0,1},{1,0},{2,3},{3,2},{4,5},{5,4},{6,7},{7,6},{8,9},{9,8},{10,11... | collective-permute-start | bytes 3145736 | tf_op jit(solution)/shard_map/ppermute | solution.py:39
  140.7 40.2 %collective-permute-start.11 = (bf16[256,2048]{1,0:T(8,128)(2,1)S(1)}, bf16[256,2048]{1,0:T(8,128)(2,1)}, u32[]{:S(2)}, u32[]{:S(2)}) collective-permute-start(bf16[256,2048]{1,0:T(8,128)(2,1)S(1)} %bitcast.87), channel_id=1, source_target_pairs={{0,2},{1,5},{2,0},{3,7},{4,6},{5,1},{6,4},{7,3},{8,10},{9,13},{10,... | collective-permute-start | bytes 3145736 | tf_op jit(solution)/shard_map/ppermute | solution.py:39
  141.4 39.5 %collective-permute-start.12 = (bf16[256,2048]{1,0:T(8,128)(2,1)}, bf16[256,2048]{1,0:T(8,128)(2,1)}, u32[]{:S(2)}, u32[]{:S(2)}) collective-permute-start(bf16[256,2048]{1,0:T(8,128)(2,1)} %collective-permute-done.10.refs_1_), channel_id=1, source_target_pairs={{0,2},{1,5},{2,0},{3,7},{4,6},{5,1},{6,4},{7,3},{8,10},{9,13},{10,... | collective-permute-start | bytes 3145736 | tf_op jit(solution)/shard_map/ppermute | solution.py:39
  191.5 26.4 %collective-permute-start.18 = (bf16[256,2048]{1,0:T(8,128)(2,1)}, bf16[256,2048]{1,0:T(8,128)(2,1)}, u32[]{:S(2)}, u32[]{:S(2)}) collective-permute-start(bf16[256,2048]{1,0:T(8,128)(2,1)} %add_convert_fusion.11), channel_id=1, source_target_pairs={{0,2},{1,5},{2,0},{3,7},{4,6},{5,1},{6,4},{7,3},{8,10},{9,13},{10,... | collective-permute-start | bytes 3145736 | tf_op jit(solution)/shard_map/ppermute | solution.py:39
  193.4 36.8 %all-to-all-start.2 = ((bf16[64,8,1024]{2,0,1:T(8,128)(2,1)}), bf16[64,8,1024]{2,0,1:T(8,128)(2,1)}, u32[]{:S(2)}, u32[]{:S(2)}) async-start(bf16[64,8,1024]{2,0,1:T(8,128)(2,1)} %bitcast.95), calls=%async_computation.2 | async-start | bytes 2097152 | tf_op jit(solution)/shard_map/all_to_all | solution.py:138
  197.7 140.5 %all-gather.11.cloned.1.call-start = ((), (), s32[]{:S(2)}) async-start(), calls=%async_computation.12 | async-start | bytes 5242880 | tf_op jit(solution)/shard_map/all_gather | solution.py:141
  197.7 47.1 %collective-permute-start.22 = (bf16[256,2048]{1,0:T(8,128)(2,1)}, bf16[256,2048]{1,0:T(8,128)(2,1)}, u32[]{:S(2)}, u32[]{:S(2)}) collective-permute-start(bf16[256,2048]{1,0:T(8,128)(2,1)} %collective-permute-done.11.refs_2_), channel_id=1, source_target_pairs={{0,4},{1,3},{2,6},{3,1},{4,0},{5,7},{6,2},{7,5},{8,12},{9,11},{10,... | collective-permute-start | bytes 3145736 | tf_op jit(solution)/shard_map/ppermute | solution.py:39
  215.2 31.8 %collective-permute-start.17 = (bf16[256,2048]{1,0:T(8,128)(2,1)}, bf16[256,2048]{1,0:T(8,128)(2,1)}, u32[]{:S(2)}, u32[]{:S(2)}) collective-permute-start(bf16[256,2048]{1,0:T(8,128)(2,1)} %add_convert_fusion.12), channel_id=1, source_target_pairs={{0,2},{1,5},{2,0},{3,7},{4,6},{5,1},{6,4},{7,3},{8,10},{9,13},{10,... | collective-permute-start | bytes 3145736 | tf_op jit(solution)/shard_map/ppermute | solution.py:39
  220.4 26.6 %collective-permute-start.19 = (bf16[256,2048]{1,0:T(8,128)(2,1)}, bf16[256,2048]{1,0:T(8,128)(2,1)}, u32[]{:S(2)}, u32[]{:S(2)}) collective-permute-start(bf16[256,2048]{1,0:T(8,128)(2,1)} %add_convert_fusion.10), channel_id=1, source_target_pairs={{0,1},{1,0},{2,3},{3,2},{4,5},{5,4},{6,7},{7,6},{8,9},{9,8},{10,11... | collective-permute-start | bytes 3145736 | tf_op jit(solution)/shard_map/ppermute | solution.py:39
  230.2 192.6 %reduce-scatter.4.cloned.1.call-start = ((), (), s32[]{:S(2)}) async-start(), calls=%async_computation.13 | async-start | bytes 5242880 | tf_op jit(solution)/shard_map/reduce_scatter | solution.py:151
  265.2 25.6 %collective-permute-start.29 = (bf16[256,2048]{1,0:T(8,128)(2,1)S(1)}, bf16[256,2048]{1,0:T(8,128)(2,1)S(1)}, u32[]{:S(2)}, u32[]{:S(2)}) collective-permute-start(bf16[256,2048]{1,0:T(8,128)(2,1)S(1)} %collective-permute-done.25.refs_2_), channel_id=1, source_target_pairs={{0,4},{1,3},{2,6},{3,1},{4,0},{5,7},{6,2},{7,5},{8,12},{9,11},{10,... | collective-permute-start | bytes 3145736 | tf_op jit(solution)/shard_map/ppermute | solution.py:39
  265.6 25.2 %collective-permute-start.26 = (bf16[256,2048]{1,0:T(8,128)(2,1)S(1)}, bf16[256,2048]{1,0:T(8,128)(2,1)S(1)}, u32[]{:S(2)}, u32[]{:S(2)}) collective-permute-start(bf16[256,2048]{1,0:T(8,128)(2,1)S(1)} %collective-permute-done.24.refs_1_), channel_id=1, source_target_pairs={{0,2},{1,5},{2,0},{3,7},{4,6},{5,1},{6,4},{7,3},{8,10},{9,13},{10,... | collective-permute-start | bytes 3145736 | tf_op jit(solution)/shard_map/ppermute | solution.py:39
  266.5 24.8 %collective-permute-start.27 = (bf16[256,2048]{1,0:T(8,128)(2,1)S(1)}, bf16[256,2048]{1,0:T(8,128)(2,1)S(1)}, u32[]{:S(2)}, u32[]{:S(2)}) collective-permute-start(bf16[256,2048]{1,0:T(8,128)(2,1)S(1)} %collective-permute-done.25.refs_2_), channel_id=1, source_target_pairs={{0,1},{1,0},{2,3},{3,2},{4,5},{5,4},{6,7},{7,6},{8,9},{9,8},{10,11... | collective-permute-start | bytes 3145736 | tf_op jit(solution)/shard_map/ppermute | solution.py:39
  337.7 228.8 %reduce-scatter.6.cloned.1.call-start = ((), (), s32[]{:S(2)}) async-start(), calls=%async_computation.14 | async-start | bytes 10485760 | tf_op jit(solution)/shard_map/reduce_scatter | solution.py:151
  385.6 37.2 %collective-permute-start.36 = (bf16[256,2048]{1,0:T(8,128)(2,1)}, bf16[256,2048]{1,0:T(8,128)(2,1)}, u32[]{:S(2)}, u32[]{:S(2)}) collective-permute-start(bf16[256,2048]{1,0:T(8,128)(2,1)} %add_convert_fusion.8), channel_id=1, source_target_pairs={{0,2},{1,5},{2,0},{3,7},{4,6},{5,1},{6,4},{7,3},{8,10},{9,13},{10,... | collective-permute-start | bytes 3145736 | tf_op jit(solution)/shard_map/ppermute | solution.py:39
  396.9 25.9 %collective-permute-start.35 = (bf16[256,2048]{1,0:T(8,128)(2,1)}, bf16[256,2048]{1,0:T(8,128)(2,1)S(1)}, u32[]{:S(2)}, u32[]{:S(2)}) collective-permute-start(bf16[256,2048]{1,0:T(8,128)(2,1)} %add_convert_fusion.9), channel_id=1, source_target_pairs={{0,2},{1,5},{2,0},{3,7},{4,6},{5,1},{6,4},{7,3},{8,10},{9,13},{10,... | collective-permute-start | bytes 3145736 | tf_op jit(solution)/shard_map/ppermute | solution.py:39
  422.9 223.5 %reduce-scatter.8.cloned.1.call-start = ((), (), s32[]{:S(2)}) async-start(), calls=%async_computation.15 | async-start | bytes 5242880 | tf_op jit(solution)/shard_map/reduce_scatter | solution.py:151
  445.9 25.7 %collective-permute-start.47 = (bf16[256,2048]{1,0:T(8,128)(2,1)S(1)}, bf16[256,2048]{1,0:T(8,128)(2,1)}, u32[]{:S(2)}, u32[]{:S(2)}) collective-permute-start(bf16[256,2048]{1,0:T(8,128)(2,1)S(1)} %collective-permute-done.43.refs_2_.refs_10_), channel_id=1, source_target_pairs={{0,4},{1,3},{2,6},{3,1},{4,0},{5,7},{6,2},{7,5},{8,12},{9,11},{10,... | collective-permute-start | bytes 3145736 | tf_op jit(solution)/shard_map/ppermute | solution.py:39
  447.4 26.4 %collective-permute-start.44 = (bf16[256,2048]{1,0:T(8,128)(2,1)}, bf16[256,2048]{1,0:T(8,128)(2,1)}, u32[]{:S(2)}, u32[]{:S(2)}) collective-permute-start(bf16[256,2048]{1,0:T(8,128)(2,1)} %collective-permute-done.42.refs_1_.refs_9_), channel_id=1, source_target_pairs={{0,2},{1,5},{2,0},{3,7},{4,6},{5,1},{6,4},{7,3},{8,10},{9,13},{10,... | collective-permute-start | bytes 3145736 | tf_op jit(solution)/shard_map/ppermute | solution.py:39
  448.8 26.3 %collective-permute-start.39 = (bf16[256,2048]{1,0:T(8,128)(2,1)S(1)}, bf16[256,2048]{1,0:T(8,128)(2,1)S(1)}, u32[]{:S(2)}, u32[]{:S(2)}) collective-permute-start(bf16[256,2048]{1,0:T(8,128)(2,1)S(1)} %get-tuple-element.176), channel_id=1, source_target_pairs={{0,1},{1,0},{2,3},{3,2},{4,5},{5,4},{6,7},{7,6},{8,9},{9,8},{10,11... | collective-permute-start | bytes 3145736 | tf_op jit(solution)/shard_map/ppermute | solution.py:39
  449.1 33.6 %collective-permute-start.40 = (bf16[256,2048]{1,0:T(8,128)(2,1)S(1)}, bf16[256,2048]{1,0:T(8,128)(2,1)S(1)}, u32[]{:S(2)}, u32[]{:S(2)}) collective-permute-start(bf16[256,2048]{1,0:T(8,128)(2,1)S(1)} %convert_add_fusion.3), channel_id=1, source_target_pairs={{0,4},{1,3},{2,6},{3,1},{4,0},{5,7},{6,2},{7,5},{8,12},{9,11},{10,... | collective-permute-start | bytes 3145736 | tf_op jit(solution)/shard_map/ppermute | solution.py:39
  455.9 28.2 %collective-permute-start.45 = (bf16[256,2048]{1,0:T(8,128)(2,1)S(1)}, bf16[256,2048]{1,0:T(8,128)(2,1)S(1)}, u32[]{:S(2)}, u32[]{:S(2)}) collective-permute-start(bf16[256,2048]{1,0:T(8,128)(2,1)S(1)} %collective-permute-done.43.refs_2_.refs_10_), channel_id=1, source_target_pairs={{0,1},{1,0},{2,3},{3,2},{4,5},{5,4},{6,7},{7,6},{8,9},{9,8},{10,11... | collective-permute-start | bytes 3145736 | tf_op jit(solution)/shard_map/ppermute | solution.py:39
  568.0 26.5 %collective-permute-start.54 = (bf16[256,2048]{1,0:T(8,128)(2,1)}, bf16[256,2048]{1,0:T(8,128)(2,1)}, u32[]{:S(2)}, u32[]{:S(2)}) collective-permute-start(bf16[256,2048]{1,0:T(8,128)(2,1)} %add_convert_fusion.5), channel_id=1, source_target_pairs={{0,2},{1,5},{2,0},{3,7},{4,6},{5,1},{6,4},{7,3},{8,10},{9,13},{10,... | collective-permute-start | bytes 3145736 | tf_op jit(solution)/shard_map/ppermute | solution.py:39
  582.6 39.1 %collective-permute-start.58 = (bf16[256,2048]{1,0:T(8,128)(2,1)}, bf16[256,2048]{1,0:T(8,128)(2,1)}, u32[]{:S(2)}, u32[]{:S(2)}) collective-permute-start(bf16[256,2048]{1,0:T(8,128)(2,1)} %add_convert_fusion), channel_id=1, source_target_pairs={{0,1},{1,0},{2,3},{3,2},{4,5},{5,4},{6,7},{7,6},{8,9},{9,8},{10,11... | collective-permute-start | bytes 3145736 | tf_op jit(solution)/shard_map/ppermute | solution.py:39
  582.6 39.1 %collective-permute-start.56 = (bf16[256,2048]{1,0:T(8,128)(2,1)}, bf16[256,2048]{1,0:T(8,128)(2,1)}, u32[]{:S(2)}, u32[]{:S(2)}) collective-permute-start(bf16[256,2048]{1,0:T(8,128)(2,1)} %add_convert_fusion.4), channel_id=1, source_target_pairs={{0,2},{1,5},{2,0},{3,7},{4,6},{5,1},{6,4},{7,3},{8,10},{9,13},{10,... | collective-permute-start | bytes 3145736 | tf_op jit(solution)/shard_map/ppermute | solution.py:39
  584.1 32.0 %all-to-all-start.3 = ((bf16[8,64,1024]{2,1,0:T(8,128)(2,1)}), bf16[8,64,1024]{2,1,0:T(8,128)(2,1)S(1)}, u32[]{:S(2)}, u32[]{:S(2)}) async-start(bf16[8,64,1024]{2,1,0:T(8,128)(2,1)} %bitcast.104), calls=%async_computation.6 | async-start | bytes 2097152 | tf_op jit(solution)/shard_map/all_to_all | solution.py:154
  587.6 40.4 %collective-permute-start.53 = (bf16[256,2048]{1,0:T(8,128)(2,1)}, bf16[256,2048]{1,0:T(8,128)(2,1)}, u32[]{:S(2)}, u32[]{:S(2)}) collective-permute-start(bf16[256,2048]{1,0:T(8,128)(2,1)} %add_convert_fusion.6), channel_id=1, source_target_pairs={{0,2},{1,5},{2,0},{3,7},{4,6},{5,1},{6,4},{7,3},{8,10},{9,13},{10,... | collective-permute-start | bytes 3145736 | tf_op jit(solution)/shard_map/ppermute | solution.py:39
  596.9 31.1 %collective-permute-start.55 = (bf16[256,2048]{1,0:T(8,128)(2,1)}, bf16[256,2048]{1,0:T(8,128)(2,1)}, u32[]{:S(2)}, u32[]{:S(2)}) collective-permute-start(bf16[256,2048]{1,0:T(8,128)(2,1)} %add_convert_fusion.2), channel_id=1, source_target_pairs={{0,1},{1,0},{2,3},{3,2},{4,5},{5,4},{6,7},{7,6},{8,9},{9,8},{10,11... | collective-permute-start | bytes 3145736 | tf_op jit(solution)/shard_map/ppermute | solution.py:39
  617.0 32.8 %all-to-all-start.5 = ((bf16[8,64,2048]{2,1,0:T(8,128)(2,1)}), bf16[8,64,2048]{2,1,0:T(8,128)(2,1)}, u32[]{:S(2)}, u32[]{:S(2)}) async-start(bf16[8,64,2048]{2,1,0:T(8,128)(2,1)} %bitcast.99), calls=%async_computation.8 | async-start | bytes 4194304 | tf_op jit(solution)/shard_map/all_to_all | solution.py:154
  (113 other events, 1516.5 us)
Sparse Core Ops, SparseCore 0:
  9.6 30.6 all-gather.4
  42.4 62.9 all-gather.6
  107.0 148.2 all-gather.8
  256.7 78.9 all-gather.10
  337.9 75.2 reduce-scatter.3
  423.0 143.3 reduce-scatter.5
  568.8 77.4 reduce-scatter.7

commit v6 on v5

--- a/solution.py
+++ b/solution.py
@@ -725,9 +725,10 @@
     mlp_out = MLP.scatter_end(mlp_sums)
     block_out = (first_sum + MLP.from_slots(mlp_out, outer)).astype(BF16)
 
-    down_w = jnp.transpose(MLP.return_columns(down_grad).astype(F32))
-    gate_w, up_w, gain_mlp = part_columns(MLP.return_columns(gate_up_grad), [w_gate, w_up], gain_two, UNIT)
-    attn_grad = after(attn_grad, tokens_grad, block_out, down_w)
+    gate_up_back = MLP.return_columns(gate_up_grad)
+    down_w = jnp.transpose(MLP.return_columns(after(down_grad, gate_up_back)).astype(F32))
+    gate_w, up_w, gain_mlp = part_columns(gate_up_back, [w_gate, w_up], gain_two, UNIT)
+    attn_grad = after(attn_grad, tokens_grad, block_out, down_w, gate_w)
     query_w, key_w, value_w, out_w, gain_attn = part_columns(
         ATTN.return_columns(attn_grad), [w_query, w_key, w_value], gain_one, LANES, w_out.shape[0]
     )

time: 689 us -> 693 us (level)
    ppermute x56, waiting for transfers between devices: 164 us -> 193 us  [flip(): return lax.ppermute(x, axes, [(i, i ^ masks[i & 1]) for i in range(8)])]
    reduce_scatter x3, waiting for transfers between devices: 17.7 us -> 4.39 us  [scatter_weight(): return lax.psum_scatter(terms, self.spread, scatter_dimension=0, tiled=True)]
    all_to_all x3, waiting for transfers between devices: 28.5 us -> 17.6 us  [return_columns(): lax.all_to_all(grad, self.axes, split_axis=0, concat_axis=1, tiled=True)]
    unnamed x148 -> x150, local copies, waits for them, and re-layouts: 20.7 us -> 20 us
  transfers between devices with their start and end apart: 71 -> 71, of which waited for: 28 -> 26; matrix products, arithmetic and copies ran while one was open for 9% -> 9% of each run, Pallas kernels for 36% -> 36%
where the time goes in v6:
time: 693 us; the launch traced here: 685 us
  Pallas kernels  246 us (35%)
  waiting for transfers between devices  238 us (34%)
  starting transfers between devices  57.3 us (8%)
  other arithmetic  48.8 us (7%)
  blocking collectives  41.3 us (6%)
  local copies, waits for them, and re-layouts  38 us (5%)
  between operations  15.4 us (2%)
    ppermute x56, waiting for transfers between devices, flip(): return lax.ppermute(x, axes, [(i, i ^ masks[i & 1]) for i in range(8)])  193 us
    pallas_call x16, Pallas kernels, rows_product(): pl.pallas_call(body, grid=(count * inner,), out_shape=[jax.ShapeDtypeStru...  59.9 us
    all_to_all x1, blocking collectives, share_columns(): lax.all_to_all(weight, self.axes, split_axis=1, concat_axis=0, tiled=True)  41.3 us
    pallas_call x2, Pallas kernels, parts_product(): pl.pallas_call(body, grid=(model // step,), out_shape=jax.ShapeDtypeStruc...  37.8 us
    pallas_call x1, Pallas kernels, attend_back(): pl.pallas_call(functools.partial(attend_back_body, blocks=length // size,...  35.9 us
    pallas_call x1, Pallas kernels, attend(): pl.pallas_call(functools.partial(attend_body, blocks=length // size, size...  34.8 us
    ppermute x56, starting transfers between devices, flip(): return lax.ppermute(x, axes, [(i, i ^ masks[i & 1]) for i in range(8)])  31 us
    pallas_call x1, Pallas kernels, feed_forward(): pl.pallas_call(body, grid=(width // (2 * UNIT),), out_shape=[jax.ShapeDty...  29.1 us
  transfers between devices with their start and end apart: 71, of which 26 were waited for; matrix products, arithmetic and copies ran while one was open for 9% of the time, Pallas kernels for 36%

profile of v6, /device:TPU:0, one launch (start us, length us, event | category | flops | bytes accessed | tf_op | source)
XLA Modules:
  0.0 684.8 jit_solution(9891831796368996811)
XLA Ops:
  14.2 5.0 all-to-all-start.1
  22.2 8.7 %collective-permute-done.8 = s32[512,1]{0,1:T(1,128)S(1)} collective-permute-done((s32[512,1]{0,1:T(1,128)S(1)}, s32[512,1]{0,1:T(1,128)S(1)}, u32[]{:S(2)}, u32[]{:S(2)}) %collective-permute-start.8) | collective-permute-done | bytes 2080 | tf_op jit(solution)/shard_map/ppermute | solution.py:43
  34.4 5.8 all-gather.5.cloned.1.call-done
  56.3 41.3 %all_to_all.108 = bf16[64,8,3072]{2,0,1:T(8,128)(2,1)S(1)} all-to-all(bf16[64,8,3072]{2,0,1:T(8,128)(2,1)S(1)} %bitcast.92), channel_id=1, replica_groups=mesh['r'=1,'zh'=2,'zl'=2,'y'=2,'x'=2,'c'=2] {'y','x','c'}, dimensions={1} | all-to-all | bytes 6291456 | tf_op jit(solution)/shard_map/all_to_all | solution.py:138
  101.4 14.2 %collective-permute-done.1.refs_2_ = bf16[256,2048]{1,0:T(8,128)(2,1)S(1)} collective-permute-done((bf16[256,2048]{1,0:T(8,128)(2,1)S(1)}, bf16[256,2048]{1,0:T(8,128)(2,1)S(1)}, u32[]{:S(2)}, u32[]{:S(2)}) %collective-permute-start.1) | collective-permute-done | bytes 1048608 | tf_op jit(solution)/shard_map/ppermute | solution.py:39
  117.3 22.9 %collective-permute-done.5.refs_6_ = bf16[256,2048]{1,0:T(8,128)(2,1)S(1)} collective-permute-done((bf16[256,2048]{1,0:T(8,128)(2,1)S(1)}, bf16[256,2048]{1,0:T(8,128)(2,1)S(1)}, u32[]{:S(2)}, u32[]{:S(2)}) %collective-permute-start.5) | collective-permute-done | bytes 1048608 | tf_op jit(solution)/shard_map/ppermute | solution.py:39
  146.2 34.8 %attend.1 = (bf16[2048,768]{1,0:T(8,128)(2,1)}, bf16[2048,256]{1,0:T(8,128)(2,1)}, f32[2048,256]{1,0:T(8,128)}) custom-call(s32[16]{0:T(128)} %concatenate.62.place_ref, bf16[256,2048]{1,0:T(8,128)(2,1)} %copy-done.12, bf16[256,2048]{1,0:T(8,128)(2,1)} %copy-done.30, bf16[256,2048]{1,0:T(8,128)(2,1)} %copy-done.28, bf16[256,2048]{1,0:T(8,128)(2,1)} %copy-done.32, ...), custom_call_target="tpu_custom_call" | custom-call | flops 1024 | bytes 1024 | tf_op jit(solution)/shard_map/attend/pallas_call | solution.py:574
  201.3 10.8 %collective-permute-done.15 = bf16[256,2048]{1,0:T(8,128)(2,1)} collective-permute-done((bf16[256,2048]{1,0:T(8,128)(2,1)}, bf16[256,2048]{1,0:T(8,128)(2,1)}, u32[]{:S(2)}, u32[]{:S(2)}) %collective-permute-start.15) | collective-permute-done | bytes 1048608 | tf_op jit(solution)/shard_map/ppermute | solution.py:39
  222.5 7.7 %all-to-all-done.2 = bf16[64,8,1024]{2,0,1:T(8,128)(2,1)} async-done(((bf16[64,8,1024]{2,0,1:T(8,128)(2,1)}), bf16[64,8,1024]{2,0,1:T(8,128)(2,1)}, u32[]{:S(2)}, u32[]{:S(2)}) %all-to-all-start.2) | async-done | bytes 1048608 | tf_op jit(solution)/shard_map/all_to_all | solution.py:138
  230.9 14.0 %collective-permute-done.22.refs_6_ = bf16[256,2048]{1,0:T(8,128)(2,1)} collective-permute-done((bf16[256,2048]{1,0:T(8,128)(2,1)}, bf16[256,2048]{1,0:T(8,128)(2,1)}, u32[]{:S(2)}, u32[]{:S(2)}) %collective-permute-start.22) | collective-permute-done | bytes 1048608 | tf_op jit(solution)/shard_map/ppermute | solution.py:39
  251.5 13.7 %collective-permute-done.25.refs_2_ = bf16[256,2048]{1,0:T(8,128)(2,1)S(1)} collective-permute-done((bf16[256,2048]{1,0:T(8,128)(2,1)S(1)}, bf16[256,2048]{1,0:T(8,128)(2,1)S(1)}, u32[]{:S(2)}, u32[]{:S(2)}) %collective-permute-start.25) | collective-permute-done | bytes 1048608 | tf_op jit(solution)/shard_map/ppermute | solution.py:39
  266.5 24.3 %collective-permute-done.29.refs_6_ = bf16[256,2048]{1,0:T(8,128)(2,1)S(1)} collective-permute-done((bf16[256,2048]{1,0:T(8,128)(2,1)S(1)}, bf16[256,2048]{1,0:T(8,128)(2,1)S(1)}, u32[]{:S(2)}, u32[]{:S(2)}) %collective-permute-start.29) | collective-permute-done | bytes 1048608 | tf_op jit(solution)/shard_map/ppermute | solution.py:39
  295.2 29.1 %feed_forward.1 = (bf16[2048,1024]{1,0:T(8,128)(2,1)}, f32[2048,2048]{1,0:T(8,128)}) custom-call(bf16[256,2048]{1,0:T(8,128)(2,1)} %copy-done.10, bf16[256,2048]{1,0:T(8,128)(2,1)} %copy-done.38, bf16[256,2048]{1,0:T(8,128)(2,1)} %copy-done.36, bf16[256,2048]{1,0:T(8,128)(2,1)} %copy-done.40, bf16[256,2048]{1,0:T(8,128)(2,1)} %copy-done.42, ...), custom_call_target="tpu_custom_call" | custom-call | flops 1024 | bytes 1024 | tf_op jit(solution)/shard_map/feed_forward/pallas_call | solution.py:382
  324.3 13.3 %parts_product.2 = bf16[2048,1024]{1,0:T(8,128)(2,1)} custom-call(bf16[256,2048]{1,0:T(8,128)(2,1)S(1)} %bitcast.88, bf16[256,2048]{1,0:T(8,128)(2,1)} %collective-permute-done.10.refs_1_, bf16[256,2048]{1,0:T(8,128)(2,1)} %collective-permute-done.11.refs_2_, bf16[256,2048]{1,0:T(8,128)(2,1)} %collective-permute-done.12.refs_3_, ...), custom_call_target="tpu_custom_call" | custom-call | flops 13182098432 | bytes 35951176 | tf_op jit(solution)/shard_map/parts_product/pallas_call | solution.py:294
  338.2 19.7 %feed_back.1.array_ref.refs_8_ = bf16[2048,2048]{1,0:T(8,128)(2,1)} custom-call(bf16[256,2048]{1,0:T(8,128)(2,1)} %bitcast.85, bf16[256,2048]{1,0:T(8,128)(2,1)} %collective-permute-done.10.refs_1_, bf16[256,2048]{1,0:T(8,128)(2,1)} %collective-permute-done.11.refs_2_, bf16[256,2048]{1,0:T(8,128)(2,1)} %collective-permute-done.12.refs_3_, ...), custom_call_target="tpu_custom_call" | custom-call | flops 1024 | bytes 1024 | tf_op jit(solution)/shard_map/feed_back/pallas_call | solution.py:416
  361.2 7.3 %rows_product.20 = (f32[256,2048]{1,0:T(8,128)S(1)}, bf16[256,2048]{1,0:T(8,128)(2,1)S(1)}) custom-call(bf16[2048,2048]{1,0:T(8,128)(2,1)S(1)} %copy-done, bf16[2048,2048]{1,0:T(8,128)(2,1)} %all-gather.9.cloned.1.call-done.refs_8_.refs_0_), custom_call_target="tpu_custom_call" | custom-call | flops 1024 | bytes 1024 | tf_op jit(solution)/shard_map/rows_product/pallas_call | solution.py:264
  368.6 7.3 %rows_product.23 = (bf16[256,2048]{1,0:T(8,128)(2,1)S(1)}, bf16[256,2048]{1,0:T(8,128)(2,1)S(1)}) custom-call(bf16[2048,2048]{1,0:T(8,128)(2,1)S(1)} %copy-done, bf16[2048,2048]{1,0:T(8,128)(2,1)} %all-gather.9.cloned.1.call-done.refs_8_.refs_0_), custom_call_target="tpu_custom_call" | custom-call | flops 1024 | bytes 1024 | tf_op jit(solution)/shard_map/rows_product/pallas_call | solution.py:264
  376.9 7.4 %rows_product.22 = (f32[256,2048]{1,0:T(8,128)S(1)}, f32[256,2048]{1,0:T(8,128)S(1)}) custom-call(bf16[2048,2048]{1,0:T(8,128)(2,1)S(1)} %copy-done, bf16[2048,2048]{1,0:T(8,128)(2,1)} %all-gather.9.cloned.1.call-done.refs_8_.refs_0_), custom_call_target="tpu_custom_call" | custom-call | flops 1024 | bytes 1024 | tf_op jit(solution)/shard_map/rows_product/pallas_call | solution.py:264
  386.7 7.3 %rows_product.21 = (f32[256,2048]{1,0:T(8,128)S(1)}, f32[256,2048]{1,0:T(8,128)S(1)}) custom-call(bf16[2048,2048]{1,0:T(8,128)(2,1)S(1)} %copy-done, bf16[2048,2048]{1,0:T(8,128)(2,1)} %all-gather.9.cloned.1.call-done.refs_8_.refs_0_), custom_call_target="tpu_custom_call" | custom-call | flops 1024 | bytes 1024 | tf_op jit(solution)/shard_map/rows_product/pallas_call | solution.py:264
  398.3 24.5 %parts_product.3 = bf16[2048,2048]{1,0:T(8,128)(2,1)} custom-call(bf16[256,2048]{1,0:T(8,128)(2,1)S(1)} %copy-done.11, bf16[256,2048]{1,0:T(8,128)(2,1)S(1)} %copy-done.39, bf16[256,2048]{1,0:T(8,128)(2,1)S(1)} %copy-done.37, bf16[256,2048]{1,0:T(8,128)(2,1)S(1)} %copy-done.41, bf16[256,2048]{1,0:T(8,128)(2,1)S(1)} %copy-done.43, ...), custom_call_target="tpu_custom_call" | custom-call | flops 26364196864 | bytes 71902352 | tf_op jit(solution)/shard_map/parts_product/pallas_call | solution.py:294
  440.5 5.3 collective-permute-done.43.refs_2_.refs_10_
  456.8 14.7 %collective-permute-done.47.refs_6_.refs_14_ = bf16[256,2048]{1,0:T(8,128)(2,1)} collective-permute-done((bf16[256,2048]{1,0:T(8,128)(2,1)S(1)}, bf16[256,2048]{1,0:T(8,128)(2,1)}, u32[]{:S(2)}, u32[]{:S(2)}) %collective-permute-start.47) | collective-permute-done | bytes 1048608 | tf_op jit(solution)/shard_map/ppermute | solution.py:39
  475.2 7.5 %collective-permute-done.40 = bf16[256,2048]{1,0:T(8,128)(2,1)S(1)} collective-permute-done((bf16[256,2048]{1,0:T(8,128)(2,1)S(1)}, bf16[256,2048]{1,0:T(8,128)(2,1)S(1)}, u32[]{:S(2)}, u32[]{:S(2)}) %collective-permute-start.40) | collective-permute-done | bytes 1048608 | tf_op jit(solution)/shard_map/ppermute | solution.py:39
  485.9 35.9 %attend_back.1.refs_16_.array_ref = bf16[2048,768]{1,0:T(8,128)(2,1)} custom-call(s32[16]{0:T(128)} %concatenate.62.place_ref, bf16[256,2048]{1,0:T(8,128)(2,1)} %copy-done.65, bf16[256,2048]{1,0:T(8,128)(2,1)} %collective-permute-done.42.refs_1_.refs_9_, bf16[256,2048]{1,0:T(8,128)(2,1)} %copy-done.70, ...), custom_call_target="tpu_custom_call" | custom-call | flops 39600001024 | bytes 108000000 | tf_op jit(solution)/shard_map/attend_back/pallas_call | solution.py:598
  523.0 14.4 %attention_terms.1 = bf16[2048,1024]{1,0:T(8,128)(2,1)} custom-call(bf16[256,2048]{1,0:T(8,128)(2,1)S(1)} %copy-done.13, bf16[256,2048]{1,0:T(8,128)(2,1)S(1)} %copy-done.31, bf16[256,2048]{1,0:T(8,128)(2,1)S(1)} %copy-done.29, bf16[256,2048]{1,0:T(8,128)(2,1)S(1)} %copy-done.33, bf16[256,2048]{1,0:T(8,128)(2,1)S(1)} %copy-done.35, ...), custom_call_target="tpu_custom_call" | custom-call | flops 15399999488 | bytes 42000000 | tf_op jit(solution)/shard_map/attention_terms/pallas_call | solution.py:322
  555.1 5.5 collective-permute-done.51
  568.5 4.5 all-to-all-start.3
  573.0 13.5 %collective-permute-done.57 = bf16[256,2048]{1,0:T(8,128)(2,1)} collective-permute-done((bf16[256,2048]{1,0:T(8,128)(2,1)S(1)}, bf16[256,2048]{1,0:T(8,128)(2,1)}, u32[]{:S(2)}, u32[]{:S(2)}) %collective-permute-start.57) | collective-permute-done | bytes 1048608 | tf_op jit(solution)/shard_map/ppermute | solution.py:39
  590.9 13.0 %collective-permute-done.54 = bf16[256,2048]{1,0:T(8,128)(2,1)} collective-permute-done((bf16[256,2048]{1,0:T(8,128)(2,1)}, bf16[256,2048]{1,0:T(8,128)(2,1)}, u32[]{:S(2)}, u32[]{:S(2)}) %collective-permute-start.54) | collective-permute-done | bytes 1048608 | tf_op jit(solution)/shard_map/ppermute | solution.py:39
  606.5 19.9 %collective-permute-done.56 = bf16[256,2048]{1,0:T(8,128)(2,1)S(1)} collective-permute-done((bf16[256,2048]{1,0:T(8,128)(2,1)S(1)}, bf16[256,2048]{1,0:T(8,128)(2,1)S(1)}, u32[]{:S(2)}, u32[]{:S(2)}) %collective-permute-start.56) | collective-permute-done | bytes 1048608 | tf_op jit(solution)/shard_map/ppermute | solution.py:39
  642.3 5.0 part_columns.2
  657.4 14.7 %all-to-all-done.5 = bf16[8,64,1024]{2,1,0:T(8,128)(2,1)S(1)} async-done(((bf16[8,64,1024]{2,1,0:T(8,128)(2,1)}), bf16[8,64,1024]{2,1,0:T(8,128)(2,1)S(1)}, u32[]{:S(2)}, u32[]{:S(2)}) %all-to-all-start.5) | async-done | bytes 1048608 | tf_op jit(solution)/shard_map/all_to_all | solution.py:154
  (356 shorter events, 196.5 us)
Async XLA Ops:
  7.2 33.1 %all-gather.5.cloned.1.call-start = ((), (), s32[]{:S(2)}) async-start(), calls=%async_computation.9 | async-start | bytes 1310720 | tf_op jit(solution)/shard_map/all_gather | solution.py:141
  19.2 127.0 %all-gather.7.cloned.1.call-start = ((), (), s32[]{:S(2)}) async-start(), calls=%async_computation.10 | async-start | bytes 3932160 | tf_op jit(solution)/shard_map/all_gather | solution.py:141
  40.3 254.9 %all-gather.9.cloned.1.call-start = ((), (), s32[]{:S(2)}) async-start(), calls=%async_computation.11 | async-start | bytes 10485760 | tf_op jit(solution)/shard_map/all_gather | solution.py:141
  115.7 24.5 %collective-permute-start.5 = (bf16[256,2048]{1,0:T(8,128)(2,1)S(1)}, bf16[256,2048]{1,0:T(8,128)(2,1)S(1)}, u32[]{:S(2)}, u32[]{:S(2)}) collective-permute-start(bf16[256,2048]{1,0:T(8,128)(2,1)S(1)} %collective-permute-done.1.refs_2_), channel_id=1, source_target_pairs={{0,4},{1,3},{2,6},{3,1},{4,0},{5,7},{6,2},{7,5},{8,12},{9,11},{10,... | collective-permute-start | bytes 3145736 | tf_op jit(solution)/shard_map/ppermute | solution.py:39
  116.8 24.6 %collective-permute-start.10 = (bf16[256,2048]{1,0:T(8,128)(2,1)S(1)}, bf16[256,2048]{1,0:T(8,128)(2,1)}, u32[]{:S(2)}, u32[]{:S(2)}) collective-permute-start(bf16[256,2048]{1,0:T(8,128)(2,1)S(1)} %bitcast.86), channel_id=1, source_target_pairs={{0,1},{1,0},{2,3},{3,2},{4,5},{5,4},{6,7},{7,6},{8,9},{9,8},{10,11... | collective-permute-start | bytes 3145736 | tf_op jit(solution)/shard_map/ppermute | solution.py:39
  116.8 25.9 %collective-permute-start.3 = (bf16[256,2048]{1,0:T(8,128)(2,1)S(1)}, bf16[256,2048]{1,0:T(8,128)(2,1)S(1)}, u32[]{:S(2)}, u32[]{:S(2)}) collective-permute-start(bf16[256,2048]{1,0:T(8,128)(2,1)S(1)} %collective-permute-done.1.refs_2_), channel_id=1, source_target_pairs={{0,1},{1,0},{2,3},{3,2},{4,5},{5,4},{6,7},{7,6},{8,9},{9,8},{10,11... | collective-permute-start | bytes 3145736 | tf_op jit(solution)/shard_map/ppermute | solution.py:39
  140.7 40.2 %collective-permute-start.11 = (bf16[256,2048]{1,0:T(8,128)(2,1)S(1)}, bf16[256,2048]{1,0:T(8,128)(2,1)}, u32[]{:S(2)}, u32[]{:S(2)}) collective-permute-start(bf16[256,2048]{1,0:T(8,128)(2,1)S(1)} %bitcast.87), channel_id=1, source_target_pairs={{0,2},{1,5},{2,0},{3,7},{4,6},{5,1},{6,4},{7,3},{8,10},{9,13},{10,... | collective-permute-start | bytes 3145736 | tf_op jit(solution)/shard_map/ppermute | solution.py:39
  141.4 39.5 %collective-permute-start.12 = (bf16[256,2048]{1,0:T(8,128)(2,1)}, bf16[256,2048]{1,0:T(8,128)(2,1)}, u32[]{:S(2)}, u32[]{:S(2)}) collective-permute-start(bf16[256,2048]{1,0:T(8,128)(2,1)} %collective-permute-done.10.refs_1_), channel_id=1, source_target_pairs={{0,2},{1,5},{2,0},{3,7},{4,6},{5,1},{6,4},{7,3},{8,10},{9,13},{10,... | collective-permute-start | bytes 3145736 | tf_op jit(solution)/shard_map/ppermute | solution.py:39
  191.5 26.4 %collective-permute-start.18 = (bf16[256,2048]{1,0:T(8,128)(2,1)}, bf16[256,2048]{1,0:T(8,128)(2,1)}, u32[]{:S(2)}, u32[]{:S(2)}) collective-permute-start(bf16[256,2048]{1,0:T(8,128)(2,1)} %add_convert_fusion.11), channel_id=1, source_target_pairs={{0,2},{1,5},{2,0},{3,7},{4,6},{5,1},{6,4},{7,3},{8,10},{9,13},{10,... | collective-permute-start | bytes 3145736 | tf_op jit(solution)/shard_map/ppermute | solution.py:39
  193.4 36.8 %all-to-all-start.2 = ((bf16[64,8,1024]{2,0,1:T(8,128)(2,1)}), bf16[64,8,1024]{2,0,1:T(8,128)(2,1)}, u32[]{:S(2)}, u32[]{:S(2)}) async-start(bf16[64,8,1024]{2,0,1:T(8,128)(2,1)} %bitcast.95), calls=%async_computation.2 | async-start | bytes 2097152 | tf_op jit(solution)/shard_map/all_to_all | solution.py:138
  197.7 140.5 %all-gather.11.cloned.1.call-start = ((), (), s32[]{:S(2)}) async-start(), calls=%async_computation.12 | async-start | bytes 5242880 | tf_op jit(solution)/shard_map/all_gather | solution.py:141
  197.7 47.1 %collective-permute-start.22 = (bf16[256,2048]{1,0:T(8,128)(2,1)}, bf16[256,2048]{1,0:T(8,128)(2,1)}, u32[]{:S(2)}, u32[]{:S(2)}) collective-permute-start(bf16[256,2048]{1,0:T(8,128)(2,1)} %collective-permute-done.11.refs_2_), channel_id=1, source_target_pairs={{0,4},{1,3},{2,6},{3,1},{4,0},{5,7},{6,2},{7,5},{8,12},{9,11},{10,... | collective-permute-start | bytes 3145736 | tf_op jit(solution)/shard_map/ppermute | solution.py:39
  215.1 31.8 %collective-permute-start.17 = (bf16[256,2048]{1,0:T(8,128)(2,1)}, bf16[256,2048]{1,0:T(8,128)(2,1)}, u32[]{:S(2)}, u32[]{:S(2)}) collective-permute-start(bf16[256,2048]{1,0:T(8,128)(2,1)} %add_convert_fusion.12), channel_id=1, source_target_pairs={{0,2},{1,5},{2,0},{3,7},{4,6},{5,1},{6,4},{7,3},{8,10},{9,13},{10,... | collective-permute-start | bytes 3145736 | tf_op jit(solution)/shard_map/ppermute | solution.py:39
  220.4 26.6 %collective-permute-start.19 = (bf16[256,2048]{1,0:T(8,128)(2,1)}, bf16[256,2048]{1,0:T(8,128)(2,1)}, u32[]{:S(2)}, u32[]{:S(2)}) collective-permute-start(bf16[256,2048]{1,0:T(8,128)(2,1)} %add_convert_fusion.10), channel_id=1, source_target_pairs={{0,1},{1,0},{2,3},{3,2},{4,5},{5,4},{6,7},{7,6},{8,9},{9,8},{10,11... | collective-permute-start | bytes 3145736 | tf_op jit(solution)/shard_map/ppermute | solution.py:39
  230.2 192.6 %reduce-scatter.4.cloned.1.call-start = ((), (), s32[]{:S(2)}) async-start(), calls=%async_computation.13 | async-start | bytes 5242880 | tf_op jit(solution)/shard_map/reduce_scatter | solution.py:151
  265.2 25.6 %collective-permute-start.29 = (bf16[256,2048]{1,0:T(8,128)(2,1)S(1)}, bf16[256,2048]{1,0:T(8,128)(2,1)S(1)}, u32[]{:S(2)}, u32[]{:S(2)}) collective-permute-start(bf16[256,2048]{1,0:T(8,128)(2,1)S(1)} %collective-permute-done.25.refs_2_), channel_id=1, source_target_pairs={{0,4},{1,3},{2,6},{3,1},{4,0},{5,7},{6,2},{7,5},{8,12},{9,11},{10,... | collective-permute-start | bytes 3145736 | tf_op jit(solution)/shard_map/ppermute | solution.py:39
  265.6 25.2 %collective-permute-start.26 = (bf16[256,2048]{1,0:T(8,128)(2,1)S(1)}, bf16[256,2048]{1,0:T(8,128)(2,1)S(1)}, u32[]{:S(2)}, u32[]{:S(2)}) collective-permute-start(bf16[256,2048]{1,0:T(8,128)(2,1)S(1)} %collective-permute-done.24.refs_1_), channel_id=1, source_target_pairs={{0,2},{1,5},{2,0},{3,7},{4,6},{5,1},{6,4},{7,3},{8,10},{9,13},{10,... | collective-permute-start | bytes 3145736 | tf_op jit(solution)/shard_map/ppermute | solution.py:39
  266.5 24.8 %collective-permute-start.27 = (bf16[256,2048]{1,0:T(8,128)(2,1)S(1)}, bf16[256,2048]{1,0:T(8,128)(2,1)S(1)}, u32[]{:S(2)}, u32[]{:S(2)}) collective-permute-start(bf16[256,2048]{1,0:T(8,128)(2,1)S(1)} %collective-permute-done.25.refs_2_), channel_id=1, source_target_pairs={{0,1},{1,0},{2,3},{3,2},{4,5},{5,4},{6,7},{7,6},{8,9},{9,8},{10,11... | collective-permute-start | bytes 3145736 | tf_op jit(solution)/shard_map/ppermute | solution.py:39
  337.7 228.7 %reduce-scatter.6.cloned.1.call-start = ((), (), s32[]{:S(2)}) async-start(), calls=%async_computation.14 | async-start | bytes 10485760 | tf_op jit(solution)/shard_map/reduce_scatter | solution.py:151
  385.6 37.2 %collective-permute-start.36 = (bf16[256,2048]{1,0:T(8,128)(2,1)}, bf16[256,2048]{1,0:T(8,128)(2,1)}, u32[]{:S(2)}, u32[]{:S(2)}) collective-permute-start(bf16[256,2048]{1,0:T(8,128)(2,1)} %add_convert_fusion.8), channel_id=1, source_target_pairs={{0,2},{1,5},{2,0},{3,7},{4,6},{5,1},{6,4},{7,3},{8,10},{9,13},{10,... | collective-permute-start | bytes 3145736 | tf_op jit(solution)/shard_map/ppermute | solution.py:39
  396.9 25.9 %collective-permute-start.35 = (bf16[256,2048]{1,0:T(8,128)(2,1)}, bf16[256,2048]{1,0:T(8,128)(2,1)S(1)}, u32[]{:S(2)}, u32[]{:S(2)}) collective-permute-start(bf16[256,2048]{1,0:T(8,128)(2,1)} %add_convert_fusion.9), channel_id=1, source_target_pairs={{0,2},{1,5},{2,0},{3,7},{4,6},{5,1},{6,4},{7,3},{8,10},{9,13},{10,... | collective-permute-start | bytes 3145736 | tf_op jit(solution)/shard_map/ppermute | solution.py:39
  422.9 230.2 %reduce-scatter.8.cloned.1.call-start = ((), (), s32[]{:S(2)}) async-start(), calls=%async_computation.15 | async-start | bytes 5242880 | tf_op jit(solution)/shard_map/reduce_scatter | solution.py:151
  445.9 25.7 %collective-permute-start.47 = (bf16[256,2048]{1,0:T(8,128)(2,1)S(1)}, bf16[256,2048]{1,0:T(8,128)(2,1)}, u32[]{:S(2)}, u32[]{:S(2)}) collective-permute-start(bf16[256,2048]{1,0:T(8,128)(2,1)S(1)} %collective-permute-done.43.refs_2_.refs_10_), channel_id=1, source_target_pairs={{0,4},{1,3},{2,6},{3,1},{4,0},{5,7},{6,2},{7,5},{8,12},{9,11},{10,... | collective-permute-start | bytes 3145736 | tf_op jit(solution)/shard_map/ppermute | solution.py:39
  447.4 26.4 %collective-permute-start.44 = (bf16[256,2048]{1,0:T(8,128)(2,1)}, bf16[256,2048]{1,0:T(8,128)(2,1)}, u32[]{:S(2)}, u32[]{:S(2)}) collective-permute-start(bf16[256,2048]{1,0:T(8,128)(2,1)} %collective-permute-done.42.refs_1_.refs_9_), channel_id=1, source_target_pairs={{0,2},{1,5},{2,0},{3,7},{4,6},{5,1},{6,4},{7,3},{8,10},{9,13},{10,... | collective-permute-start | bytes 3145736 | tf_op jit(solution)/shard_map/ppermute | solution.py:39
  448.8 26.4 %collective-permute-start.39 = (bf16[256,2048]{1,0:T(8,128)(2,1)S(1)}, bf16[256,2048]{1,0:T(8,128)(2,1)S(1)}, u32[]{:S(2)}, u32[]{:S(2)}) collective-permute-start(bf16[256,2048]{1,0:T(8,128)(2,1)S(1)} %get-tuple-element.177), channel_id=1, source_target_pairs={{0,1},{1,0},{2,3},{3,2},{4,5},{5,4},{6,7},{7,6},{8,9},{9,8},{10,11... | collective-permute-start | bytes 3145736 | tf_op jit(solution)/shard_map/ppermute | solution.py:39
  449.1 33.6 %collective-permute-start.40 = (bf16[256,2048]{1,0:T(8,128)(2,1)S(1)}, bf16[256,2048]{1,0:T(8,128)(2,1)S(1)}, u32[]{:S(2)}, u32[]{:S(2)}) collective-permute-start(bf16[256,2048]{1,0:T(8,128)(2,1)S(1)} %convert_add_fusion.3), channel_id=1, source_target_pairs={{0,4},{1,3},{2,6},{3,1},{4,0},{5,7},{6,2},{7,5},{8,12},{9,11},{10,... | collective-permute-start | bytes 3145736 | tf_op jit(solution)/shard_map/ppermute | solution.py:39
  455.9 28.2 %collective-permute-start.45 = (bf16[256,2048]{1,0:T(8,128)(2,1)S(1)}, bf16[256,2048]{1,0:T(8,128)(2,1)S(1)}, u32[]{:S(2)}, u32[]{:S(2)}) collective-permute-start(bf16[256,2048]{1,0:T(8,128)(2,1)S(1)} %collective-permute-done.43.refs_2_.refs_10_), channel_id=1, source_target_pairs={{0,1},{1,0},{2,3},{3,2},{4,5},{5,4},{6,7},{7,6},{8,9},{9,8},{10,11... | collective-permute-start | bytes 3145736 | tf_op jit(solution)/shard_map/ppermute | solution.py:39
  568.0 35.9 %collective-permute-start.54 = (bf16[256,2048]{1,0:T(8,128)(2,1)}, bf16[256,2048]{1,0:T(8,128)(2,1)}, u32[]{:S(2)}, u32[]{:S(2)}) collective-permute-start(bf16[256,2048]{1,0:T(8,128)(2,1)} %add_convert_fusion.5), channel_id=1, source_target_pairs={{0,2},{1,5},{2,0},{3,7},{4,6},{5,1},{6,4},{7,3},{8,10},{9,13},{10,... | collective-permute-start | bytes 3145736 | tf_op jit(solution)/shard_map/ppermute | solution.py:39
  568.5 58.8 %all-to-all-start.3 = ((bf16[8,64,2048]{2,1,0:T(8,128)(2,1)}), bf16[8,64,2048]{2,1,0:T(8,128)(2,1)}, u32[]{:S(2)}, u32[]{:S(2)}) async-start(bf16[8,64,2048]{2,1,0:T(8,128)(2,1)} %bitcast.99), calls=%async_computation.6 | async-start | bytes 4194304 | tf_op jit(solution)/shard_map/all_to_all | solution.py:154
  588.2 38.2 %collective-permute-start.56 = (bf16[256,2048]{1,0:T(8,128)(2,1)S(1)}, bf16[256,2048]{1,0:T(8,128)(2,1)S(1)}, u32[]{:S(2)}, u32[]{:S(2)}) collective-permute-start(bf16[256,2048]{1,0:T(8,128)(2,1)S(1)} %copy-done.62), channel_id=1, source_target_pairs={{0,2},{1,5},{2,0},{3,7},{4,6},{5,1},{6,4},{7,3},{8,10},{9,13},{10,... | collective-permute-start | bytes 3145736 | tf_op jit(solution)/shard_map/ppermute | solution.py:39
  590.8 48.3 %collective-permute-start.53 = (bf16[256,2048]{1,0:T(8,128)(2,1)}, bf16[256,2048]{1,0:T(8,128)(2,1)}, u32[]{:S(2)}, u32[]{:S(2)}) collective-permute-start(bf16[256,2048]{1,0:T(8,128)(2,1)} %add_convert_fusion.6), channel_id=1, source_target_pairs={{0,2},{1,5},{2,0},{3,7},{4,6},{5,1},{6,4},{7,3},{8,10},{9,13},{10,... | collective-permute-start | bytes 3145736 | tf_op jit(solution)/shard_map/ppermute | solution.py:39
  606.4 32.6 %collective-permute-start.55 = (bf16[256,2048]{1,0:T(8,128)(2,1)}, bf16[256,2048]{1,0:T(8,128)(2,1)}, u32[]{:S(2)}, u32[]{:S(2)}) collective-permute-start(bf16[256,2048]{1,0:T(8,128)(2,1)} %add_convert_fusion.2), channel_id=1, source_target_pairs={{0,1},{1,0},{2,3},{3,2},{4,5},{5,4},{6,7},{7,6},{8,9},{9,8},{10,11... | collective-permute-start | bytes 3145736 | tf_op jit(solution)/shard_map/ppermute | solution.py:39
  (114 other events, 1664.0 us)
Sparse Core Ops, SparseCore 0:
  9.6 30.6 all-gather.4
  42.4 62.9 all-gather.6
  107.0 148.2 all-gather.8
  256.7 78.9 all-gather.10
  337.9 75.2 reduce-scatter.3
  423.0 143.3 reduce-scatter.5
  568.8 77.4 reduce-scatter.7

commit v7 on v6

--- a/solution.py
+++ b/solution.py
@@ -728,7 +728,7 @@
     gate_up_back = MLP.return_columns(gate_up_grad)
     down_w = jnp.transpose(MLP.return_columns(after(down_grad, gate_up_back)).astype(F32))
     gate_w, up_w, gain_mlp = part_columns(gate_up_back, [w_gate, w_up], gain_two, UNIT)
-    attn_grad = after(attn_grad, tokens_grad, block_out, down_w, gate_w)
+    attn_grad = after(attn_grad, tokens_grad, block_out, gate_w)
     query_w, key_w, value_w, out_w, gain_attn = part_columns(
         ATTN.return_columns(attn_grad), [w_query, w_key, w_value], gain_one, LANES, w_out.shape[0]
     )

time: 693 us -> 689 us (level)
  no operation moved by 1% of the time
where the time goes in v7:
time: 689 us; the launch traced here: 682 us
  Pallas kernels  246 us (36%)
  waiting for transfers between devices  235 us (34%)
  starting transfers between devices  57.2 us (8%)
  other arithmetic  48.8 us (7%)
  blocking collectives  41.3 us (6%)
  local copies, waits for them, and re-layouts  38 us (6%)
  between operations  15.4 us (2%)
    ppermute x56, waiting for transfers between devices, flip(): return lax.ppermute(x, axes, [(i, i ^ masks[i & 1]) for i in range(8)])  193 us
    pallas_call x16, Pallas kernels, rows_product(): pl.pallas_call(body, grid=(count * inner,), out_shape=[jax.ShapeDtypeStru...  59.9 us
    all_to_all x1, blocking collectives, share_columns(): lax.all_to_all(weight, self.axes, split_axis=1, concat_axis=0, tiled=True)  41.3 us
    pallas_call x2, Pallas kernels, parts_product(): pl.pallas_call(body, grid=(model // step,), out_shape=jax.ShapeDtypeStruc...  37.8 us
    pallas_call x1, Pallas kernels, attend_back(): pl.pallas_call(functools.partial(attend_back_body, blocks=length // size,...  35.9 us
    pallas_call x1, Pallas kernels, attend(): pl.pallas_call(functools.partial(attend_body, blocks=length // size, size...  34.8 us
    ppermute x56, starting transfers between devices, flip(): return lax.ppermute(x, axes, [(i, i ^ masks[i & 1]) for i in range(8)])  31 us
    pallas_call x1, Pallas kernels, feed_forward(): pl.pallas_call(body, grid=(width // (2 * UNIT),), out_shape=[jax.ShapeDty...  29.1 us
  transfers between devices with their start and end apart: 71, of which 26 were waited for; matrix products, arithmetic and copies ran while one was open for 9% of the time, Pallas kernels for 36%

profile of v7, /device:TPU:0, one launch (start us, length us, event | category | flops | bytes accessed | tf_op | source)
XLA Modules:
  0.0 681.7 jit_solution(8495425469550506007)
XLA Ops:
  14.2 5.0 all-to-all-start.1
  22.2 8.7 %collective-permute-done.8 = s32[512,1]{0,1:T(1,128)S(1)} collective-permute-done((s32[512,1]{0,1:T(1,128)S(1)}, s32[512,1]{0,1:T(1,128)S(1)}, u32[]{:S(2)}, u32[]{:S(2)}) %collective-permute-start.8) | collective-permute-done | bytes 2080 | tf_op jit(solution)/shard_map/ppermute | solution.py:43
  34.4 5.8 all-gather.5.cloned.1.call-done
  56.3 41.3 %all_to_all.108 = bf16[64,8,3072]{2,0,1:T(8,128)(2,1)S(1)} all-to-all(bf16[64,8,3072]{2,0,1:T(8,128)(2,1)S(1)} %bitcast.92), channel_id=1, replica_groups=mesh['r'=1,'zh'=2,'zl'=2,'y'=2,'x'=2,'c'=2] {'y','x','c'}, dimensions={1} | all-to-all | bytes 6291456 | tf_op jit(solution)/shard_map/all_to_all | solution.py:138
  101.4 14.2 %collective-permute-done.1.refs_2_ = bf16[256,2048]{1,0:T(8,128)(2,1)S(1)} collective-permute-done((bf16[256,2048]{1,0:T(8,128)(2,1)S(1)}, bf16[256,2048]{1,0:T(8,128)(2,1)S(1)}, u32[]{:S(2)}, u32[]{:S(2)}) %collective-permute-start.1) | collective-permute-done | bytes 1048608 | tf_op jit(solution)/shard_map/ppermute | solution.py:39
  117.3 22.9 %collective-permute-done.5.refs_6_ = bf16[256,2048]{1,0:T(8,128)(2,1)S(1)} collective-permute-done((bf16[256,2048]{1,0:T(8,128)(2,1)S(1)}, bf16[256,2048]{1,0:T(8,128)(2,1)S(1)}, u32[]{:S(2)}, u32[]{:S(2)}) %collective-permute-start.5) | collective-permute-done | bytes 1048608 | tf_op jit(solution)/shard_map/ppermute | solution.py:39
  146.2 34.8 %attend.1 = (bf16[2048,768]{1,0:T(8,128)(2,1)}, bf16[2048,256]{1,0:T(8,128)(2,1)}, f32[2048,256]{1,0:T(8,128)}) custom-call(s32[16]{0:T(128)} %concatenate.62.place_ref, bf16[256,2048]{1,0:T(8,128)(2,1)} %copy-done.12, bf16[256,2048]{1,0:T(8,128)(2,1)} %copy-done.30, bf16[256,2048]{1,0:T(8,128)(2,1)} %copy-done.28, bf16[256,2048]{1,0:T(8,128)(2,1)} %copy-done.32, ...), custom_call_target="tpu_custom_call" | custom-call | flops 1024 | bytes 1024 | tf_op jit(solution)/shard_map/attend/pallas_call | solution.py:574
  201.3 10.8 %collective-permute-done.15 = bf16[256,2048]{1,0:T(8,128)(2,1)} collective-permute-done((bf16[256,2048]{1,0:T(8,128)(2,1)}, bf16[256,2048]{1,0:T(8,128)(2,1)}, u32[]{:S(2)}, u32[]{:S(2)}) %collective-permute-start.15) | collective-permute-done | bytes 1048608 | tf_op jit(solution)/shard_map/ppermute | solution.py:39
  222.5 7.7 %all-to-all-done.2 = bf16[64,8,1024]{2,0,1:T(8,128)(2,1)} async-done(((bf16[64,8,1024]{2,0,1:T(8,128)(2,1)}), bf16[64,8,1024]{2,0,1:T(8,128)(2,1)}, u32[]{:S(2)}, u32[]{:S(2)}) %all-to-all-start.2) | async-done | bytes 1048608 | tf_op jit(solution)/shard_map/all_to_all | solution.py:138
  230.9 14.0 %collective-permute-done.22.refs_6_ = bf16[256,2048]{1,0:T(8,128)(2,1)} collective-permute-done((bf16[256,2048]{1,0:T(8,128)(2,1)}, bf16[256,2048]{1,0:T(8,128)(2,1)}, u32[]{:S(2)}, u32[]{:S(2)}) %collective-permute-start.22) | collective-permute-done | bytes 1048608 | tf_op jit(solution)/shard_map/ppermute | solution.py:39
  251.5 13.7 %collective-permute-done.25.refs_2_ = bf16[256,2048]{1,0:T(8,128)(2,1)S(1)} collective-permute-done((bf16[256,2048]{1,0:T(8,128)(2,1)S(1)}, bf16[256,2048]{1,0:T(8,128)(2,1)S(1)}, u32[]{:S(2)}, u32[]{:S(2)}) %collective-permute-start.25) | collective-permute-done | bytes 1048608 | tf_op jit(solution)/shard_map/ppermute | solution.py:39
  266.5 24.3 %collective-permute-done.29.refs_6_ = bf16[256,2048]{1,0:T(8,128)(2,1)S(1)} collective-permute-done((bf16[256,2048]{1,0:T(8,128)(2,1)S(1)}, bf16[256,2048]{1,0:T(8,128)(2,1)S(1)}, u32[]{:S(2)}, u32[]{:S(2)}) %collective-permute-start.29) | collective-permute-done | bytes 1048608 | tf_op jit(solution)/shard_map/ppermute | solution.py:39
  295.2 29.1 %feed_forward.1 = (bf16[2048,1024]{1,0:T(8,128)(2,1)}, f32[2048,2048]{1,0:T(8,128)}) custom-call(bf16[256,2048]{1,0:T(8,128)(2,1)} %copy-done.10, bf16[256,2048]{1,0:T(8,128)(2,1)} %copy-done.38, bf16[256,2048]{1,0:T(8,128)(2,1)} %copy-done.36, bf16[256,2048]{1,0:T(8,128)(2,1)} %copy-done.40, bf16[256,2048]{1,0:T(8,128)(2,1)} %copy-done.42, ...), custom_call_target="tpu_custom_call" | custom-call | flops 1024 | bytes 1024 | tf_op jit(solution)/shard_map/feed_forward/pallas_call | solution.py:382
  324.3 13.3 %parts_product.2 = bf16[2048,1024]{1,0:T(8,128)(2,1)} custom-call(bf16[256,2048]{1,0:T(8,128)(2,1)S(1)} %bitcast.88, bf16[256,2048]{1,0:T(8,128)(2,1)} %collective-permute-done.10.refs_1_, bf16[256,2048]{1,0:T(8,128)(2,1)} %collective-permute-done.11.refs_2_, bf16[256,2048]{1,0:T(8,128)(2,1)} %collective-permute-done.12.refs_3_, ...), custom_call_target="tpu_custom_call" | custom-call | flops 13182098432 | bytes 35951176 | tf_op jit(solution)/shard_map/parts_product/pallas_call | solution.py:294
  338.2 19.7 %feed_back.1.array_ref.refs_8_ = bf16[2048,2048]{1,0:T(8,128)(2,1)} custom-call(bf16[256,2048]{1,0:T(8,128)(2,1)} %bitcast.85, bf16[256,2048]{1,0:T(8,128)(2,1)} %collective-permute-done.10.refs_1_, bf16[256,2048]{1,0:T(8,128)(2,1)} %collective-permute-done.11.refs_2_, bf16[256,2048]{1,0:T(8,128)(2,1)} %collective-permute-done.12.refs_3_, ...), custom_call_target="tpu_custom_call" | custom-call | flops 1024 | bytes 1024 | tf_op jit(solution)/shard_map/feed_back/pallas_call | solution.py:416
  361.2 7.3 %rows_product.20 = (f32[256,2048]{1,0:T(8,128)S(1)}, bf16[256,2048]{1,0:T(8,128)(2,1)S(1)}) custom-call(bf16[2048,2048]{1,0:T(8,128)(2,1)S(1)} %copy-done, bf16[2048,2048]{1,0:T(8,128)(2,1)} %all-gather.9.cloned.1.call-done.refs_8_.refs_0_), custom_call_target="tpu_custom_call" | custom-call | flops 1024 | bytes 1024 | tf_op jit(solution)/shard_map/rows_product/pallas_call | solution.py:264
  368.6 7.3 %rows_product.23 = (bf16[256,2048]{1,0:T(8,128)(2,1)S(1)}, bf16[256,2048]{1,0:T(8,128)(2,1)S(1)}) custom-call(bf16[2048,2048]{1,0:T(8,128)(2,1)S(1)} %copy-done, bf16[2048,2048]{1,0:T(8,128)(2,1)} %all-gather.9.cloned.1.call-done.refs_8_.refs_0_), custom_call_target="tpu_custom_call" | custom-call | flops 1024 | bytes 1024 | tf_op jit(solution)/shard_map/rows_product/pallas_call | solution.py:264
  376.9 7.4 %rows_product.22 = (f32[256,2048]{1,0:T(8,128)S(1)}, f32[256,2048]{1,0:T(8,128)S(1)}) custom-call(bf16[2048,2048]{1,0:T(8,128)(2,1)S(1)} %copy-done, bf16[2048,2048]{1,0:T(8,128)(2,1)} %all-gather.9.cloned.1.call-done.refs_8_.refs_0_), custom_call_target="tpu_custom_call" | custom-call | flops 1024 | bytes 1024 | tf_op jit(solution)/shard_map/rows_product/pallas_call | solution.py:264
  386.7 7.3 %rows_product.21 = (f32[256,2048]{1,0:T(8,128)S(1)}, f32[256,2048]{1,0:T(8,128)S(1)}) custom-call(bf16[2048,2048]{1,0:T(8,128)(2,1)S(1)} %copy-done, bf16[2048,2048]{1,0:T(8,128)(2,1)} %all-gather.9.cloned.1.call-done.refs_8_.refs_0_), custom_call_target="tpu_custom_call" | custom-call | flops 1024 | bytes 1024 | tf_op jit(solution)/shard_map/rows_product/pallas_call | solution.py:264
  398.3 24.5 %parts_product.3 = bf16[2048,2048]{1,0:T(8,128)(2,1)} custom-call(bf16[256,2048]{1,0:T(8,128)(2,1)S(1)} %copy-done.11, bf16[256,2048]{1,0:T(8,128)(2,1)S(1)} %copy-done.39, bf16[256,2048]{1,0:T(8,128)(2,1)S(1)} %copy-done.37, bf16[256,2048]{1,0:T(8,128)(2,1)S(1)} %copy-done.41, bf16[256,2048]{1,0:T(8,128)(2,1)S(1)} %copy-done.43, ...), custom_call_target="tpu_custom_call" | custom-call | flops 26364196864 | bytes 71902352 | tf_op jit(solution)/shard_map/parts_product/pallas_call | solution.py:294
  440.5 5.3 collective-permute-done.43.refs_2_.refs_10_
  456.8 14.7 %collective-permute-done.47.refs_6_.refs_14_ = bf16[256,2048]{1,0:T(8,128)(2,1)} collective-permute-done((bf16[256,2048]{1,0:T(8,128)(2,1)S(1)}, bf16[256,2048]{1,0:T(8,128)(2,1)}, u32[]{:S(2)}, u32[]{:S(2)}) %collective-permute-start.47) | collective-permute-done | bytes 1048608 | tf_op jit(solution)/shard_map/ppermute | solution.py:39
  475.2 7.5 %collective-permute-done.40 = bf16[256,2048]{1,0:T(8,128)(2,1)S(1)} collective-permute-done((bf16[256,2048]{1,0:T(8,128)(2,1)S(1)}, bf16[256,2048]{1,0:T(8,128)(2,1)S(1)}, u32[]{:S(2)}, u32[]{:S(2)}) %collective-permute-start.40) | collective-permute-done | bytes 1048608 | tf_op jit(solution)/shard_map/ppermute | solution.py:39
  485.9 35.9 %attend_back.1.refs_16_.array_ref = bf16[2048,768]{1,0:T(8,128)(2,1)} custom-call(s32[16]{0:T(128)} %concatenate.62.place_ref, bf16[256,2048]{1,0:T(8,128)(2,1)} %copy-done.65, bf16[256,2048]{1,0:T(8,128)(2,1)} %collective-permute-done.42.refs_1_.refs_9_, bf16[256,2048]{1,0:T(8,128)(2,1)} %copy-done.70, ...), custom_call_target="tpu_custom_call" | custom-call | flops 39600001024 | bytes 108000000 | tf_op jit(solution)/shard_map/attend_back/pallas_call | solution.py:598
  523.0 14.4 %attention_terms.1 = bf16[2048,1024]{1,0:T(8,128)(2,1)} custom-call(bf16[256,2048]{1,0:T(8,128)(2,1)S(1)} %copy-done.13, bf16[256,2048]{1,0:T(8,128)(2,1)S(1)} %copy-done.31, bf16[256,2048]{1,0:T(8,128)(2,1)S(1)} %copy-done.29, bf16[256,2048]{1,0:T(8,128)(2,1)S(1)} %copy-done.33, bf16[256,2048]{1,0:T(8,128)(2,1)S(1)} %copy-done.35, ...), custom_call_target="tpu_custom_call" | custom-call | flops 15399999488 | bytes 42000000 | tf_op jit(solution)/shard_map/attention_terms/pallas_call | solution.py:322
  555.1 5.5 collective-permute-done.51
  568.5 4.5 all-to-all-start.3
  573.0 13.5 %collective-permute-done.57 = bf16[256,2048]{1,0:T(8,128)(2,1)} collective-permute-done((bf16[256,2048]{1,0:T(8,128)(2,1)S(1)}, bf16[256,2048]{1,0:T(8,128)(2,1)}, u32[]{:S(2)}, u32[]{:S(2)}) %collective-permute-start.57) | collective-permute-done | bytes 1048608 | tf_op jit(solution)/shard_map/ppermute | solution.py:39
  590.9 13.0 %collective-permute-done.54 = bf16[256,2048]{1,0:T(8,128)(2,1)} collective-permute-done((bf16[256,2048]{1,0:T(8,128)(2,1)}, bf16[256,2048]{1,0:T(8,128)(2,1)}, u32[]{:S(2)}, u32[]{:S(2)}) %collective-permute-start.54) | collective-permute-done | bytes 1048608 | tf_op jit(solution)/shard_map/ppermute | solution.py:39
  606.5 19.9 %collective-permute-done.56 = bf16[256,2048]{1,0:T(8,128)(2,1)S(1)} collective-permute-done((bf16[256,2048]{1,0:T(8,128)(2,1)S(1)}, bf16[256,2048]{1,0:T(8,128)(2,1)S(1)}, u32[]{:S(2)}, u32[]{:S(2)}) %collective-permute-start.56) | collective-permute-done | bytes 1048608 | tf_op jit(solution)/shard_map/ppermute | solution.py:39
  642.3 5.0 part_columns.2
  657.3 11.8 %all-to-all-done.4 = bf16[8,64,1024]{2,1,0:T(8,128)(2,1)S(1)} async-done(((bf16[8,64,1024]{2,1,0:T(8,128)(2,1)}), bf16[8,64,1024]{2,1,0:T(8,128)(2,1)S(1)}, u32[]{:S(2)}, u32[]{:S(2)}) %all-to-all-start.4) | async-done | bytes 1048608 | tf_op jit(solution)/shard_map/all_to_all | solution.py:154
  (356 shorter events, 196.3 us)
Async XLA Ops:
  7.2 33.1 %all-gather.5.cloned.1.call-start = ((), (), s32[]{:S(2)}) async-start(), calls=%async_computation.9 | async-start | bytes 1310720 | tf_op jit(solution)/shard_map/all_gather | solution.py:141
  19.2 127.0 %all-gather.7.cloned.1.call-start = ((), (), s32[]{:S(2)}) async-start(), calls=%async_computation.10 | async-start | bytes 3932160 | tf_op jit(solution)/shard_map/all_gather | solution.py:141
  40.3 254.9 %all-gather.9.cloned.1.call-start = ((), (), s32[]{:S(2)}) async-start(), calls=%async_computation.11 | async-start | bytes 10485760 | tf_op jit(solution)/shard_map/all_gather | solution.py:141
  115.7 24.5 %collective-permute-start.5 = (bf16[256,2048]{1,0:T(8,128)(2,1)S(1)}, bf16[256,2048]{1,0:T(8,128)(2,1)S(1)}, u32[]{:S(2)}, u32[]{:S(2)}) collective-permute-start(bf16[256,2048]{1,0:T(8,128)(2,1)S(1)} %collective-permute-done.1.refs_2_), channel_id=1, source_target_pairs={{0,4},{1,3},{2,6},{3,1},{4,0},{5,7},{6,2},{7,5},{8,12},{9,11},{10,... | collective-permute-start | bytes 3145736 | tf_op jit(solution)/shard_map/ppermute | solution.py:39
  116.8 24.6 %collective-permute-start.10 = (bf16[256,2048]{1,0:T(8,128)(2,1)S(1)}, bf16[256,2048]{1,0:T(8,128)(2,1)}, u32[]{:S(2)}, u32[]{:S(2)}) collective-permute-start(bf16[256,2048]{1,0:T(8,128)(2,1)S(1)} %bitcast.86), channel_id=1, source_target_pairs={{0,1},{1,0},{2,3},{3,2},{4,5},{5,4},{6,7},{7,6},{8,9},{9,8},{10,11... | collective-permute-start | bytes 3145736 | tf_op jit(solution)/shard_map/ppermute | solution.py:39
  116.8 25.9 %collective-permute-start.3 = (bf16[256,2048]{1,0:T(8,128)(2,1)S(1)}, bf16[256,2048]{1,0:T(8,128)(2,1)S(1)}, u32[]{:S(2)}, u32[]{:S(2)}) collective-permute-start(bf16[256,2048]{1,0:T(8,128)(2,1)S(1)} %collective-permute-done.1.refs_2_), channel_id=1, source_target_pairs={{0,1},{1,0},{2,3},{3,2},{4,5},{5,4},{6,7},{7,6},{8,9},{9,8},{10,11... | collective-permute-start | bytes 3145736 | tf_op jit(solution)/shard_map/ppermute | solution.py:39
  140.7 40.2 %collective-permute-start.11 = (bf16[256,2048]{1,0:T(8,128)(2,1)S(1)}, bf16[256,2048]{1,0:T(8,128)(2,1)}, u32[]{:S(2)}, u32[]{:S(2)}) collective-permute-start(bf16[256,2048]{1,0:T(8,128)(2,1)S(1)} %bitcast.87), channel_id=1, source_target_pairs={{0,2},{1,5},{2,0},{3,7},{4,6},{5,1},{6,4},{7,3},{8,10},{9,13},{10,... | collective-permute-start | bytes 3145736 | tf_op jit(solution)/shard_map/ppermute | solution.py:39
  141.4 39.5 %collective-permute-start.12 = (bf16[256,2048]{1,0:T(8,128)(2,1)}, bf16[256,2048]{1,0:T(8,128)(2,1)}, u32[]{:S(2)}, u32[]{:S(2)}) collective-permute-start(bf16[256,2048]{1,0:T(8,128)(2,1)} %collective-permute-done.10.refs_1_), channel_id=1, source_target_pairs={{0,2},{1,5},{2,0},{3,7},{4,6},{5,1},{6,4},{7,3},{8,10},{9,13},{10,... | collective-permute-start | bytes 3145736 | tf_op jit(solution)/shard_map/ppermute | solution.py:39
  191.5 26.4 %collective-permute-start.18 = (bf16[256,2048]{1,0:T(8,128)(2,1)}, bf16[256,2048]{1,0:T(8,128)(2,1)}, u32[]{:S(2)}, u32[]{:S(2)}) collective-permute-start(bf16[256,2048]{1,0:T(8,128)(2,1)} %add_convert_fusion.11), channel_id=1, source_target_pairs={{0,2},{1,5},{2,0},{3,7},{4,6},{5,1},{6,4},{7,3},{8,10},{9,13},{10,... | collective-permute-start | bytes 3145736 | tf_op jit(solution)/shard_map/ppermute | solution.py:39
  193.4 36.8 %all-to-all-start.2 = ((bf16[64,8,1024]{2,0,1:T(8,128)(2,1)}), bf16[64,8,1024]{2,0,1:T(8,128)(2,1)}, u32[]{:S(2)}, u32[]{:S(2)}) async-start(bf16[64,8,1024]{2,0,1:T(8,128)(2,1)} %bitcast.95), calls=%async_computation.2 | async-start | bytes 2097152 | tf_op jit(solution)/shard_map/all_to_all | solution.py:138
  197.7 140.5 %all-gather.11.cloned.1.call-start = ((), (), s32[]{:S(2)}) async-start(), calls=%async_computation.12 | async-start | bytes 5242880 | tf_op jit(solution)/shard_map/all_gather | solution.py:141
  197.7 47.1 %collective-permute-start.22 = (bf16[256,2048]{1,0:T(8,128)(2,1)}, bf16[256,2048]{1,0:T(8,128)(2,1)}, u32[]{:S(2)}, u32[]{:S(2)}) collective-permute-start(bf16[256,2048]{1,0:T(8,128)(2,1)} %collective-permute-done.11.refs_2_), channel_id=1, source_target_pairs={{0,4},{1,3},{2,6},{3,1},{4,0},{5,7},{6,2},{7,5},{8,12},{9,11},{10,... | collective-permute-start | bytes 3145736 | tf_op jit(solution)/shard_map/ppermute | solution.py:39
  215.1 31.8 %collective-permute-start.17 = (bf16[256,2048]{1,0:T(8,128)(2,1)}, bf16[256,2048]{1,0:T(8,128)(2,1)}, u32[]{:S(2)}, u32[]{:S(2)}) collective-permute-start(bf16[256,2048]{1,0:T(8,128)(2,1)} %add_convert_fusion.12), channel_id=1, source_target_pairs={{0,2},{1,5},{2,0},{3,7},{4,6},{5,1},{6,4},{7,3},{8,10},{9,13},{10,... | collective-permute-start | bytes 3145736 | tf_op jit(solution)/shard_map/ppermute | solution.py:39
  220.4 26.6 %collective-permute-start.19 = (bf16[256,2048]{1,0:T(8,128)(2,1)}, bf16[256,2048]{1,0:T(8,128)(2,1)}, u32[]{:S(2)}, u32[]{:S(2)}) collective-permute-start(bf16[256,2048]{1,0:T(8,128)(2,1)} %add_convert_fusion.10), channel_id=1, source_target_pairs={{0,1},{1,0},{2,3},{3,2},{4,5},{5,4},{6,7},{7,6},{8,9},{9,8},{10,11... | collective-permute-start | bytes 3145736 | tf_op jit(solution)/shard_map/ppermute | solution.py:39
  230.2 192.6 %reduce-scatter.4.cloned.1.call-start = ((), (), s32[]{:S(2)}) async-start(), calls=%async_computation.13 | async-start | bytes 5242880 | tf_op jit(solution)/shard_map/reduce_scatter | solution.py:151
  265.2 25.6 %collective-permute-start.29 = (bf16[256,2048]{1,0:T(8,128)(2,1)S(1)}, bf16[256,2048]{1,0:T(8,128)(2,1)S(1)}, u32[]{:S(2)}, u32[]{:S(2)}) collective-permute-start(bf16[256,2048]{1,0:T(8,128)(2,1)S(1)} %collective-permute-done.25.refs_2_), channel_id=1, source_target_pairs={{0,4},{1,3},{2,6},{3,1},{4,0},{5,7},{6,2},{7,5},{8,12},{9,11},{10,... | collective-permute-start | bytes 3145736 | tf_op jit(solution)/shard_map/ppermute | solution.py:39
  265.6 25.2 %collective-permute-start.26 = (bf16[256,2048]{1,0:T(8,128)(2,1)S(1)}, bf16[256,2048]{1,0:T(8,128)(2,1)S(1)}, u32[]{:S(2)}, u32[]{:S(2)}) collective-permute-start(bf16[256,2048]{1,0:T(8,128)(2,1)S(1)} %collective-permute-done.24.refs_1_), channel_id=1, source_target_pairs={{0,2},{1,5},{2,0},{3,7},{4,6},{5,1},{6,4},{7,3},{8,10},{9,13},{10,... | collective-permute-start | bytes 3145736 | tf_op jit(solution)/shard_map/ppermute | solution.py:39
  266.5 24.8 %collective-permute-start.27 = (bf16[256,2048]{1,0:T(8,128)(2,1)S(1)}, bf16[256,2048]{1,0:T(8,128)(2,1)S(1)}, u32[]{:S(2)}, u32[]{:S(2)}) collective-permute-start(bf16[256,2048]{1,0:T(8,128)(2,1)S(1)} %collective-permute-done.25.refs_2_), channel_id=1, source_target_pairs={{0,1},{1,0},{2,3},{3,2},{4,5},{5,4},{6,7},{7,6},{8,9},{9,8},{10,11... | collective-permute-start | bytes 3145736 | tf_op jit(solution)/shard_map/ppermute | solution.py:39
  337.7 228.7 %reduce-scatter.6.cloned.1.call-start = ((), (), s32[]{:S(2)}) async-start(), calls=%async_computation.14 | async-start | bytes 10485760 | tf_op jit(solution)/shard_map/reduce_scatter | solution.py:151
  385.6 37.2 %collective-permute-start.36 = (bf16[256,2048]{1,0:T(8,128)(2,1)}, bf16[256,2048]{1,0:T(8,128)(2,1)}, u32[]{:S(2)}, u32[]{:S(2)}) collective-permute-start(bf16[256,2048]{1,0:T(8,128)(2,1)} %add_convert_fusion.8), channel_id=1, source_target_pairs={{0,2},{1,5},{2,0},{3,7},{4,6},{5,1},{6,4},{7,3},{8,10},{9,13},{10,... | collective-permute-start | bytes 3145736 | tf_op jit(solution)/shard_map/ppermute | solution.py:39
  396.9 25.9 %collective-permute-start.35 = (bf16[256,2048]{1,0:T(8,128)(2,1)}, bf16[256,2048]{1,0:T(8,128)(2,1)S(1)}, u32[]{:S(2)}, u32[]{:S(2)}) collective-permute-start(bf16[256,2048]{1,0:T(8,128)(2,1)} %add_convert_fusion.9), channel_id=1, source_target_pairs={{0,2},{1,5},{2,0},{3,7},{4,6},{5,1},{6,4},{7,3},{8,10},{9,13},{10,... | collective-permute-start | bytes 3145736 | tf_op jit(solution)/shard_map/ppermute | solution.py:39
  422.9 224.4 %reduce-scatter.8.cloned.1.call-start = ((), (), s32[]{:S(2)}) async-start(), calls=%async_computation.15 | async-start | bytes 5242880 | tf_op jit(solution)/shard_map/reduce_scatter | solution.py:151
  445.9 25.7 %collective-permute-start.47 = (bf16[256,2048]{1,0:T(8,128)(2,1)S(1)}, bf16[256,2048]{1,0:T(8,128)(2,1)}, u32[]{:S(2)}, u32[]{:S(2)}) collective-permute-start(bf16[256,2048]{1,0:T(8,128)(2,1)S(1)} %collective-permute-done.43.refs_2_.refs_10_), channel_id=1, source_target_pairs={{0,4},{1,3},{2,6},{3,1},{4,0},{5,7},{6,2},{7,5},{8,12},{9,11},{10,... | collective-permute-start | bytes 3145736 | tf_op jit(solution)/shard_map/ppermute | solution.py:39
  447.4 26.4 %collective-permute-start.44 = (bf16[256,2048]{1,0:T(8,128)(2,1)}, bf16[256,2048]{1,0:T(8,128)(2,1)}, u32[]{:S(2)}, u32[]{:S(2)}) collective-permute-start(bf16[256,2048]{1,0:T(8,128)(2,1)} %collective-permute-done.42.refs_1_.refs_9_), channel_id=1, source_target_pairs={{0,2},{1,5},{2,0},{3,7},{4,6},{5,1},{6,4},{7,3},{8,10},{9,13},{10,... | collective-permute-start | bytes 3145736 | tf_op jit(solution)/shard_map/ppermute | solution.py:39
  448.8 26.4 %collective-permute-start.39 = (bf16[256,2048]{1,0:T(8,128)(2,1)S(1)}, bf16[256,2048]{1,0:T(8,128)(2,1)S(1)}, u32[]{:S(2)}, u32[]{:S(2)}) collective-permute-start(bf16[256,2048]{1,0:T(8,128)(2,1)S(1)} %get-tuple-element.177), channel_id=1, source_target_pairs={{0,1},{1,0},{2,3},{3,2},{4,5},{5,4},{6,7},{7,6},{8,9},{9,8},{10,11... | collective-permute-start | bytes 3145736 | tf_op jit(solution)/shard_map/ppermute | solution.py:39
  449.1 33.6 %collective-permute-start.40 = (bf16[256,2048]{1,0:T(8,128)(2,1)S(1)}, bf16[256,2048]{1,0:T(8,128)(2,1)S(1)}, u32[]{:S(2)}, u32[]{:S(2)}) collective-permute-start(bf16[256,2048]{1,0:T(8,128)(2,1)S(1)} %convert_add_fusion.3), channel_id=1, source_target_pairs={{0,4},{1,3},{2,6},{3,1},{4,0},{5,7},{6,2},{7,5},{8,12},{9,11},{10,... | collective-permute-start | bytes 3145736 | tf_op jit(solution)/shard_map/ppermute | solution.py:39
  455.9 28.2 %collective-permute-start.45 = (bf16[256,2048]{1,0:T(8,128)(2,1)S(1)}, bf16[256,2048]{1,0:T(8,128)(2,1)S(1)}, u32[]{:S(2)}, u32[]{:S(2)}) collective-permute-start(bf16[256,2048]{1,0:T(8,128)(2,1)S(1)} %collective-permute-done.43.refs_2_.refs_10_), channel_id=1, source_target_pairs={{0,1},{1,0},{2,3},{3,2},{4,5},{5,4},{6,7},{7,6},{8,9},{9,8},{10,11... | collective-permute-start | bytes 3145736 | tf_op jit(solution)/shard_map/ppermute | solution.py:39
  568.0 35.9 %collective-permute-start.54 = (bf16[256,2048]{1,0:T(8,128)(2,1)}, bf16[256,2048]{1,0:T(8,128)(2,1)}, u32[]{:S(2)}, u32[]{:S(2)}) collective-permute-start(bf16[256,2048]{1,0:T(8,128)(2,1)} %add_convert_fusion.5), channel_id=1, source_target_pairs={{0,2},{1,5},{2,0},{3,7},{4,6},{5,1},{6,4},{7,3},{8,10},{9,13},{10,... | collective-permute-start | bytes 3145736 | tf_op jit(solution)/shard_map/ppermute | solution.py:39
  568.5 58.8 %all-to-all-start.3 = ((bf16[8,64,2048]{2,1,0:T(8,128)(2,1)}), bf16[8,64,2048]{2,1,0:T(8,128)(2,1)}, u32[]{:S(2)}, u32[]{:S(2)}) async-start(bf16[8,64,2048]{2,1,0:T(8,128)(2,1)} %bitcast.99), calls=%async_computation.6 | async-start | bytes 4194304 | tf_op jit(solution)/shard_map/all_to_all | solution.py:154
  588.2 38.2 %collective-permute-start.56 = (bf16[256,2048]{1,0:T(8,128)(2,1)S(1)}, bf16[256,2048]{1,0:T(8,128)(2,1)S(1)}, u32[]{:S(2)}, u32[]{:S(2)}) collective-permute-start(bf16[256,2048]{1,0:T(8,128)(2,1)S(1)} %copy-done.62), channel_id=1, source_target_pairs={{0,2},{1,5},{2,0},{3,7},{4,6},{5,1},{6,4},{7,3},{8,10},{9,13},{10,... | collective-permute-start | bytes 3145736 | tf_op jit(solution)/shard_map/ppermute | solution.py:39
  590.8 48.3 %collective-permute-start.53 = (bf16[256,2048]{1,0:T(8,128)(2,1)}, bf16[256,2048]{1,0:T(8,128)(2,1)}, u32[]{:S(2)}, u32[]{:S(2)}) collective-permute-start(bf16[256,2048]{1,0:T(8,128)(2,1)} %add_convert_fusion.6), channel_id=1, source_target_pairs={{0,2},{1,5},{2,0},{3,7},{4,6},{5,1},{6,4},{7,3},{8,10},{9,13},{10,... | collective-permute-start | bytes 3145736 | tf_op jit(solution)/shard_map/ppermute | solution.py:39
  606.4 32.6 %collective-permute-start.55 = (bf16[256,2048]{1,0:T(8,128)(2,1)}, bf16[256,2048]{1,0:T(8,128)(2,1)}, u32[]{:S(2)}, u32[]{:S(2)}) collective-permute-start(bf16[256,2048]{1,0:T(8,128)(2,1)} %add_convert_fusion.2), channel_id=1, source_target_pairs={{0,1},{1,0},{2,3},{3,2},{4,5},{5,4},{6,7},{7,6},{8,9},{9,8},{10,11... | collective-permute-start | bytes 3145736 | tf_op jit(solution)/shard_map/ppermute | solution.py:39
  (114 other events, 1666.6 us)
Sparse Core Ops, SparseCore 0:
  9.6 30.6 all-gather.4
  42.4 62.9 all-gather.6
  107.0 148.2 all-gather.8
  256.7 78.9 all-gather.10
  337.9 75.2 reduce-scatter.3
  423.0 143.3 reduce-scatter.5
  568.8 77.4 reduce-scatter.7
